TPU v7x, 256 devices: a whole 4x4x8 slice. The times are simulated.
256 devices in a mesh: row: 8 (over y, core), col: 32 (over z, x).
Axes of the slice: x: 4, y: 4, z: 8, core: 2. Of those that a mesh axis runs over, the one named last changes fastest.
Arguments:
- uv_coords: float32 [65536, 2, 128], P(('row', 'col')), may hold values from -12 to 12
- visibilities: float32 [65536, 2, 128], P(('row', 'col')), may hold values from -6 to 6
- aterm_left: bfloat16 [65536, 2, 1024], P(('row', 'col')), may hold values from -4 to 4
- aterm_right: bfloat16 [65536, 2, 1024], P(('row', 'col')), may hold values from -4 to 4
- block_subgrid: int32 [256, 256], P(('row', 'col')), may hold values from 0 to 127, never falling along the last dimension, each value on 1 to 4 neighbouring positions
- subgrid_tile: int32 [32768, 1], P(('row', 'col')), may hold values from 0 to 255; in each aligned block of 128 rows (0 to 127, 128 to 255, ...) at most 2 rows name the same one
- block_row: int32 [32768], P(('row', 'col')), may hold values from 0 to 31
- block_col: int32 [32768], P(('row', 'col')), may hold values from 0 to 7
Outputs:
- sky: float32 [8192, 8192], P(('row', 'col'))
Inputs may be any that keep to these rules, and one draw needn't show every extreme that they name: `subgrid_tile`: among one device's 128 subgrids no tile is named more than 2 times, a bound that some block reaches. `block_subgrid`: each row, for one device's blocks in order, never falls; every local subgrid gets 1 to 4 blocks, and some exactly 4.
All inputs are finite; a program needn't handle non-finite values.
Results may differ from a plain program's by a relative error of at most 0.0003.
Values sent between devices are 32-bit elements; how exact they have to be, the bound alone decides.
A program may use at most 128 MiB of HBM per device.

v0:
```python
from functools import partial
import math

import jax
import jax.numpy as jnp
from jax import lax
from jax.sharding import PartitionSpec as P

G = 8192
SUB = 32


exact_prec = lax.Precision.HIGHEST


def phasor_image(coords, visib, left_term, right_term):
    centred = jnp.arange(SUB).astype(jnp.float32) - SUB / 2
    step_angle = 2 * math.pi / SUB
    theta_l = step_angle * coords[:, 0, :, None] * centred
    theta_m = step_angle * coords[:, 1, :, None] * centred
    vis_re = visib[:, 0, :, None]
    vis_im = visib[:, 1, :, None]
    cos_l = jnp.cos(theta_l)
    sin_l = jnp.sin(theta_l)
    cos_m = jnp.cos(theta_m)
    sin_m = jnp.sin(theta_m)
    wave_re = vis_re * cos_l - vis_im * sin_l
    wave_im = vis_re * sin_l + vis_im * cos_l
    pattern = "bkl,bkm->blm"
    image_re = jnp.einsum(pattern, wave_re, cos_m, precision=exact_prec) - jnp.einsum(
        pattern, wave_im, sin_m, precision=exact_prec
    )
    image_im = jnp.einsum(pattern, wave_re, sin_m, precision=exact_prec) + jnp.einsum(
        pattern, wave_im, cos_m, precision=exact_prec
    )
    number = image_re.shape[0]
    image_re = image_re.reshape(number, SUB * SUB)
    image_im = image_im.reshape(number, SUB * SUB)
    left_beam = left_term.astype(jnp.float32)
    right_beam = right_term.astype(jnp.float32)
    beam_re = left_beam[:, 0] * right_beam[:, 0] + left_beam[:, 1] * right_beam[:, 1]
    beam_im = left_beam[:, 1] * right_beam[:, 0] - left_beam[:, 0] * right_beam[:, 1]
    norm_scale = coords.shape[2] ** (-0.5)
    contrib_re = (beam_re * image_re - beam_im * image_im) * norm_scale
    contrib_im = (beam_re * image_im + beam_im * image_re) * norm_scale
    return jnp.concatenate([contrib_re, contrib_im], axis=1)


def taper_table():
    position = jnp.arange(SUB).astype(jnp.float32)
    window = jnp.sin(math.pi * (position + 0.5) / SUB)
    square = (window[:, None] * window[None, :]).reshape(SUB * SUB)
    return jnp.concatenate([square, square])


def subgrid_dft(images):
    number = images.shape[0]
    stacked = images.reshape(number, 2, SUB, SUB)
    position = jnp.arange(SUB, dtype=jnp.int32)
    product = position[:, None] * position[None, :] % SUB
    angles = -2 * math.pi / SUB * product.astype(jnp.float32)
    fwd_re = jnp.cos(angles)
    fwd_im = jnp.sin(angles)
    first = "nlm,bm->nlb"
    mid_re = jnp.einsum(first, stacked[:, 0], fwd_re, precision=exact_prec) - jnp.einsum(
        first, stacked[:, 1], fwd_im, precision=exact_prec
    )
    mid_im = jnp.einsum(first, stacked[:, 0], fwd_im, precision=exact_prec) + jnp.einsum(
        first, stacked[:, 1], fwd_re, precision=exact_prec
    )
    second = "al,nlb->nab"
    out_re = jnp.einsum(second, fwd_re, mid_re, precision=exact_prec) - jnp.einsum(
        second, fwd_im, mid_im, precision=exact_prec
    )
    out_im = jnp.einsum(second, fwd_im, mid_re, precision=exact_prec) + jnp.einsum(
        second, fwd_re, mid_im, precision=exact_prec
    )
    result = jnp.stack([out_re, out_im], axis=1) / SUB
    return result.reshape(number, 2 * SUB * SUB)


def phase_table(size_a, size_b, modulus):
    index_a = jnp.arange(size_a, dtype=jnp.int32)
    index_b = jnp.arange(size_b, dtype=jnp.int32)
    angles = (
        2 * math.pi / modulus * (index_a[:, None] * index_b[None, :] % modulus).astype(jnp.float32)
    )
    return (jnp.cos(angles), jnp.sin(angles))


def transform_down(stacked):
    length = stacked.shape[1]
    split = math.gcd(length, 128)
    inner = length // split
    outer_cos, outer_sin = phase_table(split, split, split)
    twist_cos, twist_sin = phase_table(split, inner, length)
    inner_cos, inner_sin = phase_table(inner, inner, inner)
    contract = partial(jnp.einsum, precision=exact_prec)
    data_re = stacked[0].reshape(split, inner, -1)
    data_im = stacked[1].reshape(split, inner, -1)
    mid_re = contract("kj,jac->kac", outer_cos, data_re) - contract(
        "kj,jac->kac", outer_sin, data_im
    )
    mid_im = contract("kj,jac->kac", outer_cos, data_im) + contract(
        "kj,jac->kac", outer_sin, data_re
    )
    turn_re = mid_re * twist_cos[:, :, None] - mid_im * twist_sin[:, :, None]
    turn_im = mid_re * twist_sin[:, :, None] + mid_im * twist_cos[:, :, None]
    out_re = contract("ba,kac->bkc", inner_cos, turn_re) - contract(
        "ba,kac->bkc", inner_sin, turn_im
    )
    out_im = contract("ba,kac->bkc", inner_cos, turn_im) + contract(
        "ba,kac->bkc", inner_sin, turn_re
    )
    return jnp.stack([out_re.reshape(length, -1), out_im.reshape(length, -1)])


def transform_across_real(stacked):
    number = stacked.shape[1]
    length = stacked.shape[2]
    split = math.gcd(length, 128)
    inner = length // split
    outer_cos, outer_sin = phase_table(split, split, split)
    twist_cos, twist_sin = phase_table(split, inner, length)
    inner_cos, inner_sin = phase_table(inner, inner, inner)
    contract = partial(jnp.einsum, precision=exact_prec)
    data_re = stacked[0].reshape(number, split, inner)
    data_im = stacked[1].reshape(number, split, inner)
    mid_re = contract("kj,rja->rka", outer_cos, data_re) - contract(
        "kj,rja->rka", outer_sin, data_im
    )
    mid_im = contract("kj,rja->rka", outer_cos, data_im) + contract(
        "kj,rja->rka", outer_sin, data_re
    )
    turn_re = mid_re * twist_cos[None] - mid_im * twist_sin[None]
    turn_im = mid_re * twist_sin[None] + mid_im * twist_cos[None]
    out_re = contract("ba,rka->rbk", inner_cos, turn_re) - contract(
        "ba,rka->rbk", inner_sin, turn_im
    )
    return out_re.reshape(number, length)


def body(
    uv_coords,
    visibilities,
    aterm_left,
    aterm_right,
    block_subgrid,
    subgrid_tile,
    block_row,
    block_col,
):
    n_row = lax.axis_size("row")
    n_col = lax.axis_size("col")
    devices = n_row * n_col
    blocks = uv_coords.shape[0]
    visible = uv_coords.shape[2]
    sub_count = subgrid_tile.shape[0]
    group_size = math.gcd(blocks, 128)
    batches = blocks // group_size

    def grid_group(pieces):
        return phasor_image(pieces[0], pieces[1], pieces[2], pieces[3])

    contrib = lax.map(
        grid_group,
        (
            uv_coords.reshape(batches, group_size, 2, visible),
            visibilities.reshape(batches, group_size, 2, visible),
            aterm_left.reshape(batches, group_size, 2, SUB * SUB),
            aterm_right.reshape(batches, group_size, 2, SUB * SUB),
        ),
    ).reshape(blocks, 2 * SUB * SUB)
    owner_map = (
        block_subgrid[0][None, :] == jnp.arange(sub_count, dtype=jnp.int32)[:, None]
    ).astype(jnp.float32)
    images = (
        jnp.dot(owner_map, contrib, precision=exact_prec, preferred_element_type=jnp.float32)
        * taper_table()
    )
    payload = subgrid_dft(images)
    capacity = max(2, 2 * sub_count // devices)
    target = subgrid_tile[:, 0]
    order_ids = jnp.arange(sub_count, dtype=jnp.int32)
    earlier = (target[None, :] == target[:, None]) & (order_ids[None, :] < order_ids[:, None])
    slot_index = target * capacity + jnp.sum(earlier.astype(jnp.int32), axis=1)
    tile_u = G // n_row
    tile_v = G // n_col
    blocks_down = tile_u // SUB
    blocks_across = tile_v // SUB
    place_code = (block_row * blocks_across + block_col).astype(jnp.float32)
    outbox = jnp.zeros((devices * capacity, 2 * SUB * SUB), jnp.float32).at[slot_index].set(payload)
    outbox = outbox.reshape(n_row, n_col, capacity, 2 * SUB * SUB)
    labels = jnp.full((devices * capacity,), -1.0, jnp.float32).at[slot_index].set(place_code)
    labels = labels.reshape(n_row, n_col, capacity)
    arrived, arrived_labels = (
        lax.all_to_all(
            lax.all_to_all(outbox, "row", split_axis=0, concat_axis=0, tiled=True),
            "col",
            split_axis=1,
            concat_axis=1,
            tiled=True,
        ),
        lax.all_to_all(
            lax.all_to_all(labels, "row", split_axis=0, concat_axis=0, tiled=True),
            "col",
            split_axis=1,
            concat_axis=1,
            tiled=True,
        ),
    )
    arrived = arrived.reshape(devices * capacity, 2 * SUB * SUB)
    arrived_labels = arrived_labels.reshape(devices * capacity)
    positions = jnp.arange(blocks_down * blocks_across).astype(jnp.float32)
    choose = (arrived_labels[None, :] == positions[:, None]).astype(jnp.float32)
    summed = jnp.dot(choose, arrived, precision=exact_prec, preferred_element_type=jnp.float32)
    tile_grid = (
        summed.reshape(blocks_down, blocks_across, 2, SUB, SUB)
        .transpose(2, 0, 3, 1, 4)
        .reshape(2, tile_u, tile_v)
    )
    column_band = lax.all_to_all(tile_grid, "row", split_axis=2, concat_axis=1, tiled=True)
    half_done = transform_down(column_band)
    pencils = lax.all_to_all(
        lax.all_to_all(half_done, "row", split_axis=1, concat_axis=2, tiled=True),
        "col",
        split_axis=1,
        concat_axis=2,
        tiled=True,
    )
    return transform_across_real(pencils) / G


def solution(mesh):
    placed = (
        P(("row", "col"), None, None),
        P(("row", "col"), None, None),
        P(("row", "col"), None, None),
        P(("row", "col"), None, None),
        P(("row", "col"), None),
        P(("row", "col"), None),
        P(("row", "col")),
        P(("row", "col")),
    )
    return jax.shard_map(
        body, mesh=mesh, in_specs=placed, out_specs=P(("row", "col"), None), check_vma=False
    )
```

profile of v0, /device:TPU:32, one launch (start us, length us, event | category | flops | bytes accessed | tf_op | source)
XLA Modules:
  0.0 650.2 jit_solution(16654469506064857754)
XLA Ops:
  4.1 4.5 all-to-all-start
  8.6 170.3 %while.12 = (s32[]{:T(128)}, f32[2,128,2048]{2,1,0:T(8,128)}, bf16[2,128,2,1024]{3,2,1,0:T(2,128)(2,1)}, bf16[2,128,2,1024]{3,2,1,0:T(2,128)(2,1)}, f32[2,128,2,...) while((s32[]{:T(128)}, f32[2,128,2048]{2,1,0:T(8,128)}, bf16[2,128,2,1024]{3,2,1,0:T(2,128)(2,1)}, ...), condition=%wide.region_3.4_spmd, body=%wide.region_2.3_spmd.sunk | while | flops 818708544 | bytes 28837076 | solution.py:165
  10.2 17.7 %fusion.281 = f32[128,32,32]{2,1,0:T(8,128)S(1)} fusion(f32[128,128]{1,0:T(8,128)S(1)} %get-tuple-element.191, f32[128,128]{1,0:T(8,128)S(1)} %get-tuple-element.193, f32[32]{0:T(128)S(1)} %convert_add_fusion.2, f32[128,128]{1,0:T(8,128)S(1)} %get-tuple-element.194, f32[128,128]{1,0:T(8,128)S(1)} %get-tuple-element.195), kind=kOutput, calls=%fused_computation.11.clone.1 | convolution fusion | flops 203948032 | bytes 786560 | tf_op jit(solution)/shard_map/while/body/eval_jaxpr/bkl,bkm->blm/dot_general | solution.py:30
  28.0 18.0 %fusion.282 = f32[128,32,32]{2,1,0:T(8,128)S(1)} fusion(f32[128,32,32]{2,1,0:T(8,128)S(1)} %fusion.281, f32[128,128]{1,0:T(8,128)S(1)} %get-tuple-element.191, f32[128,128]{1,0:T(8,128)S(1)} %get-tuple-element.193, f32[32]{0:T(128)S(1)} %convert_add_fusion.2, f32[128,128]{1,0:T(8,128)S(1)} %get-tuple-element.194, f32[128,128]{1,0:T(8,128)S(1)} %get-tuple-element.195), kind=kOutput, calls=%fused_computation.16.clone.1 | convolution fusion | flops 204079104 | bytes 1310848 | tf_op jit(solution)/shard_map/while/body/eval_jaxpr/bkl,bkm->blm/dot_general | solution.py:30
  46.0 1.3 copy.266
  47.3 18.0 %fusion.279 = f32[128,32,32]{2,1,0:T(8,128)S(1)} fusion(f32[128,128]{1,0:T(8,128)S(1)} %get-tuple-element.191, f32[128,128]{1,0:T(8,128)S(1)} %get-tuple-element.193, f32[32]{0:T(128)S(1)} %convert_add_fusion.2, f32[128,128]{1,0:T(8,128)S(1)} %get-tuple-element.194, f32[128,128]{1,0:T(8,128)S(1)} %get-tuple-element.195), kind=kOutput, calls=%fused_computation.10.clone.1 | convolution fusion | flops 203948032 | bytes 786560 | tf_op jit(solution)/shard_map/while/body/eval_jaxpr/bkl,bkm->blm/dot_general | solution.py:33
  65.3 18.3 %fusion.280 = f32[128,32,32]{2,1,0:T(8,128)S(1)} fusion(f32[128,32,32]{2,1,0:T(8,128)S(1)} %fusion.279, f32[128,128]{1,0:T(8,128)S(1)} %get-tuple-element.191, f32[128,128]{1,0:T(8,128)S(1)} %get-tuple-element.193, f32[32]{0:T(128)S(1)} %convert_add_fusion.2, f32[128,128]{1,0:T(8,128)S(1)} %get-tuple-element.194, f32[128,128]{1,0:T(8,128)S(1)} %get-tuple-element.195), kind=kOutput, calls=%fused_computation.17.clone.1 | convolution fusion | flops 204079104 | bytes 1310848 | tf_op jit(solution)/shard_map/while/body/eval_jaxpr/bkl,bkm->blm/dot_general | solution.py:33
  83.6 1.3 copy.265
  84.8 1.9 constant_dynamic-slice_fusion.7
  91.2 17.7 %fusion.281 = f32[128,32,32]{2,1,0:T(8,128)S(1)} fusion(f32[128,128]{1,0:T(8,128)S(1)} %get-tuple-element.191, f32[128,128]{1,0:T(8,128)S(1)} %get-tuple-element.193, f32[32]{0:T(128)S(1)} %convert_add_fusion.2, f32[128,128]{1,0:T(8,128)S(1)} %get-tuple-element.194, f32[128,128]{1,0:T(8,128)S(1)} %get-tuple-element.195), kind=kOutput, calls=%fused_computation.11.clone.1 | convolution fusion | flops 203948032 | bytes 786560 | tf_op jit(solution)/shard_map/while/body/eval_jaxpr/bkl,bkm->blm/dot_general | solution.py:30
  108.9 18.1 %fusion.282 = f32[128,32,32]{2,1,0:T(8,128)S(1)} fusion(f32[128,32,32]{2,1,0:T(8,128)S(1)} %fusion.281, f32[128,128]{1,0:T(8,128)S(1)} %get-tuple-element.191, f32[128,128]{1,0:T(8,128)S(1)} %get-tuple-element.193, f32[32]{0:T(128)S(1)} %convert_add_fusion.2, f32[128,128]{1,0:T(8,128)S(1)} %get-tuple-element.194, f32[128,128]{1,0:T(8,128)S(1)} %get-tuple-element.195), kind=kOutput, calls=%fused_computation.16.clone.1 | convolution fusion | flops 204079104 | bytes 1310848 | tf_op jit(solution)/shard_map/while/body/eval_jaxpr/bkl,bkm->blm/dot_general | solution.py:30
  127.0 1.3 copy.266
  128.3 18.2 %fusion.279 = f32[128,32,32]{2,1,0:T(8,128)S(1)} fusion(f32[128,128]{1,0:T(8,128)S(1)} %get-tuple-element.191, f32[128,128]{1,0:T(8,128)S(1)} %get-tuple-element.193, f32[32]{0:T(128)S(1)} %convert_add_fusion.2, f32[128,128]{1,0:T(8,128)S(1)} %get-tuple-element.194, f32[128,128]{1,0:T(8,128)S(1)} %get-tuple-element.195), kind=kOutput, calls=%fused_computation.10.clone.1 | convolution fusion | flops 203948032 | bytes 786560 | tf_op jit(solution)/shard_map/while/body/eval_jaxpr/bkl,bkm->blm/dot_general | solution.py:33
  146.4 18.0 %fusion.280 = f32[128,32,32]{2,1,0:T(8,128)S(1)} fusion(f32[128,32,32]{2,1,0:T(8,128)S(1)} %fusion.279, f32[128,128]{1,0:T(8,128)S(1)} %get-tuple-element.191, f32[128,128]{1,0:T(8,128)S(1)} %get-tuple-element.193, f32[32]{0:T(128)S(1)} %convert_add_fusion.2, f32[128,128]{1,0:T(8,128)S(1)} %get-tuple-element.194, f32[128,128]{1,0:T(8,128)S(1)} %get-tuple-element.195), kind=kOutput, calls=%fused_computation.17.clone.1 | convolution fusion | flops 204079104 | bytes 1310848 | tf_op jit(solution)/shard_map/while/body/eval_jaxpr/bkl,bkm->blm/dot_general | solution.py:33
  164.5 1.3 copy.265
  165.8 1.9 constant_dynamic-slice_fusion.7
  179.1 2.5 convolution_multiply_fusion
  189.5 3.4 scatter_custom_fusion.1
  192.9 5.9 reshape.219
  198.8 4.8 all-to-all-start.2
  204.3 49.1 %all-to-all-done.2 = f32[8,32,2,2048]{3,2,1,0:T(2,128)} async-done(((f32[8,32,2,2048]{3,2,1,0:T(2,128)}), f32[8,32,2,2048]{3,2,1,0:T(2,128)}, u32[]{:S(2)}, u32[]{:S(2)}) %all-to-all-start.2) | async-done | bytes 4194336 | tf_op jit(solution)/shard_map/all_to_all | solution.py:198
  253.3 11.5 %all-to-all-start.1 = ((f32[8,32,2]{0,2,1:T(2,128)}), f32[8,32,2]{0,2,1:T(2,128)S(1)}, u32[]{:S(2)}, u32[]{:S(2)}) async-start(f32[8,32,2]{0,2,1:T(2,128)} %copy.173), calls=%async_computation.1 | async-start | bytes 65536 | tf_op jit(solution)/shard_map/all_to_all | solution.py:204
  264.8 6.9 %copy.191 = f32[8,32,2,2048]{3,2,0,1:T(2,128)} copy(f32[8,32,2,2048]{3,2,1,0:T(2,128)} %all-to-all-done.2) | data formatting | bytes 8388608 | tf_op jit(solution)/shard_map/all_to_all | solution.py:198
  271.8 1.7 all-to-all-done.1
  273.4 8.2 %all-to-all-start.3 = ((f32[8,32,2,2048]{3,2,0,1:T(2,128)}), f32[8,32,2,2048]{3,2,0,1:T(2,128)}, u32[]{:S(2)}, u32[]{:S(2)}) async-start(f32[8,32,2,2048]{3,2,0,1:T(2,128)} %copy.191), calls=%async_computation.3 | async-start | bytes 8388608 | tf_op jit(solution)/shard_map/all_to_all | solution.py:197
  282.0 93.5 %all-to-all-done.3 = f32[8,32,2,2048]{3,2,0,1:T(2,128)} async-done(((f32[8,32,2,2048]{3,2,0,1:T(2,128)}), f32[8,32,2,2048]{3,2,0,1:T(2,128)}, u32[]{:S(2)}, u32[]{:S(2)}) %all-to-all-start.3) | async-done | bytes 4194336 | tf_op jit(solution)/shard_map/all_to_all | solution.py:197
  375.5 6.9 %copy.192 = f32[8,32,2,2048]{3,2,1,0:T(2,128)} copy(f32[8,32,2,2048]{3,2,0,1:T(2,128)} %all-to-all-done.3) | data formatting | bytes 8388608 | tf_op jit(solution)/shard_map/all_to_all | solution.py:197
  382.4 6.1 reshape.220
  388.5 5.4 copy.193
  393.8 10.5 %convolution_bitcast_fusion = f32[2,32,32,8,32]{4,3,2,0,1:T(8,128)} fusion(f32[2,32,32,512,1]{3,2,1,0,4:T(8,128)} %bitcast.234, f32[32,8]{1,0:T(8,128)S(1)} %add_convert_fusion, f32[512]{0:T(512)S(1)} %eq.65), kind=kOutput, calls=%fused_computation.65 | convolution fusion | flops 3221356544 | bytes 6294528 | tf_op jit(solution)/shard_map/dot_general | solution.py:216
  404.4 10.1 %copy.231 = f32[2,32,32,8,32]{2,1,0,4,3:T(8,128)} copy(f32[2,32,32,8,32]{4,3,2,0,1:T(8,128)} %convolution_bitcast_fusion) | data formatting | bytes 4194304 | tf_op jit(solution)/shard_map/reshape | solution.py:220
  414.5 8.1 %reshape.248 = f32[2,1024,256]{1,0,2:T(2,128)} reshape(f32[2,32,32,8,32]{2,1,0,4,3:T(8,128)} %copy.231) | data formatting | bytes 4194304 | tf_op jit(solution)/shard_map/reshape | solution.py:220
  422.6 3.8 all-to-all-start.4
  426.6 26.8 %all-to-all-done.4 = f32[2,1024,256]{1,0,2:T(2,128)S(1)} async-done(((f32[2,1024,256]{1,0,2:T(2,128)}), f32[2,1024,256]{1,0,2:T(2,128)S(1)}, u32[]{:S(2)}, u32[]{:S(2)}) %all-to-all-start.4) | async-done | bytes 2097184 | tf_op jit(solution)/shard_map/all_to_all | solution.py:222
  454.0 1.2 fusion.252
  456.4 4.4 fusion.91
  461.4 1.9 reshape_squeeze.13
  463.3 5.2 fusion.89
  468.6 3.9 convolution_subtract_fusion.3
  472.5 3.5 convolution_add_fusion.2
  476.0 1.2 fusion.74
  477.2 1.2 fusion.75
  478.3 2.1 convolution_subtract_fusion.2
  480.5 2.4 stack_reshape.6
  482.9 2.1 convolution_add_fusion.1
  485.0 2.5 stack_reshape.7
  487.5 1.4 pad_maximum_fusion
  488.9 7.9 %copy.203 = f32[2,8192,32]{2,0,1:T(2,128)} copy(f32[2,8192,32]{1,2,0:T(8,128)S(1)} %pad_maximum_fusion) | data formatting | bytes 4194304 | tf_op jit(solution)/shard_map/stack | solution.py:115
  496.7 10.3 %reshape.253 = f32[8,1,65536]{2,1,0:T(1,128)S(1)} reshape(f32[8192,2,32]{2,1,0:T(2,128)} %bitcast.220) | data formatting | bytes 4194304
  507.1 30.8 %all_to_all.68 = f32[8,1,65536]{2,1,0:T(1,128)} all-to-all(f32[8,1,65536]{2,1,0:T(1,128)S(1)} %reshape.253), channel_id=1, replica_groups=mesh['row'=8,'col'=32] {'row'}, dimensions={0} | all-to-all | bytes 4194304 | tf_op jit(solution)/shard_map/all_to_all | solution.py:225
  538.4 7.2 %reduce = f32[8,65536]{1,0:T(8,128)S(1)} reduce(f32[8,1,65536]{2,1,0:T(1,128)} %all_to_all.68, f32[]{:T(128)} %broadcast.394), dimensions={1}, to_apply=%all_to_all.54.reduce_sub_computation | reduce | bytes 4194308 | tf_op jit(solution)/shard_map/all_to_all | solution.py:225
  545.7 10.3 %reshape.254 = f32[8192,2,32]{2,1,0:T(2,128)} reshape(f32[8,65536]{1,0:T(8,128)S(1)} %reduce) | data formatting | bytes 4194304
  555.9 10.2 %copy.233 = f32[2,8,1024,32]{2,3,1,0:T(8,128)S(1)} copy(f32[2,8,1024,32]{3,0,2,1:T(2,128)} %bitcast.221) | data formatting | bytes 4194304 | tf_op jit(solution)/shard_map/all_to_all | solution.py:225
  566.1 2.4 copy.206
  568.5 55.7 %all_to_all.69 = f32[2,1024,256]{2,0,1:T(2,128)S(1)} all-to-all(f32[2,1024,256]{2,0,1:T(2,128)} %copy.206), channel_id=1, replica_groups=mesh['row'=8,'col'=32] {'col'}, dimensions={1} | all-to-all | bytes 4194304 | tf_op jit(solution)/shard_map/all_to_all | solution.py:224
  624.3 1.2 fusion.251
  626.5 4.4 fusion.87
  631.5 1.7 reshape_squeeze.15
  633.2 5.2 fusion.85
  638.4 3.5 fusion.50
  641.9 3.7 fusion.49
  645.7 1.3 fusion.56
  647.0 1.4 fusion.48
  648.4 1.6 copy.255
  (88 shorter events, 26.4 us)
Async XLA Ops:
  4.1 194.7 %all-to-all-start = ((f32[8,32,2]{1,2,0:T(2,128)}), f32[8,32,2]{1,2,0:T(2,128)S(1)}, u32[]{:S(2)}, u32[]{:S(2)}) async-start(f32[8,32,2]{1,2,0:T(2,128)} %copy.172), calls=%async_computation | async-start | bytes 16384 | tf_op jit(solution)/shard_map/all_to_all | solution.py:205
  8.6 170.5 %copy-start.9 = (s32[1,256]{1,0:T(1,128)S(1)}, s32[1,256]{1,0:T(1,128)}, u32[]{:S(2)}) copy-start(s32[1,256]{1,0:T(1,128)} %param.14) | copy-start | bytes 3076
  198.8 54.6 %all-to-all-start.2 = ((f32[8,32,2,2048]{3,2,1,0:T(2,128)}), f32[8,32,2,2048]{3,2,1,0:T(2,128)}, u32[]{:S(2)}, u32[]{:S(2)}) async-start(f32[8,32,2,2048]{3,2,1,0:T(2,128)} %reshape.219), calls=%async_computation.2 | async-start | bytes 8388608 | tf_op jit(solution)/shard_map/all_to_all | solution.py:198
  253.3 20.1 %all-to-all-start.1 = ((f32[8,32,2]{0,2,1:T(2,128)}), f32[8,32,2]{0,2,1:T(2,128)S(1)}, u32[]{:S(2)}, u32[]{:S(2)}) async-start(f32[8,32,2]{0,2,1:T(2,128)} %copy.173), calls=%async_computation.1 | async-start | bytes 65536 | tf_op jit(solution)/shard_map/all_to_all | solution.py:204
  273.4 102.1 %all-to-all-start.3 = ((f32[8,32,2,2048]{3,2,0,1:T(2,128)}), f32[8,32,2,2048]{3,2,0,1:T(2,128)}, u32[]{:S(2)}, u32[]{:S(2)}) async-start(f32[8,32,2,2048]{3,2,0,1:T(2,128)} %copy.191), calls=%async_computation.3 | async-start | bytes 8388608 | tf_op jit(solution)/shard_map/all_to_all | solution.py:197
  422.6 30.7 %all-to-all-start.4 = ((f32[2,1024,256]{1,0,2:T(2,128)}), f32[2,1024,256]{1,0,2:T(2,128)S(1)}, u32[]{:S(2)}, u32[]{:S(2)}) async-start(f32[2,1024,256]{1,0,2:T(2,128)} %reshape.248), calls=%async_computation.4 | async-start | bytes 4194304 | tf_op jit(solution)/shard_map/all_to_all | solution.py:222
  456.3 5.1 copy-start
  456.4 4.5 copy-start.6
  463.3 5.2 copy-start.2
  463.3 5.2 copy-start.4
  468.6 3.9 copy-start.1
  485.0 2.5 copy-start.7
  626.5 4.4 copy-start.8
  633.2 5.2 copy-start.3
  633.2 5.2 copy-start.5
where the time goes:
time: 655 us; the launch traced here: 650 us
  matrix products  207 us (32%)
  waiting for transfers between devices  171 us (26%)
  local copies, waits for them, and re-layouts  131 us (20%)
  blocking collectives  86.5 us (13%)
  starting transfers between devices  32.7 us (5%)
  other arithmetic  12.6 us (2%)
  loops' own time  9.01 us (1%)
    all_to_all x1, waiting for transfers between devices, body(): lax.all_to_all(lax.all_to_all(outbox, 'row', split_axis=0, concat_axis=0,...  93.5 us
    all_to_all x1, blocking collectives, body(): lax.all_to_all(lax.all_to_all(half_done, 'row', split_axis=1, concat_axis...  55.7 us
    all_to_all x1, waiting for transfers between devices, body(): lax.all_to_all(outbox, 'row', split_axis=0, concat_axis=0, tiled=True)  49.1 us
    dot_general x2, matrix products, phasor_image(): jnp.einsum(pattern, wave_re, sin_m, precision=exact_prec)  36.3 us
    dot_general x2, matrix products, phasor_image(): jnp.einsum(pattern, wave_im, cos_m, precision=exact_prec)  36.1 us
    dot_general x2, matrix products, phasor_image(): jnp.einsum(pattern, wave_im, sin_m, precision=exact_prec)  36.1 us
    dot_general x2, matrix products, phasor_image(): jnp.einsum(pattern, wave_re, cos_m, precision=exact_prec)  35.5 us
    all_to_all x1, blocking collectives, body(): lax.all_to_all(half_done, 'row', split_axis=1, concat_axis=2, tiled=True)  30.8 us
  transfers between devices with their start and end apart: 5, of which 4 were waited for; matrix products, arithmetic and copies ran while one was open for 29% of the time, Pallas kernels for 0%

commit v1 on v0

v1 whole, which is shorter than its diff:
```python
import math
from functools import partial

import jax
import jax.numpy as jnp
import ml_dtypes
import numpy as np
from jax import lax
from jax.experimental import pallas as pl
from jax.experimental.pallas import tpu as pltpu
from jax.sharding import PartitionSpec as P

G = 8192
SUB = 32
PAIRS = 16
CLASSES = 16
STEP = 32
F32 = jnp.float32
BF16 = jnp.bfloat16
MB = 1 << 20


def halves(table):
    high = np.asarray(table, np.float32).astype(ml_dtypes.bfloat16)
    low = (np.asarray(table, np.float64) - high.astype(np.float64)).astype(ml_dtypes.bfloat16)
    return high, low


def split(x):
    high = x.astype(BF16)
    return high, (x - high.astype(F32)).astype(BF16)


def dot(a, b):
    return lax.dot_general(a, b, (((1,), (0,)), ((), ())), preferred_element_type=F32)


def dot_nt(a, b):
    return lax.dot_general(a, b, (((1,), (1,)), ((), ())), preferred_element_type=F32)


def dot3(ah, al, bh, bl):
    return dot(ah, bh) + (dot(al, bh) + dot(ah, bl))


def taper(p):
    return np.sin(math.pi * (p + 0.5) / SUB)


def class_column(j, c2):
    return j if c2 == 0 else (16 if j == 0 else 32 - j)


def subgrid_tables(visible):
    m = np.arange(32)
    first = np.zeros((2, 4, 32, 2, 4, 2, 8, 2))
    second = np.zeros((8, 4, 2, 8, 2, 8, 2, 2, 32))
    for cg in range(2):
        for j8 in range(8):
            for c2 in range(2):
                phi = 2 * math.pi * ((class_column(cg * 8 + j8, c2) * m) % 32) / 32
                for l4 in range(4):
                    first[0, l4, :, cg, l4, 0, j8, c2] = np.cos(phi) * taper(m)
                    first[1, l4, :, cg, l4, 0, j8, c2] = np.sin(phi) * taper(m)
                    first[0, l4, :, cg, l4, 1, j8, c2] = -np.sin(phi) * taper(m)
                    first[1, l4, :, cg, l4, 1, j8, c2] = np.cos(phi) * taper(m)
    a = np.arange(32)
    scale = visible ** (-0.5) / SUB / G
    for l8 in range(8):
        for l4 in range(4):
            l = 4 * l8 + l4
            phi = 2 * math.pi * ((a * l) % 32) / 32
            weight = taper(l) * scale
            for j8 in range(8):
                for c2 in range(2):
                    second[l8, l4, 0, j8, c2, j8, c2, 0] = np.cos(phi) * weight
                    second[l8, l4, 1, j8, c2, j8, c2, 0] = np.sin(phi) * weight
                    second[l8, l4, 0, j8, c2, j8, c2, 1] = -np.sin(phi) * weight
                    second[l8, l4, 1, j8, c2, j8, c2, 1] = np.cos(phi) * weight
    return first.reshape(256, 256), second.reshape(1024, 1024)


def down_tables():
    r = np.arange(256)[:, None, None, None]
    nt, q4, lo = np.meshgrid(np.arange(2), np.arange(4), np.arange(32), indexing="ij")
    l1 = ((nt * 4 + q4) * 32 + lo)[None]
    phi = 2 * math.pi * ((r * l1) % 256) / 256
    c, s = np.cos(phi), np.sin(phi)
    w = np.zeros((2, 256, 2, 2, 4, 2, 32))
    w[0, :, :, 0, :, 0], w[1, :, :, 0, :, 0] = c, -s
    w[0, :, :, 0, :, 1], w[1, :, :, 0, :, 1] = s, c
    w[0, :, :, 1, :, 0], w[1, :, :, 1, :, 0] = -s, -c
    w[0, :, :, 1, :, 1], w[1, :, :, 1, :, 1] = c, -s
    a = np.arange(32)[None, :, None, None]
    l1 = ((nt * 4 + q4) * 32 + lo)[:, None]
    psi = 2 * math.pi * a * l1 / G
    c, s = np.cos(psi), np.sin(psi)
    t = np.zeros((2, 4, 2, 2, 32, 4, 2, 32))
    for which in range(2):
        t[which, 0, :, 0, :, :, 0], t[which, 1, :, 0, :, :, 0] = c, s
        t[which, 2, :, 0, :, :, 0], t[which, 3, :, 0, :, :, 0] = -s, c
    t[0, 0, :, 0, :, :, 1], t[0, 1, :, 0, :, :, 1] = c, s
    t[0, 2, :, 0, :, :, 1], t[0, 3, :, 0, :, :, 1] = -s, c
    t[0, 0, :, 1, :, :, 0], t[0, 1, :, 1, :, :, 0] = c, s
    t[0, 2, :, 1, :, :, 0], t[0, 3, :, 1, :, :, 0] = s, -c
    t[0, 0, :, 1, :, :, 1], t[0, 1, :, 1, :, :, 1] = -c, -s
    t[0, 2, :, 1, :, :, 1], t[0, 3, :, 1, :, :, 1] = -s, c
    t[1, 0, :, 1, :, :, 1], t[1, 1, :, 1, :, :, 1] = -s, c
    t[1, 2, :, 1, :, :, 1], t[1, 3, :, 1, :, :, 1] = c, s
    phi = 2 * math.pi * ((np.arange(32)[:, None] * np.arange(32)[None, :]) % 32) / 32
    e = np.zeros((32, 2, 2, 32))
    e[:, 0, 0], e[:, 0, 1] = np.cos(phi), np.cos(phi)
    e[:, 1, 0], e[:, 1, 1] = np.sin(phi), -np.sin(phi)
    return w.reshape(512, 1024), t.reshape(16, 64, 256).astype(np.float32), e.reshape(32, 128)


def across_tables():
    p, bc = np.meshgrid(np.arange(16), np.arange(8), indexing="ij")
    m1 = np.arange(256)[None, None, :]
    w = np.zeros((2, 2, 128, 2, 256))
    for s in range(2):
        v1 = (8 * p + bc if s == 0 else 8 * (31 - p) + bc).reshape(128, 1)
        phi = 2 * math.pi * ((v1 * np.arange(256)[None, :]) % 256) / 256
        w[s, 0, :, 0], w[s, 1, :, 0] = np.cos(phi), -np.sin(phi)
        w[s, 0, :, 1], w[s, 1, :, 1] = np.sin(phi), np.cos(phi)
    zero = w[0].copy()
    zero[1, 0, 0] = 1 - 2 * (np.arange(256) % 2)
    zero[1, 0, 1] = 0
    psi = 2 * math.pi * np.arange(17)[:, None] * np.arange(256)[None, :] / G
    twist = np.concatenate([np.cos(psi), np.sin(psi)], axis=1).astype(np.float32)
    return w.reshape(512, 512), zero.reshape(256, 512), twist


def turn(t):
    quarter = jnp.round(t * 4.0)
    x = (t - quarter * 0.25) * (2 * math.pi)
    y = x * x
    sine = x * (1 + y * (-1 / 6 + y * (1 / 120 + y * (-1 / 5040 + y * (1 / 362880)))))
    cosine = 1 + y * (-0.5 + y * (1 / 24 + y * (-1 / 720 + y * (1 / 40320))))
    q = quarter.astype(jnp.int32)
    odd = (q & 1) != 0
    c = jnp.where(odd, sine, cosine)
    s = jnp.where(odd, cosine, sine)
    c = jnp.where(((q + 1) & 2) != 0, -c, c)
    s = jnp.where((q & 2) != 0, -s, s)
    return c, s


def times(x, y):
    return x[0] * y[0] - x[1] * y[1], x[0] * y[1] + x[1] * y[0]


def conj(x):
    return x[0], -x[1]


def grid_kernel(
    uv_ref, vis_ref, beam_ref, seg_ref, slot_ref, d1h, d1l, d2h, d2l,
    out_ref,
    base_l, base_m, fact_l, fact_m, image, ch, cl, ah, al,
):
    step = pl.program_id(0)
    n = STEP
    zu = turn(uv_ref[:, 0, :] * (1 / 32))
    zv = turn(uv_ref[:, 1, :] * (1 / 32))
    vis = (vis_ref[:, 0, :], vis_ref[:, 1, :])
    u2 = times(zu, zu)
    u3 = times(u2, zu)
    u4 = times(u2, u2)
    u8 = times(u4, u4)
    u12 = times(u8, u4)
    u16 = times(u8, u8)
    for i, f in enumerate((conj(u16), conj(u12), conj(u8), conj(u4), None, u4, u8, u12)):
        b = vis if f is None else times(vis, f)
        base_l[0, pl.ds(i, n, stride=8), :] = b[0]
        base_l[1, pl.ds(i, n, stride=8), :] = b[1]
    for i, f in enumerate((zu, u2, u3)):
        fact_l[2 * i] = f[0]
        fact_l[2 * i + 1] = f[1]
    v2 = times(zv, zv)
    v3 = times(v2, zv)
    v4 = times(v2, v2)
    v5 = times(v4, zv)
    v6 = times(v4, v2)
    v7 = times(v4, v3)
    v8 = times(v4, v4)
    v16 = times(v8, v8)
    one = (jnp.ones_like(zv[0]), jnp.zeros_like(zv[0]))
    for i, f in enumerate((one, zv, v2, v3, v4, v5, v6, v7)):
        base_m[0, pl.ds(i, n, stride=8), :] = f[0]
        base_m[1, pl.ds(i, n, stride=8), :] = f[1]
    for i, f in enumerate((conj(v16), conj(v8), v8)):
        fact_m[2 * i] = f[0]
        fact_m[2 * i + 1] = f[1]

    def one_block(b, _):
        rows = pl.ds(pl.multiple_of(b * 8, 8), 8)
        line = pl.ds(b, 1)
        bl = (base_l[0, rows, :], base_l[1, rows, :])
        bm = (base_m[0, rows, :], base_m[1, rows, :])
        left, right = [], []
        for t in range(4):
            w = bl if t == 0 else times(bl, (fact_l[2 * t - 2, line, :], fact_l[2 * t - 1, line, :]))
            left += [w[0], w[1]]
            right += [-w[1], w[0]]
        lh, ll = split(jnp.concatenate(
            [jnp.concatenate(left, axis=0), jnp.concatenate(right, axis=0)], axis=1))
        cosine, sine = [], []
        for t in range(4):
            i = {0: 0, 1: 1, 3: 2}.get(t)
            w = bm if i is None else times(bm, (fact_m[2 * i, line, :], fact_m[2 * i + 1, line, :]))
            cosine.append(w[0])
            sine.append(w[1])
        mh, ml = split(jnp.concatenate(
            [jnp.concatenate(cosine, axis=0), jnp.concatenate(sine, axis=0)], axis=1))
        o = dot_nt(lh, mh) + (dot_nt(ll, mh) + dot_nt(lh, ml))
        image[0, rows, :] = jnp.concatenate([o[16 * t:16 * t + 8] for t in range(4)], axis=1)
        image[1, rows, :] = jnp.concatenate([o[16 * t + 8:16 * t + 16] for t in range(4)], axis=1)
        return 0

    lax.fori_loop(0, n, one_block, 0, unroll=4)

    here = pl.ds(pl.multiple_of(step * n, n), n)
    for l8 in range(8):
        im = (image[0, pl.ds(l8, n, stride=8), :], image[1, pl.ds(l8, n, stride=8), :])
        bm = (beam_ref[0, :, l8 * 128:(l8 + 1) * 128], beam_ref[1, :, l8 * 128:(l8 + 1) * 128])
        c = times(bm, im)
        for ri in range(2):
            h, l = split(c[ri])
            ch[here, (2 * l8 + ri) * 128:(2 * l8 + ri + 1) * 128] = h
            cl[here, (2 * l8 + ri) * 128:(2 * l8 + ri + 1) * 128] = l

    @pl.when(step == pl.num_programs(0) - 1)
    def _():
        subs = slot_ref.shape[1]
        blocks = seg_ref.shape[1]
        pick = (seg_ref[...] == lax.broadcasted_iota(jnp.int32, (subs, blocks), 0)).astype(F32).astype(BF16)
        for l8 in range(8):
            lanes = slice(l8 * 256, (l8 + 1) * 256)
            ih, il = split(dot(pick, ch[:, lanes]) + dot(pick, cl[:, lanes]))
            a = dot3(ih, il, d1h[...], d1l[...])
            for cg in range(2):
                h, l = split(a[:, cg * 128:(cg + 1) * 128])
                ah[cg * subs:(cg + 1) * subs, l8 * 128:(l8 + 1) * 128] = h
                al[cg * subs:(cg + 1) * subs, l8 * 128:(l8 + 1) * 128] = l
        slots = 2 * 256
        place = (slot_ref[...] == lax.broadcasted_iota(jnp.int32, (slots, subs), 0)).astype(F32).astype(BF16)
        place = jnp.concatenate([place, place], axis=1)
        for tile in range(4):
            lanes = slice(tile * 256, (tile + 1) * 256)
            spec = dot3(ah[...], al[...], d2h[:, lanes], d2l[:, lanes])
            for cg in range(2):
                h, l = split(spec[cg * subs:(cg + 1) * subs])
                o = dot(place, jnp.concatenate([h, l], axis=0))
                j = cg * 8 + tile * 2
                out_ref[j * slots:(j + 1) * slots, :] = o[:, :128]
                out_ref[(j + 1) * slots:(j + 2) * slots, :] = o[:, 128:]


def make_outbox(uv, vis, beam, seg, slot, tables):
    blocks, _, visible = uv.shape
    subs = slot.shape[1]
    (d1h, d1l), (d2h, d2l) = [halves(t) for t in tables]
    whole = lambda shape: pl.BlockSpec(shape, lambda i: (0,) * len(shape))
    return pl.pallas_call(
        grid_kernel,
        grid=(blocks // STEP,),
        in_specs=[
            pl.BlockSpec((STEP, 2, visible), lambda i: (i, 0, 0)),
            pl.BlockSpec((STEP, 2, visible), lambda i: (i, 0, 0)),
            pl.BlockSpec((2, STEP, SUB * SUB), lambda i: (0, i, 0)),
            whole((1, blocks)), whole((1, subs)),
            whole((256, 256)), whole((256, 256)), whole((1024, 1024)), whole((1024, 1024)),
        ],
        out_specs=whole((8192, 128)),
        out_shape=jax.ShapeDtypeStruct((8192, 128), F32),
        scratch_shapes=[
            pltpu.VMEM((2, STEP * 8, 128), F32),
            pltpu.VMEM((2, STEP * 8, 128), F32),
            pltpu.VMEM((6, STEP, 128), F32),
            pltpu.VMEM((6, STEP, 128), F32),
            pltpu.VMEM((2, STEP * 8, 128), F32),
            pltpu.VMEM((blocks, 2048), BF16),
            pltpu.VMEM((blocks, 2048), BF16),
            pltpu.VMEM((2 * subs, 1024), BF16),
            pltpu.VMEM((2 * subs, 1024), BF16),
        ],
        compiler_params=pltpu.CompilerParams(vmem_limit_bytes=48 * MB),
        name="gridding",
    )(uv, vis, beam, seg, slot, d1h, d1l, d2h, d2l)


def place_kernel(data_ref, label_ref, out_ref, grid_ref):
    pos = lax.broadcasted_iota(jnp.int32, (256, 256), 0).astype(F32)

    def one(i, _):
        s, r = i // 8, i % 8
        hot, data = [], []
        for k in range(2):
            slot = i * 2 + k
            label = label_ref[pl.ds(slot, 1), :]
            hot.append((label == pos).astype(F32).astype(BF16))
            data.append(data_ref[pl.ds(slot, 256, stride=32), :])
        h, l = split(jnp.concatenate(data, axis=0))
        g = dot(jnp.concatenate(hot, axis=1), jnp.concatenate([h, l], axis=1))
        g = g[:, :128] + g[:, 128:]
        for bc in range(8):
            grid_ref[s * 8 + bc, pl.ds(pl.multiple_of(r * 32, 32), 32), :] = g[bc * 32:(bc + 1) * 32]
        return 0

    lax.fori_loop(0, 16, one, 0)

    def flip(i, _):
        out_ref[i] = grid_ref[i].T
        return 0

    lax.fori_loop(0, 16, flip, 0)


def place(data, labels):
    return pl.pallas_call(
        place_kernel,
        out_shape=jax.ShapeDtypeStruct((16, 128, 256), F32),
        scratch_shapes=[pltpu.VMEM((16, 256, 128), F32)],
        compiler_params=pltpu.CompilerParams(vmem_limit_bytes=32 * MB),
        name="placing",
    )(data, labels)


def down_kernel(flag_ref, x_ref, extra_ref, wh, wl, t_ref, eh, el, out_ref, lh, ll):
    zero_class = flag_ref[0]
    special = flag_ref[1]
    for bc in range(8):
        for s in range(2):
            plain = (s * 8 + bc) * 128
            other = ((1 - s) * 8 + 7 - bc) * 128 + 64
            if s == 0:
                own = x_ref[plain:plain + 64, :]
                if bc == 0:
                    mirror = jnp.where(zero_class == 1, extra_ref[...], x_ref[other:other + 64, :])
                else:
                    off = jnp.where(zero_class == 1, (16 - bc) * 128, other)
                    mirror = x_ref[pl.ds(pl.multiple_of(off, 64), 64), :]
            else:
                off = jnp.where(zero_class == 1, bc * 128 + 64, plain)
                own = x_ref[pl.ds(pl.multiple_of(off, 64), 64), :]
                off = jnp.where(zero_class == 1, (15 - bc) * 128 + 64, other)
                mirror = x_ref[pl.ds(pl.multiple_of(off, 64), 64), :]
            for c2, v in enumerate((own, mirror)):
                h, l = split(v)
                row = (bc * 2 + s) * 64 + c2 * 32
                for ri in range(2):
                    lh[row:row + 32, ri * 256:(ri + 1) * 256] = h[ri * 32:(ri + 1) * 32]
                    ll[row:row + 32, ri * 256:(ri + 1) * 256] = l[ri * 32:(ri + 1) * 32]
    e2 = jnp.concatenate([eh[...], eh[...]], axis=1)
    low = lax.broadcasted_iota(jnp.int32, (32, 128), 1) < 64

    def one(i, _):
        rows = pl.ds(pl.multiple_of(i * 256, 256), 256)
        for nt in range(2):
            cols = slice(nt * 512, (nt + 1) * 512)
            y = dot3(lh[rows, :], ll[rows, :], wh[:, cols], wl[:, cols])
            for k in range(2):
                bc = i * 2 + k
                parts = []
                for s in range(2):
                    r = (k * 2 + s) * 64
                    ya, yb = y[r:r + 64, :256], y[r:r + 64, 256:]
                    which = 0
                    if s == 0 and k == 0:
                        which = jnp.where(i == 0, special, 0)
                    tab = lambda n: t_ref[which * 8 + n * 2 + nt]
                    parts.append(jnp.concatenate(
                        [ya * tab(0) + yb * tab(1), ya * tab(2) + yb * tab(3)], axis=0))
                th, tl = split(jnp.concatenate(parts, axis=1))
                o = dot(e2, jnp.concatenate([th, tl], axis=0)) + dot(el[...], th)
                for g in range(2):
                    o0 = o[:, g * 128:(g + 1) * 128]
                    o1 = o[:, 256 + g * 128:256 + (g + 1) * 128]
                    q = nt * 4 + g * 2
                    out_ref[pl.ds(q * 8 + bc, 32, stride=64), :] = jnp.where(low, o0, pltpu.roll(o1, 64, 1))
                    out_ref[pl.ds((q + 1) * 8 + bc, 32, stride=64), :] = jnp.where(low, pltpu.roll(o0, 64, 1), o1)
        return 0

    lax.fori_loop(0, 4, one, 0)


def down(flags, x, extra):
    w, t, e = down_tables()
    wh, wl = halves(w)
    eh, el = halves(e)
    vmem = pl.BlockSpec(memory_space=pltpu.VMEM)
    return pl.pallas_call(
        down_kernel,
        in_specs=[pl.BlockSpec(memory_space=pltpu.SMEM)] + [vmem] * 7,
        out_shape=jax.ShapeDtypeStruct((2048, 128), F32),
        scratch_shapes=[pltpu.VMEM((1024, 512), BF16), pltpu.VMEM((1024, 512), BF16)],
        compiler_params=pltpu.CompilerParams(vmem_limit_bytes=40 * MB),
        name="down",
    )(flags, x, extra, wh, wl, t, eh, el)


def across_kernel(k_ref, wh, wl, zh, zl, twist, out_ref, lh, ll, y_ref):
    for j in range(16):
        a = k_ref[j * 128:(j + 1) * 128, :].T
        h, l = split(a)
        for i in range(4):
            lh[j * 32:(j + 1) * 32, i * 128:(i + 1) * 128] = h[i * 32:(i + 1) * 32]
            ll[j * 32:(j + 1) * 32, i * 128:(i + 1) * 128] = l[i * 32:(i + 1) * 32]
    y_ref[0:32] = dot3(lh[0:32, :256], ll[0:32, :256], zh[...], zl[...])
    y_ref[512:544] = dot3(lh[0:32, 256:], ll[0:32, 256:], wh[:256, :], wl[:256, :])
    y_ref[32:512] = dot3(lh[32:512, :], ll[32:512, :], wh[...], wl[...])

    cos = [math.cos(2 * math.pi * i / 32) for i in range(32)]
    sin = [math.sin(2 * math.pi * i / 32) for i in range(32)]

    def combine(terms):
        total = None
        for f, x in terms:
            if abs(f) < 1e-12:
                continue
            v = x if f == 1.0 else -x if f == -1.0 else x * f
            total = v if total is None else total + v
        return total

    def rows(i, _):
        at = pl.multiple_of(i * 8, 8)
        for half in range(2):
            lane = slice(half * 128, (half + 1) * 128)
            tre, tim = [], []
            for v in range(17):
                yre = y_ref[pl.ds(v * 32 + at, 8), lane]
                yim = y_ref[pl.ds(v * 32 + at, 8), 256 + half * 128:256 + (half + 1) * 128]
                c = twist[v:v + 1, lane]
                s = twist[v:v + 1, 256 + half * 128:256 + (half + 1) * 128]
                tre.append(yre * c - yim * s)
                tim.append(yre * s + yim * c)
            for m2 in range(9):
                e0 = combine([(cos[v * m2 % 32], tre[v]) for v in range(0, 17, 2)])
                e1 = combine([(cos[v * m2 % 32], tre[v]) for v in range(1, 17, 2)])
                o0 = combine([(sin[v * m2 % 32], tim[v]) for v in range(0, 17, 2)])
                o1 = combine([(sin[v * m2 % 32], tim[v]) for v in range(1, 17, 2)])
                zero = jnp.zeros((8, 128), F32)
                e0, e1, o0, o1 = [zero if x is None else x for x in (e0, e1, o0, o1)]
                puts = {m2: (e0 + e1) - (o0 + o1), (32 - m2) % 32: (e0 + e1) + (o0 + o1)}
                puts[16 - m2] = (e0 - e1) + (o0 - o1)
                puts[16 + m2] = (e0 - e1) - (o0 - o1)
                for m, v in puts.items():
                    out_ref[pl.ds(at, 8), m * 256 + half * 128:m * 256 + (half + 1) * 128] = v
        return 0

    lax.fori_loop(0, 4, rows, 0)


def across(k):
    w, zero, twist = across_tables()
    wh, wl = halves(w)
    zh, zl = halves(zero)
    return pl.pallas_call(
        across_kernel,
        out_shape=jax.ShapeDtypeStruct((32, G), F32),
        scratch_shapes=[
            pltpu.VMEM((512, 512), BF16), pltpu.VMEM((512, 512), BF16), pltpu.VMEM((544, 512), F32),
        ],
        compiler_params=pltpu.CompilerParams(vmem_limit_bytes=32 * MB),
        name="across",
    )(k, wh, wl, zh, zl, twist)


def body(uv, vis, left, right, block_subgrid, subgrid_tile, block_row, block_col):
    axes = ("row", "col")
    devices = lax.axis_size("row") * lax.axis_size("col")
    me = lax.axis_index("row") * lax.axis_size("col") + lax.axis_index("col")
    subs = subgrid_tile.shape[0]
    visible = uv.shape[2]

    tile = subgrid_tile[:, 0]
    ids = jnp.arange(subs, dtype=jnp.int32)
    earlier = (tile[None, :] == tile[:, None]) & (ids[None, :] < ids[:, None])
    rank = jnp.sum(earlier.astype(jnp.int32), axis=1)
    band = tile % 32
    side = (band >= 16).astype(jnp.int32)
    pair = jnp.where(side == 1, 31 - band, band)
    slot = pair * 32 + side * 16 + (tile // 32) * 2 + rank
    code = block_col * 32 + block_row + 1
    match = slot[None, :] == jnp.arange(512, dtype=jnp.int32)[:, None]
    labels = jnp.sum(jnp.where(match, code[None, :], 0), axis=1).astype(F32) - 1.0
    labels = jnp.broadcast_to(labels.reshape(1, PAIRS, 32), (CLASSES, PAIRS, 32)).reshape(devices, 32)
    labels = lax.all_to_all(labels, axes, split_axis=0, concat_axis=0, tiled=True).T

    l, r = left.astype(F32), right.astype(F32)
    beam = jnp.stack([
        l[:, 0] * r[:, 0] + l[:, 1] * r[:, 1],
        l[:, 1] * r[:, 0] - l[:, 0] * r[:, 1],
    ])
    outbox = make_outbox(uv, vis, beam, block_subgrid, slot[None, :], subgrid_tables(visible))
    arrived = lax.all_to_all(
        outbox.reshape(devices, 32, 128), axes, split_axis=0, concat_axis=0, tiled=True
    ).reshape(devices * 32, 128)
    x = place(arrived, labels)
    move = [(j * PAIRS + p, j * PAIRS + (p + 1) % PAIRS) for j in range(CLASSES) for p in range(PAIRS)]
    extra = lax.ppermute(x[8, :64], axes, move)
    flags = jnp.stack([me < PAIRS, me == 0]).astype(jnp.int32)
    k = down(flags, x.reshape(2048, 256), extra)
    k = lax.all_to_all(k.reshape(devices, 8, 128), axes, split_axis=0, concat_axis=0, tiled=True)
    return across(k.reshape(2048, 128))


def solution(mesh):
    placed = (
        P(("row", "col"), None, None),
        P(("row", "col"), None, None),
        P(("row", "col"), None, None),
        P(("row", "col"), None, None),
        P(("row", "col"), None),
        P(("row", "col"), None),
        P(("row", "col")),
        P(("row", "col")),
    )
    return jax.shard_map(
        body, mesh=mesh, in_specs=placed, out_specs=P(("row", "col"), None), check_vma=False
    )
```

time: 655 us -> 244 us (0.37)
  matrix products: 207 us -> 0 us
  local copies, waits for them, and re-layouts: 131 us -> 2.32 us
  waiting for transfers between devices: 171 us -> 103 us
  Pallas kernels: 0 us -> 61.7 us
  blocking collectives: 86.5 us -> 38.3 us
  loops' own time: 9.01 us -> 0 us
    dot_general x32 -> x0, matrix products: 207 us -> none  [the longest x2 36.3 us: phasor_image(): jnp.einsum(pattern, wave_re, sin_m, precision=exact_prec)]
    all_to_all x5 -> x2, waiting for transfers between devices: 171 us -> 96.3 us  [the longest x1 96.3 us: body(): lax.all_to_all(outbox.reshape(devices, 32, 128), axes, split_axis=0, conc...]
    pallas_call x0 -> x4, Pallas kernels: none -> 61.7 us  [the longest x1 42.2 us: make_outbox(): pl.pallas_call(grid_kernel, grid=(blocks // STEP,), in_specs=[pl.BlockSpe...]
    all_to_all x2 -> x1, blocking collectives: 86.5 us -> 38.3 us  [body(): lax.all_to_all(k.reshape(devices, 8, 128), axes, split_axis=0, concat_axi...]
    reshape x6 -> x0, local copies, waits for them, and re-layouts: 31 us -> none  [the longest x2 18.2 us: body(): tile_grid = summed.reshape(blocks_down, blocks_across, 2, SUB, SUB).trans...]
    all_to_all x9 -> x1, local copies, waits for them, and re-layouts: 28.7 us -> 0.06 us  [body(): lax.all_to_all(labels, axes, split_axis=0, concat_axis=0, tiled=True)]
    unnamed x23 -> x32, local copies, waits for them, and re-layouts: 22.2 us -> 1.5 us
    another operation x7 -> x0, local copies, waits for them, and re-layouts: 17.2 us -> none  [the longest x3 12.8 us: transform_down(): return jnp.stack([out_re.reshape(length, -1), out_im.reshape(length, -1)])]
  transfers between devices with their start and end apart: 5 -> 3, of which waited for: 4 -> 2; matrix products, arithmetic and copies ran while one was open for 29% -> 2% of each run, Pallas kernels for 0% -> 17%
where the time goes in v1:
time: 244 us; the launch traced here: 241 us
  waiting for transfers between devices  103 us (42%)
  Pallas kernels  61.7 us (25%)
  blocking collectives  38.3 us (16%)
  starting transfers between devices  29.4 us (12%)
  other arithmetic  6.3 us (3%)
    all_to_all x1, waiting for transfers between devices, body(): lax.all_to_all(outbox.reshape(devices, 32, 128), axes, split_axis=0, conc...  96.3 us
    pallas_call x1, Pallas kernels, make_outbox(): pl.pallas_call(grid_kernel, grid=(blocks // STEP,), in_specs=[pl.BlockSpe...  42.2 us
    all_to_all x1, blocking collectives, body(): lax.all_to_all(k.reshape(devices, 8, 128), axes, split_axis=0, concat_axi...  38.3 us
    all_to_all x1, starting transfers between devices, body(): lax.all_to_all(outbox.reshape(devices, 32, 128), axes, split_axis=0, conc...  14.7 us
    all_to_all x1, starting transfers between devices, body(): lax.all_to_all(labels, axes, split_axis=0, concat_axis=0, tiled=True)  14.4 us
    pallas_call x1, Pallas kernels, place(): pl.pallas_call(place_kernel, out_shape=jax.ShapeDtypeStruct((16, 128, 256...  9.48 us
    pallas_call x1, Pallas kernels, down(): pl.pallas_call(down_kernel, in_specs=[pl.BlockSpec(memory_space=pltpu.SME...  7.21 us
    ppermute x1, waiting for transfers between devices, body(): extra = lax.ppermute(x[8, :64], axes, move)  6.46 us
  transfers between devices with their start and end apart: 3, of which 2 were waited for; matrix products, arithmetic and copies ran while one was open for 2% of the time, Pallas kernels for 17%

profile of v1, /device:TPU:32, one launch (start us, length us, event | category | flops | bytes accessed | tf_op | source)
XLA Modules:
  0.0 241.1 jit_solution(8987529572850685523)
XLA Ops:
  0.0 0.9 convert_reduce_fusion
  0.9 0.7 fusion.8
  1.6 0.7 add_add_fusion
  2.3 0.1 select_reduce_fusion
  2.4 0.1 sub.48
  2.5 0.7 broadcast_in_dim.16
  3.2 14.4 %all-to-all-start.1 = ((f32[256,1,32]{2,1,0:T(1,128)}), f32[256,1,32]{2,1,0:T(1,128)S(1)}, u32[]{:S(2)}, u32[]{:S(2)}) async-start(f32[256,1,32]{2,1,0:T(1,128)} %bitcast.10), calls=%async_computation.1 | async-start | bytes 262144 | tf_op jit(solution)/shard_map/all_to_all | solution.py:489
  17.6 0.7 fusion.6.slot_ref
  18.2 2.3 copy_convert_fusion
  20.5 0.6 add_bitcast_fusion
  21.2 0.0 copy-start
  21.2 0.0 copy-start.8
  21.2 0.0 copy-start.9
  21.2 0.0 copy-start.10
  21.2 0.0 copy-start.11
  21.2 0.0 copy-start.15
  21.2 0.2 pad_maximum_fusion.beam_ref
  21.5 1.3 copy-done
  22.8 0.0 copy-done.8
  22.8 0.1 copy-done.9
  22.8 0.0 copy-done.10
  22.9 0.0 copy-done.11
  22.9 0.0 copy-done.15
  22.9 42.2 %gridding.1 = f32[8192,128]{1,0:T(8,128)} custom-call(f32[256,2,128]{2,1,0:T(2,128)S(1)} %copy-done.8, f32[256,2,128]{2,1,0:T(2,128)S(1)} %copy-done.9, f32[2,256,1024]{2,1,0:T(8,128)S(1)} %pad_maximum_fusion.beam_ref, s32[1,256]{1,0:T(1,128)S(1)} %copy-done.15, s32[1,128]{1,0:T(1,128)S(1)} %fusion.6.slot_ref, bf16[256,256]{1,0:T(8,128)(2,1)S(1)} %copy-done.10, ...), custom_call_target="tpu_custom_call" | custom-call | tf_op jit(solution)/shard_map/gridding/pallas_call | solution.py:265
  65.1 0.0 all-to-all-done.1
  65.1 14.7 %all-to-all-start = ((f32[256,32,128]{2,1,0:T(8,128)}), f32[256,32,128]{2,1,0:T(8,128)}, u32[]{:S(2)}, u32[]{:S(2)}) async-start(f32[256,32,128]{2,1,0:T(8,128)} %bitcast.40), calls=%async_computation | async-start | bytes 8388608 | tf_op jit(solution)/shard_map/all_to_all | solution.py:497
  79.8 0.1 copy.35
  79.9 96.3 %all-to-all-done = f32[256,32,128]{2,1,0:T(8,128)} async-done(((f32[256,32,128]{2,1,0:T(8,128)}), f32[256,32,128]{2,1,0:T(8,128)}, u32[]{:S(2)}, u32[]{:S(2)}) %all-to-all-start) | async-done | bytes 4194336 | tf_op jit(solution)/shard_map/all_to_all | solution.py:497
  176.2 0.0 copy-start.1
  176.2 0.0 copy-start.2
  176.2 0.0 copy-start.3
  176.2 0.0 copy-start.13
  176.2 0.0 copy-start.14
  176.2 9.5 %placing.1 = f32[16,128,256]{2,1,0:T(8,128)S(1)} custom-call(f32[8192,128]{1,0:T(8,128)} %bitcast.8.data_ref, f32[32,256]{1,0:T(8,128)S(1)} %bitcast.39), custom_call_target="tpu_custom_call" | custom-call | tf_op jit(solution)/shard_map/placing/pallas_call | solution.py:321
  185.7 0.3 collective-permute-start
  186.0 0.1 add_convert_fusion.flag_ref
  186.0 6.5 %collective-permute-done.extra_ref = f32[64,256]{1,0:T(8,128)S(1)} collective-permute-done((f32[64,256]{1,0:T(8,128)S(1)}, f32[64,256]{1,0:T(8,128)S(1)}, u32[]{:S(2)}, u32[]{:S(2)}) %collective-permute-start) | collective-permute-done | bytes 65568 | tf_op jit(solution)/shard_map/ppermute | solution.py:502
  192.5 0.0 copy-done.1
  192.5 0.0 copy-done.2
  192.5 0.0 copy-done.3
  192.5 0.0 copy-done.13
  192.5 0.0 copy-done.14
  192.5 7.2 %down.1 = f32[2048,128]{1,0:T(8,128)S(1)} custom-call(s32[2]{0:T(128)S(1)} %add_convert_fusion.flag_ref, f32[2048,256]{1,0:T(8,128)S(1)} %bitcast.36, f32[64,256]{1,0:T(8,128)S(1)} %collective-permute-done.extra_ref, bf16[512,1024]{1,0:T(8,128)(2,1)S(1)} %copy-done.1, bf16[512,1024]{1,0:T(8,128)(2,1)S(1)} %copy-done.2, f32[16,64,256]{2,1,0:T(8,128)S(1)} %copy-done.3, ...), custom_call_target="tpu_custom_call" | custom-call | tf_op jit(solution)/shard_map/down/pallas_call | solution.py:393
  199.8 0.0 copy-start.4
  199.8 0.0 copy-start.5
  199.8 0.0 copy-start.6
  199.8 0.0 copy-start.7
  199.8 0.0 copy-start.12
  199.8 38.3 %all_to_all.22 = f32[256,8,128]{2,1,0:T(8,128)S(1)} all-to-all(f32[256,8,128]{2,1,0:T(8,128)S(1)} %bitcast.37), channel_id=1, replica_groups=mesh['row'=8,'col'=32] {'row','col'}, dimensions={0} | all-to-all | bytes 2097152 | tf_op jit(solution)/shard_map/all_to_all | solution.py:505
  238.2 0.0 copy-done.4
  238.2 0.0 copy-done.5
  238.2 0.0 copy-done.6
  238.2 0.0 copy-done.7
  238.2 0.0 copy-done.12
  238.2 2.9 %across.1 = f32[32,8192]{1,0:T(8,128)} custom-call(f32[2048,128]{1,0:T(8,128)S(1)} %bitcast.38, bf16[512,512]{1,0:T(8,128)(2,1)S(1)} %copy-done.4, bf16[512,512]{1,0:T(8,128)(2,1)S(1)} %copy-done.5, bf16[256,512]{1,0:T(8,128)(2,1)S(1)} %copy-done.6, bf16[256,512]{1,0:T(8,128)(2,1)S(1)} %copy-done.7, f32[17,512]{1,0:T(8,128)S(1)} %copy-done.12), custom_call_target="tpu_custom_call" | custom-call | tf_op jit(solution)/shard_map/across/pallas_call | solution.py:459
  (2 shorter events, 0.0 us)
Async XLA Ops:
  3.2 61.9 %all-to-all-start.1 = ((f32[256,1,32]{2,1,0:T(1,128)}), f32[256,1,32]{2,1,0:T(1,128)S(1)}, u32[]{:S(2)}, u32[]{:S(2)}) async-start(f32[256,1,32]{2,1,0:T(1,128)} %bitcast.10), calls=%async_computation.1 | async-start | bytes 262144 | tf_op jit(solution)/shard_map/all_to_all | solution.py:489
  21.2 1.6 copy-start
  21.2 1.6 copy-start.8
  21.2 1.6 copy-start.9
  21.2 1.7 copy-start.10
  21.2 1.7 copy-start.11
  21.2 1.7 copy-start.15
  65.1 111.1 %all-to-all-start = ((f32[256,32,128]{2,1,0:T(8,128)}), f32[256,32,128]{2,1,0:T(8,128)}, u32[]{:S(2)}, u32[]{:S(2)}) async-start(f32[256,32,128]{2,1,0:T(8,128)} %bitcast.40), calls=%async_computation | async-start | bytes 8388608 | tf_op jit(solution)/shard_map/all_to_all | solution.py:497
  176.2 16.3 %copy-start.1 = (bf16[512,1024]{1,0:T(8,128)(2,1)S(1)}, bf16[512,1024]{1,0:T(8,128)(2,1)}, u32[]{:S(2)}) copy-start(bf16[512,1024]{1,0:T(8,128)(2,1)} %constant.82.clone.wh) | copy-start | bytes 3145732
  176.2 16.3 %copy-start.2 = (bf16[512,1024]{1,0:T(8,128)(2,1)S(1)}, bf16[512,1024]{1,0:T(8,128)(2,1)}, u32[]{:S(2)}) copy-start(bf16[512,1024]{1,0:T(8,128)(2,1)} %constant.83.clone.wl) | copy-start | bytes 3145732
  176.2 16.3 %copy-start.3 = (f32[16,64,256]{2,1,0:T(8,128)S(1)}, f32[16,64,256]{2,1,0:T(8,128)}, u32[]{:S(2)}) copy-start(f32[16,64,256]{2,1,0:T(8,128)} %constant.84.clone.t_ref) | copy-start | bytes 3145732
  176.2 16.3 %copy-start.13 = (bf16[32,128]{1,0:T(8,128)(2,1)S(1)}, bf16[32,128]{1,0:T(8,128)(2,1)}, u32[]{:S(2)}) copy-start(bf16[32,128]{1,0:T(8,128)(2,1)} %constant.85.clone.eh) | copy-start | bytes 24580
  176.2 16.4 %copy-start.14 = (bf16[32,128]{1,0:T(8,128)(2,1)S(1)}, bf16[32,128]{1,0:T(8,128)(2,1)}, u32[]{:S(2)}) copy-start(bf16[32,128]{1,0:T(8,128)(2,1)} %constant.86.clone.el) | copy-start | bytes 24580
  185.7 6.8 %collective-permute-start = (f32[64,256]{1,0:T(8,128)S(1)}, f32[64,256]{1,0:T(8,128)S(1)}, u32[]{:S(2)}, u32[]{:S(2)}) collective-permute-start(f32[64,256]{1,0:T(8,128)S(1)} %slice_bitcast_fusion), channel_id=1, source_target_pairs={{0,1},{1,2},{2,3},{3,4},{4,5},{5,6},{6,7},{7,8},{8,9},{9,10},{10,1... | collective-permute-start | bytes 196616 | tf_op jit(solution)/shard_map/ppermute | solution.py:502
  199.8 38.4 %copy-start.4 = (bf16[512,512]{1,0:T(8,128)(2,1)S(1)}, bf16[512,512]{1,0:T(8,128)(2,1)}, u32[]{:S(2)}) copy-start(bf16[512,512]{1,0:T(8,128)(2,1)} %constant.87.clone.wh) | copy-start | bytes 1572868
  199.8 38.4 %copy-start.5 = (bf16[512,512]{1,0:T(8,128)(2,1)S(1)}, bf16[512,512]{1,0:T(8,128)(2,1)}, u32[]{:S(2)}) copy-start(bf16[512,512]{1,0:T(8,128)(2,1)} %constant.88.clone.wl) | copy-start | bytes 1572868
  199.8 38.4 %copy-start.6 = (bf16[256,512]{1,0:T(8,128)(2,1)S(1)}, bf16[256,512]{1,0:T(8,128)(2,1)}, u32[]{:S(2)}) copy-start(bf16[256,512]{1,0:T(8,128)(2,1)} %constant.89.clone.zh) | copy-start | bytes 786436
  199.8 38.4 %copy-start.7 = (bf16[256,512]{1,0:T(8,128)(2,1)S(1)}, bf16[256,512]{1,0:T(8,128)(2,1)}, u32[]{:S(2)}) copy-start(bf16[256,512]{1,0:T(8,128)(2,1)} %constant.90.clone.zl) | copy-start | bytes 786436
  199.8 38.4 %copy-start.12 = (f32[17,512]{1,0:T(8,128)S(1)}, f32[17,512]{1,0:T(8,128)}, u32[]{:S(2)}) copy-start(f32[17,512]{1,0:T(8,128)} %constant.91.clone.twist) | copy-start | bytes 104452

commit v2 on v1

--- a/solution.py
+++ b/solution.py
@@ -8,7 +8,7 @@
 from jax import lax
 from jax.experimental import pallas as pl
 from jax.experimental.pallas import tpu as pltpu
-from jax.sharding import PartitionSpec as P
+from jax.sharding import Mesh, PartitionSpec as P
 
 G = 8192
 SUB = 32
@@ -155,7 +155,7 @@
 
 
 def grid_kernel(
-    uv_ref, vis_ref, beam_ref, seg_ref, slot_ref, d1h, d1l, d2h, d2l,
+    uv_ref, vis_ref, beam_ref, seg_ref, tile_ref, row_ref, col_ref, d1h, d1l, d2h, d2l,
     out_ref,
     base_l, base_m, fact_l, fact_m, image, ch, cl, ah, al,
 ):
@@ -232,7 +232,21 @@
 
     @pl.when(step == pl.num_programs(0) - 1)
     def _():
-        subs = slot_ref.shape[1]
+        subs = tile_ref.shape[0]
+        tall = subs + 8
+        down_it = jnp.broadcast_to(tile_ref[...].astype(F32), (subs, subs))
+        along = down_it.T
+        ids = [lax.broadcasted_iota(jnp.int32, (subs, subs), d) for d in range(2)]
+        earlier = (down_it == along) & (ids[0] < ids[1])
+        rank = jnp.sum(earlier.astype(F32), axis=0, keepdims=True).astype(jnp.int32)
+        tile = along[:1].astype(jnp.int32)
+        band = tile % 32
+        side = (band >= 16).astype(jnp.int32)
+        pair = jnp.where(side == 1, 31 - band, band)
+        slot = pair * 32 + side * 16 + (tile // 32) * 2 + rank
+        code = (slot * 256 + col_ref[...] * 32 + row_ref[...]).astype(F32)
+        for j in range(CLASSES):
+            out_ref[j * tall + subs:(j + 1) * tall, :] = jnp.broadcast_to(code, (8, subs))
         blocks = seg_ref.shape[1]
         pick = (seg_ref[...] == lax.broadcasted_iota(jnp.int32, (subs, blocks), 0)).astype(F32).astype(BF16)
         for l8 in range(8):
@@ -243,23 +257,19 @@
                 h, l = split(a[:, cg * 128:(cg + 1) * 128])
                 ah[cg * subs:(cg + 1) * subs, l8 * 128:(l8 + 1) * 128] = h
                 al[cg * subs:(cg + 1) * subs, l8 * 128:(l8 + 1) * 128] = l
-        slots = 2 * 256
-        place = (slot_ref[...] == lax.broadcasted_iota(jnp.int32, (slots, subs), 0)).astype(F32).astype(BF16)
-        place = jnp.concatenate([place, place], axis=1)
         for tile in range(4):
             lanes = slice(tile * 256, (tile + 1) * 256)
             spec = dot3(ah[...], al[...], d2h[:, lanes], d2l[:, lanes])
             for cg in range(2):
-                h, l = split(spec[cg * subs:(cg + 1) * subs])
-                o = dot(place, jnp.concatenate([h, l], axis=0))
-                j = cg * 8 + tile * 2
-                out_ref[j * slots:(j + 1) * slots, :] = o[:, :128]
-                out_ref[(j + 1) * slots:(j + 2) * slots, :] = o[:, 128:]
-
-
-def make_outbox(uv, vis, beam, seg, slot, tables):
+                for k in range(2):
+                    j = cg * 8 + tile * 2 + k
+                    out_ref[j * tall:j * tall + subs, :] = spec[cg * subs:(cg + 1) * subs, k * 128:(k + 1) * 128]
+
+
+def make_payload(uv, vis, beam, seg, tile, row, col, tables):
     blocks, _, visible = uv.shape
-    subs = slot.shape[1]
+    subs = tile.shape[0]
+    tall = subs + 8
     (d1h, d1l), (d2h, d2l) = [halves(t) for t in tables]
     whole = lambda shape: pl.BlockSpec(shape, lambda i: (0,) * len(shape))
     return pl.pallas_call(
@@ -269,11 +279,11 @@
             pl.BlockSpec((STEP, 2, visible), lambda i: (i, 0, 0)),
             pl.BlockSpec((STEP, 2, visible), lambda i: (i, 0, 0)),
             pl.BlockSpec((2, STEP, SUB * SUB), lambda i: (0, i, 0)),
-            whole((1, blocks)), whole((1, subs)),
+            whole((1, blocks)), whole((subs, 1)), whole((1, subs)), whole((1, subs)),
             whole((256, 256)), whole((256, 256)), whole((1024, 1024)), whole((1024, 1024)),
         ],
-        out_specs=whole((8192, 128)),
-        out_shape=jax.ShapeDtypeStruct((8192, 128), F32),
+        out_specs=whole((CLASSES * tall, 128)),
+        out_shape=jax.ShapeDtypeStruct((CLASSES * tall, 128), F32),
         scratch_shapes=[
             pltpu.VMEM((2, STEP * 8, 128), F32),
             pltpu.VMEM((2, STEP * 8, 128), F32),
@@ -287,65 +297,193 @@
         ],
         compiler_params=pltpu.CompilerParams(vmem_limit_bytes=48 * MB),
         name="gridding",
-    )(uv, vis, beam, seg, slot, d1h, d1l, d2h, d2l)
-
-
-def place_kernel(data_ref, label_ref, out_ref, grid_ref):
+    )(uv, vis, beam, seg, tile, row, col, d1h, d1l, d2h, d2l)
+
+
+MESH = pl.DeviceIdType.MESH
+
+
+def device(pair, kind):
+    return (pair // 4, kind % 2, kind // 2, pair % 4)
+
+
+def exchange_kernel(
+    src_ref, out_ref, extra_ref,
+    near, box, held, grid_ref, edge_src, edge_in,
+    near_send, near_recv, far_send, far_recv, edge_send, edge_recv,
+):
+    group = lax.axis_index("y") * 4 + lax.axis_index("x")
+    kind = lax.axis_index("z") * 2 + lax.axis_index("core")
+    tall = src_ref.shape[0] // CLASSES
+    subs = tall - 8
+    part = 8 * 32 + 8
+
+    barrier = pltpu.get_barrier_semaphore()
+
+    def greet(k, _):
+        pl.semaphore_signal(barrier, inc=1, device_id=device(group, (kind + k) % 16), device_id_type=MESH)
+        pl.semaphore_signal(barrier, inc=1, device_id=device((group + k) % 16, kind), device_id_type=MESH)
+        return 0
+
+    lax.fori_loop(1, 16, greet, 0)
+    pl.semaphore_wait(barrier, 30)
+
+    def near_copy(k):
+        to = (kind + k) % 16
+        return pltpu.make_async_remote_copy(
+            src_ref=src_ref.at[pl.ds(pl.multiple_of(to * tall, 8), tall), :],
+            dst_ref=near.at[k],
+            send_sem=near_send.at[k],
+            recv_sem=near_recv.at[k],
+            device_id=device(group, to),
+            device_id_type=MESH,
+        )
+
+    def far_copy(g, k):
+        to = (group + k) % 16
+        h, rows = g // 2, pl.ds((g % 2) * 128, 128 + 8 * (g % 2))
+        return pltpu.make_async_remote_copy(
+            src_ref=box.at[h, to, rows, :],
+            dst_ref=held.at[h, k, rows, :],
+            send_sem=far_send.at[g, k],
+            recv_sem=far_recv.at[g, k],
+            device_id=device((group + k) % 16, kind),
+            device_id_type=MESH,
+        )
+
+    def loop(lo, hi, f):
+        def step(k, _):
+            f(k)
+            return 0
+
+        lax.fori_loop(lo, hi, step, 0)
+
+    loop(1, 16, lambda k: near_copy(k).start())
+    near[0] = src_ref[pl.ds(pl.multiple_of(kind * tall, 8), tall), :]
+
+    slots = lax.broadcasted_iota(jnp.int32, (512, subs), 0)
+    line = lax.broadcasted_iota(jnp.int32, (8, subs), 0)
+
+    def unfold(h, k8, codes):
+        k = h * 8 + k8
+        code = near[k, subs:subs + 1, :]
+        fits = (code.astype(jnp.int32) // 256 == slots).astype(F32).astype(BF16)
+        hi, lo = split(near[k, :subs, :])
+        o = dot(jnp.concatenate([fits, fits], axis=1), jnp.concatenate([hi, lo], axis=0))
+        rows = pl.ds(pl.multiple_of(k8 * 32, 32), 32)
+        for p in range(PAIRS):
+            box[h, p, rows, :] = o[p * 32:(p + 1) * 32]
+        return jnp.where(line == k8, code, codes)
+
+    for g in range(4):
+        h = g // 2
+        if g % 2 == 0:
+            codes = jnp.zeros((8, subs), F32)
+
+        def one(i, codes):
+            k8 = (g % 2) * 4 + i
+            near_copy(h * 8 + k8).wait_recv()
+            return unfold(h, k8, codes)
+
+        if g == 0:
+            codes = unfold(0, 0, codes)
+        codes = lax.fori_loop(1 if g == 0 else 0, 4, one, codes)
+        if g % 2 == 1:
+            for p in range(PAIRS):
+                box[h, p, 256:264, :] = codes
+        loop(1, 16, lambda k: far_copy(g, k).start())
+        if g % 2 == 1:
+            held[h, 0] = box[h, group]
+
     pos = lax.broadcasted_iota(jnp.int32, (256, 256), 0).astype(F32)
-
-    def one(i, _):
-        s, r = i // 8, i % 8
-        hot, data = [], []
-        for k in range(2):
-            slot = i * 2 + k
-            label = label_ref[pl.ds(slot, 1), :]
-            hot.append((label == pos).astype(F32).astype(BF16))
-            data.append(data_ref[pl.ds(slot, 256, stride=32), :])
-        h, l = split(jnp.concatenate(data, axis=0))
-        g = dot(jnp.concatenate(hot, axis=1), jnp.concatenate([h, l], axis=1))
-        g = g[:, :128] + g[:, 128:]
-        for bc in range(8):
-            grid_ref[s * 8 + bc, pl.ds(pl.multiple_of(r * 32, 32), 32), :] = g[bc * 32:(bc + 1) * 32]
-        return 0
-
-    lax.fori_loop(0, 16, one, 0)
-
-    def flip(i, _):
+    for h in range(2):
+        for g in (2 * h, 2 * h + 1):
+            loop(1, 16, lambda k: far_copy(g, k).wait_recv())
+        code = jnp.concatenate([held[h, k, 256:264, :] for k in range(16)], axis=0).T.astype(jnp.int32)
+        at = code // 256 - group * 32
+        value = (code % 256 + 1).astype(F32)
+
+        def put(i, _):
+            hot, data = [], []
+            for rank in range(2):
+                slot = i * 2 + rank
+                label = jnp.sum(jnp.where(at == slot, value, 0.0), axis=0, keepdims=True) - 1.0
+                hot.append(label)
+                data += [held[h, k, pl.ds(slot, 8, stride=32), :] for k in range(16)]
+            fits = (jnp.concatenate(hot, axis=1) == pos).astype(F32).astype(BF16)
+            hi, lo = split(jnp.concatenate(data, axis=0))
+            v = dot(fits, jnp.concatenate([hi, lo], axis=1))
+            v = v[:, :128] + v[:, 128:]
+            rows = pl.ds(pl.multiple_of(i % 8 * 32, 32), 32)
+            for bc in range(8):
+                where = i // 8 * 8 + bc
+                add = v[bc * 32:(bc + 1) * 32]
+                grid_ref[where, rows, :] = add if h == 0 else grid_ref[where, rows, :] + add
+            return 0
+
+        if h == 0:
+            lax.fori_loop(0, 16, put, 0)
+        else:
+            lax.fori_loop(8, 16, put, 0)
+            edge_src[...] = grid_ref[8].T[:64]
+            edge = pltpu.make_async_remote_copy(
+                src_ref=edge_src, dst_ref=edge_in, send_sem=edge_send, recv_sem=edge_recv,
+                device_id=device((group + 1) % 16, kind), device_id_type=MESH,
+            )
+            edge.start()
+            lax.fori_loop(0, 8, put, 0)
+
+    def flip(i):
         out_ref[i] = grid_ref[i].T
-        return 0
-
-    lax.fori_loop(0, 16, flip, 0)
-
-
-def place(data, labels):
+
+    loop(0, 16, flip)
+    edge.wait()
+    extra_ref[...] = edge_in[...]
+    loop(1, 16, lambda k: near_copy(k).wait_send())
+    for g in range(4):
+        loop(1, 16, lambda k: far_copy(g, k).wait_send())
+
+
+def exchange(payload):
+    tall = payload.shape[0] // CLASSES
+    vmem = pl.BlockSpec(memory_space=pltpu.VMEM)
+    dma = pltpu.SemaphoreType.DMA
     return pl.pallas_call(
-        place_kernel,
-        out_shape=jax.ShapeDtypeStruct((16, 128, 256), F32),
-        scratch_shapes=[pltpu.VMEM((16, 256, 128), F32)],
-        compiler_params=pltpu.CompilerParams(vmem_limit_bytes=32 * MB),
-        name="placing",
-    )(data, labels)
+        exchange_kernel,
+        in_specs=[vmem],
+        out_specs=[vmem, vmem],
+        out_shape=[jax.ShapeDtypeStruct((16, 128, 256), F32), jax.ShapeDtypeStruct((64, 256), F32)],
+        scratch_shapes=[
+            pltpu.VMEM((16, tall, 128), F32),
+            pltpu.VMEM((2, 16, 264, 128), F32),
+            pltpu.VMEM((2, 16, 264, 128), F32),
+            pltpu.VMEM((16, 256, 128), F32),
+            pltpu.VMEM((64, 256), F32),
+            pltpu.VMEM((64, 256), F32),
+            dma((16,)), dma((16,)), dma((4, 16)), dma((4, 16)), dma(()), dma(()),
+        ],
+        compiler_params=pltpu.CompilerParams(
+            collective_id=0, has_side_effects=True, vmem_limit_bytes=40 * MB
+        ),
+        name="exchange",
+    )(payload)
 
 
 def down_kernel(flag_ref, x_ref, extra_ref, wh, wl, t_ref, eh, el, out_ref, lh, ll):
-    zero_class = flag_ref[0]
+    zero_class = flag_ref[0] == 1
     special = flag_ref[1]
+    x0_ref, x1_ref = x_ref.at[0:1024, :], x_ref.at[1024:2048, :]
+    near = lambda ref, bc: ref[bc * 128:bc * 128 + 64, :]
+    far = lambda ref, bc: ref[bc * 128 + 64:bc * 128 + 128, :]
     for bc in range(8):
         for s in range(2):
-            plain = (s * 8 + bc) * 128
-            other = ((1 - s) * 8 + 7 - bc) * 128 + 64
             if s == 0:
-                own = x_ref[plain:plain + 64, :]
-                if bc == 0:
-                    mirror = jnp.where(zero_class == 1, extra_ref[...], x_ref[other:other + 64, :])
-                else:
-                    off = jnp.where(zero_class == 1, (16 - bc) * 128, other)
-                    mirror = x_ref[pl.ds(pl.multiple_of(off, 64), 64), :]
+                own = near(x0_ref, bc)
+                edge = extra_ref[...] if bc == 0 else near(x1_ref, 8 - bc)
+                mirror = jnp.where(zero_class, edge, far(x1_ref, 7 - bc))
             else:
-                off = jnp.where(zero_class == 1, bc * 128 + 64, plain)
-                own = x_ref[pl.ds(pl.multiple_of(off, 64), 64), :]
-                off = jnp.where(zero_class == 1, (15 - bc) * 128 + 64, other)
-                mirror = x_ref[pl.ds(pl.multiple_of(off, 64), 64), :]
+                own = jnp.where(zero_class, far(x0_ref, bc), near(x1_ref, bc))
+                mirror = jnp.where(zero_class, far(x1_ref, 7 - bc), far(x0_ref, 7 - bc))
             for c2, v in enumerate((own, mirror)):
                 h, l = split(v)
                 row = (bc * 2 + s) * 64 + c2 * 32
@@ -402,7 +540,9 @@
 
 def across_kernel(k_ref, wh, wl, zh, zl, twist, out_ref, lh, ll, y_ref):
     for j in range(16):
-        a = k_ref[j * 128:(j + 1) * 128, :].T
+        z, core = j // 2, j % 2
+        at = [((y * 2 + core) * 32 + z * 4) * 8 for y in range(4)]
+        a = jnp.concatenate([k_ref[i:i + 32, :] for i in at], axis=0).T
         h, l = split(a)
         for i in range(4):
             lh[j * 32:(j + 1) * 32, i * 128:(i + 1) * 128] = h[i * 32:(i + 1) * 32]
@@ -468,55 +608,38 @@
 
 
 def body(uv, vis, left, right, block_subgrid, subgrid_tile, block_row, block_col):
-    axes = ("row", "col")
-    devices = lax.axis_size("row") * lax.axis_size("col")
-    me = lax.axis_index("row") * lax.axis_size("col") + lax.axis_index("col")
-    subs = subgrid_tile.shape[0]
+    every = ("y", "core", "z", "x")
+    devices = math.prod(lax.axis_size(a) for a in every)
+    group = lax.axis_index("y") * lax.axis_size("x") + lax.axis_index("x")
+    kind = lax.axis_index("z") * lax.axis_size("core") + lax.axis_index("core")
     visible = uv.shape[2]
-
-    tile = subgrid_tile[:, 0]
-    ids = jnp.arange(subs, dtype=jnp.int32)
-    earlier = (tile[None, :] == tile[:, None]) & (ids[None, :] < ids[:, None])
-    rank = jnp.sum(earlier.astype(jnp.int32), axis=1)
-    band = tile % 32
-    side = (band >= 16).astype(jnp.int32)
-    pair = jnp.where(side == 1, 31 - band, band)
-    slot = pair * 32 + side * 16 + (tile // 32) * 2 + rank
-    code = block_col * 32 + block_row + 1
-    match = slot[None, :] == jnp.arange(512, dtype=jnp.int32)[:, None]
-    labels = jnp.sum(jnp.where(match, code[None, :], 0), axis=1).astype(F32) - 1.0
-    labels = jnp.broadcast_to(labels.reshape(1, PAIRS, 32), (CLASSES, PAIRS, 32)).reshape(devices, 32)
-    labels = lax.all_to_all(labels, axes, split_axis=0, concat_axis=0, tiled=True).T
 
     l, r = left.astype(F32), right.astype(F32)
     beam = jnp.stack([
         l[:, 0] * r[:, 0] + l[:, 1] * r[:, 1],
         l[:, 1] * r[:, 0] - l[:, 0] * r[:, 1],
     ])
-    outbox = make_outbox(uv, vis, beam, block_subgrid, slot[None, :], subgrid_tables(visible))
-    arrived = lax.all_to_all(
-        outbox.reshape(devices, 32, 128), axes, split_axis=0, concat_axis=0, tiled=True
-    ).reshape(devices * 32, 128)
-    x = place(arrived, labels)
-    move = [(j * PAIRS + p, j * PAIRS + (p + 1) % PAIRS) for j in range(CLASSES) for p in range(PAIRS)]
-    extra = lax.ppermute(x[8, :64], axes, move)
-    flags = jnp.stack([me < PAIRS, me == 0]).astype(jnp.int32)
+    payload = make_payload(
+        uv, vis, beam, block_subgrid, subgrid_tile, block_row[None], block_col[None], subgrid_tables(visible)
+    )
+    x, extra = exchange(payload)
+    flags = jnp.stack([kind == 0, (kind == 0) & (group == 0)]).astype(jnp.int32)
     k = down(flags, x.reshape(2048, 256), extra)
-    k = lax.all_to_all(k.reshape(devices, 8, 128), axes, split_axis=0, concat_axis=0, tiled=True)
+    k = lax.all_to_all(k.reshape(devices, 8, 128), every, split_axis=0, concat_axis=0, tiled=True)
     return across(k.reshape(2048, 128))
 
 
 def solution(mesh):
+    names = ("y", "core", "z", "x")
+    axes = Mesh(mesh.devices.reshape(4, 2, 8, 4), names)
     placed = (
-        P(("row", "col"), None, None),
-        P(("row", "col"), None, None),
-        P(("row", "col"), None, None),
-        P(("row", "col"), None, None),
-        P(("row", "col"), None),
-        P(("row", "col"), None),
-        P(("row", "col")),
-        P(("row", "col")),
+        P(names, None, None),
+        P(names, None, None),
+        P(names, None, None),
+        P(names, None, None),
+        P(names, None),
+        P(names, None),
+        P(names),
+        P(names),
     )
-    return jax.shard_map(
-        body, mesh=mesh, in_specs=placed, out_specs=P(("row", "col"), None), check_vma=False
-    )
+    return jax.shard_map(body, mesh=axes, in_specs=placed, out_specs=P(names, None), check_vma=False)

time: 244 us -> 178 us (0.73)
  waiting for transfers between devices: 103 us -> 0 us
  Pallas kernels: 61.7 us -> 123 us
  starting transfers between devices: 29.4 us -> 0 us
  blocking collectives: 38.3 us -> 45.1 us
  other arithmetic: 6.3 us -> 2.92 us
  local copies, waits for them, and re-layouts: 2.32 us -> 4.79 us
    all_to_all x2 -> x0, waiting for transfers between devices: 96.3 us -> none  [the longest x1 96.3 us: body(): lax.all_to_all(outbox.reshape(devices, 32, 128), axes, split_axis=0, conc...]
    pallas_call x2, Pallas kernels: 51.7 us -> 113 us  [the longest x1 75.5 us: exchange(): pl.pallas_call(exchange_kernel, in_specs=[vmem], out_specs=[vmem, vmem],...]
    all_to_all x2 -> x0, starting transfers between devices: 29.1 us -> none  [the longest x1 14.7 us: body(): lax.all_to_all(outbox.reshape(devices, 32, 128), axes, split_axis=0, conc...]
    all_to_all x1, blocking collectives: 38.3 us -> 45.1 us  [body(): lax.all_to_all(k.reshape(devices, 8, 128), every, split_axis=0, concat_ax...]
    ppermute x1 -> x0, waiting for transfers between devices: 6.46 us -> none  [body(): extra = lax.ppermute(x[8, :64], axes, move)]
    unnamed x32 -> x37, local copies, waits for them, and re-layouts: 1.5 us -> 4.79 us
  transfers between devices with their start and end apart: 3 -> 0, of which waited for: 2 -> 0; matrix products, arithmetic and copies ran while one was open for 2% -> 0% of each run, Pallas kernels for 17% -> 0%
where the time goes in v2:
time: 178 us; the launch traced here: 176 us
  Pallas kernels  123 us (69%)
  blocking collectives  45.1 us (25%)
  local copies, waits for them, and re-layouts  4.79 us (3%)
  other arithmetic  2.92 us (2%)
    pallas_call x1, Pallas kernels, exchange(): pl.pallas_call(exchange_kernel, in_specs=[vmem], out_specs=[vmem, vmem],...  75.5 us
    all_to_all x1, blocking collectives, body(): lax.all_to_all(k.reshape(devices, 8, 128), every, split_axis=0, concat_ax...  45.1 us
    pallas_call x1, Pallas kernels, make_payload(): pl.pallas_call(grid_kernel, grid=(blocks // STEP,), in_specs=[pl.BlockSpe...  37.1 us
    pallas_call x1, Pallas kernels, down(): pl.pallas_call(down_kernel, in_specs=[pl.BlockSpec(memory_space=pltpu.SME...  7.27 us
    unnamed x37, local copies, waits for them, and re-layouts  4.79 us

profile of v2, /device:TPU:32, one launch (start us, length us, event | category | flops | bytes accessed | tf_op | source)
XLA Modules:
  0.0 175.7 jit_solution(2757876446246726810)
XLA Ops:
  0.0 0.8 copy.25.tile_ref
  0.8 2.3 %copy_convert_fusion = (f32[256,2,1024]{2,0,1:T(8,128)S(1)}, f32[256,2,1024]{2,0,1:T(8,128)S(1)}) fusion(bf16[256,2,1024]{2,1,0:T(2,128)(2,1)} %param.25, bf16[256,2,1024]{2,1,0:T(2,128)(2,1)} %param.24), kind=kLoop, calls=%fused_computation.1 | loop fusion | flops 1048576 | bytes 6291456 | tf_op jit(solution)/shard_map/convert_element_type | solution.py:617
  3.0 0.4 add_bitcast_fusion
  3.5 0.0 copy-start
  3.5 0.0 copy-start.8
  3.5 0.0 copy-start.9
  3.5 0.0 copy-start.10
  3.5 0.0 copy-start.11
  3.5 0.0 copy-start.15
  3.6 0.0 copy-start.16
  3.6 0.0 copy-start.17
  3.6 0.1 pad_maximum_fusion.beam_ref
  3.7 1.4 copy-done
  5.1 0.0 copy-done.8
  5.1 0.1 copy-done.9
  5.1 0.0 copy-done.10
  5.2 0.0 copy-done.11
  5.2 0.0 copy-done.15
  5.2 0.0 copy-done.16
  5.2 0.0 copy-done.17
  5.2 0.0 copy-start.1
  5.2 0.0 copy-start.13
  5.2 0.0 copy-start.14
  5.3 37.1 %gridding.1.src_ref = f32[2176,128]{1,0:T(8,128)S(1)} custom-call(f32[256,2,128]{2,1,0:T(2,128)S(1)} %copy-done.8, f32[256,2,128]{2,1,0:T(2,128)S(1)} %copy-done.9, f32[2,256,1024]{2,1,0:T(8,128)S(1)} %pad_maximum_fusion.beam_ref, s32[1,256]{1,0:T(1,128)S(1)} %copy-done.15, s32[128,1]{1,0:T(8,128)S(1)} %copy.25.tile_ref, s32[1,128]{1,0:T(1,128)S(1)} %bitcast.14, ...), custom_call_target="tpu_custom_call" | custom-call | tf_op jit(solution)/shard_map/gridding/pallas_call | solution.py:275
  42.4 75.5 %exchange.1 = (f32[16,128,256]{2,1,0:T(8,128)S(1)}, f32[64,256]{1,0:T(8,128)S(1)}) custom-call(f32[2176,128]{1,0:T(8,128)S(1)} %gridding.1.src_ref), custom_call_target="tpu_custom_call" | custom-call | tf_op jit(solution)/shard_map/exchange/pallas_call | solution.py:451
  117.9 0.1 add_convert_fusion.flag_ref
  117.9 0.0 copy-done.1
  117.9 0.0 copy-done.13
  117.9 0.0 copy-done.14
  117.9 0.0 copy-start.2
  118.0 1.2 copy-done.2
  119.2 0.0 copy-start.3
  119.2 1.2 copy-done.3
  120.4 7.3 %down.1 = f32[2048,128]{1,0:T(8,128)S(1)} custom-call(s32[2]{0:T(128)S(1)} %add_convert_fusion.flag_ref, f32[2048,256]{1,0:T(8,128)S(1)} %bitcast.13, f32[64,256]{1,0:T(8,128)S(1)} %get-tuple-element.8.extra_ref, bf16[512,1024]{1,0:T(8,128)(2,1)S(1)} %copy-done.1, bf16[512,1024]{1,0:T(8,128)(2,1)S(1)} %copy-done.2, f32[16,64,256]{2,1,0:T(8,128)S(1)} %copy-done.3, ...), custom_call_target="tpu_custom_call" | custom-call | tf_op jit(solution)/shard_map/down/pallas_call | solution.py:531
  127.7 0.0 copy-start.4
  127.7 0.0 copy-start.5
  127.7 0.0 copy-start.6
  127.7 0.0 copy-start.7
  127.7 0.0 copy-start.12
  127.7 45.1 %all_to_all.5 = f32[256,8,128]{2,1,0:T(8,128)S(1)} all-to-all(f32[256,8,128]{2,1,0:T(8,128)S(1)} %bitcast.11), channel_id=1, replica_groups=mesh['y'=4,'core'=2,'z'=8,'x'=4] {'y','core','z','x'}, dimensions={0} | all-to-all | bytes 2097152 | tf_op jit(solution)/shard_map/all_to_all | solution.py:628
  172.8 0.0 copy-done.4
  172.8 0.0 copy-done.5
  172.8 0.0 copy-done.6
  172.8 0.0 copy-done.7
  172.8 0.0 copy-done.12
  172.8 2.9 %across.1 = f32[32,8192]{1,0:T(8,128)} custom-call(f32[2048,128]{1,0:T(8,128)S(1)} %bitcast.12, bf16[512,512]{1,0:T(8,128)(2,1)S(1)} %copy-done.4, bf16[512,512]{1,0:T(8,128)(2,1)S(1)} %copy-done.5, bf16[256,512]{1,0:T(8,128)(2,1)S(1)} %copy-done.6, bf16[256,512]{1,0:T(8,128)(2,1)S(1)} %copy-done.7, f32[17,512]{1,0:T(8,128)S(1)} %copy-done.12), custom_call_target="tpu_custom_call" | custom-call | tf_op jit(solution)/shard_map/across/pallas_call | solution.py:599
Async XLA Ops:
  3.5 1.6 copy-start
  3.5 1.6 copy-start.8
  3.5 1.6 copy-start.9
  3.5 1.7 copy-start.10
  3.5 1.7 copy-start.11
  3.5 1.7 copy-start.15
  3.6 1.7 copy-start.16
  3.6 1.7 copy-start.17
  5.2 112.7 %copy-start.1 = (bf16[512,1024]{1,0:T(8,128)(2,1)S(1)}, bf16[512,1024]{1,0:T(8,128)(2,1)}, u32[]{:S(2)}) copy-start(bf16[512,1024]{1,0:T(8,128)(2,1)} %constant.57.clone.wh) | copy-start | bytes 3145732
  5.2 112.7 %copy-start.13 = (bf16[32,128]{1,0:T(8,128)(2,1)S(1)}, bf16[32,128]{1,0:T(8,128)(2,1)}, u32[]{:S(2)}) copy-start(bf16[32,128]{1,0:T(8,128)(2,1)} %constant.60.clone.eh) | copy-start | bytes 24580
  5.2 112.7 %copy-start.14 = (bf16[32,128]{1,0:T(8,128)(2,1)S(1)}, bf16[32,128]{1,0:T(8,128)(2,1)}, u32[]{:S(2)}) copy-start(bf16[32,128]{1,0:T(8,128)(2,1)} %constant.61.clone.el) | copy-start | bytes 24580
  117.9 1.2 copy-start.2
  119.2 1.2 copy-start.3
  127.7 45.1 %copy-start.4 = (bf16[512,512]{1,0:T(8,128)(2,1)S(1)}, bf16[512,512]{1,0:T(8,128)(2,1)}, u32[]{:S(2)}) copy-start(bf16[512,512]{1,0:T(8,128)(2,1)} %constant.62.clone.wh) | copy-start | bytes 1572868
  127.7 45.1 %copy-start.5 = (bf16[512,512]{1,0:T(8,128)(2,1)S(1)}, bf16[512,512]{1,0:T(8,128)(2,1)}, u32[]{:S(2)}) copy-start(bf16[512,512]{1,0:T(8,128)(2,1)} %constant.63.clone.wl) | copy-start | bytes 1572868
  127.7 45.1 %copy-start.6 = (bf16[256,512]{1,0:T(8,128)(2,1)S(1)}, bf16[256,512]{1,0:T(8,128)(2,1)}, u32[]{:S(2)}) copy-start(bf16[256,512]{1,0:T(8,128)(2,1)} %constant.64.clone.zh) | copy-start | bytes 786436
  127.7 45.1 %copy-start.7 = (bf16[256,512]{1,0:T(8,128)(2,1)S(1)}, bf16[256,512]{1,0:T(8,128)(2,1)}, u32[]{:S(2)}) copy-start(bf16[256,512]{1,0:T(8,128)(2,1)} %constant.65.clone.zl) | copy-start | bytes 786436
  127.7 45.1 %copy-start.12 = (f32[17,512]{1,0:T(8,128)S(1)}, f32[17,512]{1,0:T(8,128)}, u32[]{:S(2)}) copy-start(f32[17,512]{1,0:T(8,128)} %constant.66.clone.twist) | copy-start | bytes 104452

commit v3 on v2

--- a/solution.py
+++ b/solution.py
@@ -303,53 +303,29 @@
 MESH = pl.DeviceIdType.MESH
 
 
-def device(pair, kind):
-    return (pair // 4, kind % 2, kind // 2, pair % 4)
+NEAR = [(0, 0), (0, 1), (1, 0), (-1, 0), (1, 1), (-1, 1), (2, 0), (-2, 0),
+        (2, 1), (-2, 1), (3, 0), (-3, 0), (3, 1), (-3, 1), (4, 0), (4, 1)]
+FAR = [(0, 1), (1, 0), (0, -1), (-1, 0), (0, 2), (2, 0), (1, 1), (-1, -1),
+       (-1, 1), (1, -1), (2, 2), (1, 2), (2, 1), (-1, 2), (2, -1)]
 
 
 def exchange_kernel(
-    src_ref, out_ref, extra_ref,
-    near, box, held, grid_ref, edge_src, edge_in,
-    near_send, near_recv, far_send, far_recv, edge_send, edge_recv,
+    src_ref, wh_hbm, wl_hbm, t_hbm, eh, el, out_ref,
+    near, box, held, grid_ref, x_ref, edge_src, edge_in, wh, wl, t_ref, lh, ll, kbuf, near2,
+    near_send, near_recv, far_send, far_recv, edge_send, edge_recv, table_sem,
+    near2_send, near2_recv, far2_send, far2_recv,
 ):
-    group = lax.axis_index("y") * 4 + lax.axis_index("x")
-    kind = lax.axis_index("z") * 2 + lax.axis_index("core")
+    y, core, z, x = [lax.axis_index(a) for a in ("y", "core", "z", "x")]
+    group, kind = y * 4 + x, z * 2 + core
     tall = src_ref.shape[0] // CLASSES
     subs = tall - 8
-    part = 8 * 32 + 8
-
-    barrier = pltpu.get_barrier_semaphore()
-
-    def greet(k, _):
-        pl.semaphore_signal(barrier, inc=1, device_id=device(group, (kind + k) % 16), device_id_type=MESH)
-        pl.semaphore_signal(barrier, inc=1, device_id=device((group + k) % 16, kind), device_id_type=MESH)
-        return 0
-
-    lax.fori_loop(1, 16, greet, 0)
-    pl.semaphore_wait(barrier, 30)
-
-    def near_copy(k):
-        to = (kind + k) % 16
-        return pltpu.make_async_remote_copy(
-            src_ref=src_ref.at[pl.ds(pl.multiple_of(to * tall, 8), tall), :],
-            dst_ref=near.at[k],
-            send_sem=near_send.at[k],
-            recv_sem=near_recv.at[k],
-            device_id=device(group, to),
-            device_id_type=MESH,
-        )
-
-    def far_copy(g, k):
-        to = (group + k) % 16
-        h, rows = g // 2, pl.ds((g % 2) * 128, 128 + 8 * (g % 2))
-        return pltpu.make_async_remote_copy(
-            src_ref=box.at[h, to, rows, :],
-            dst_ref=held.at[h, k, rows, :],
-            send_sem=far_send.at[g, k],
-            recv_sem=far_recv.at[g, k],
-            device_id=device((group + k) % 16, kind),
-            device_id_type=MESH,
-        )
+
+    tables = [
+        pltpu.make_async_copy(a, b, table_sem.at[n])
+        for n, (a, b) in enumerate(((wh_hbm, wh), (wl_hbm, wl), (t_hbm, t_ref)))
+    ]
+    for c in tables:
+        c.start()
 
     def loop(lo, hi, f):
         def step(k, _):
@@ -358,52 +334,85 @@
 
         lax.fori_loop(lo, hi, step, 0)
 
-    loop(1, 16, lambda k: near_copy(k).start())
+    def to_near(k):
+        dz, dc = NEAR[k]
+        return (z + dz + 8) % 8, (core + dc) % 2
+
+    def to_far(k):
+        dy, dx = FAR[k]
+        return (y + dy + 4) % 4, (x + dx + 4) % 4
+
+    barrier = pltpu.get_barrier_semaphore()
+    for k in range(1, 16):
+        tz, tc = to_near(k)
+        pl.semaphore_signal(barrier, inc=1, device_id=(y, tc, tz, x), device_id_type=MESH)
+    for k in range(15):
+        ty, tx = to_far(k)
+        pl.semaphore_signal(barrier, inc=1, device_id=(ty, core, z, tx), device_id_type=MESH)
+    pl.semaphore_wait(barrier, 30)
+
+    def near_copy(k):
+        tz, tc = to_near(k)
+        return pltpu.make_async_remote_copy(
+            src_ref=src_ref.at[pl.ds(pl.multiple_of((tz * 2 + tc) * tall, 8), tall), :],
+            dst_ref=near.at[k],
+            send_sem=near_send.at[k],
+            recv_sem=near_recv.at[k],
+            device_id=(y, tc, tz, x),
+            device_id_type=MESH,
+        )
+
+    def far_copy(g, k):
+        ty, tx = to_far(k)
+        h, rows = g // 2, pl.ds((g % 2) * 128, 128 + 8 * (g % 2))
+        return pltpu.make_async_remote_copy(
+            src_ref=box.at[h, ty * 4 + tx, rows, :],
+            dst_ref=held.at[h, k, rows, :],
+            send_sem=far_send.at[g, k],
+            recv_sem=far_recv.at[g, k],
+            device_id=(ty, core, z, tx),
+            device_id_type=MESH,
+        )
+
+    for k in range(1, 16):
+        near_copy(k).start()
     near[0] = src_ref[pl.ds(pl.multiple_of(kind * tall, 8), tall), :]
 
     slots = lax.broadcasted_iota(jnp.int32, (512, subs), 0)
     line = lax.broadcasted_iota(jnp.int32, (8, subs), 0)
-
-    def unfold(h, k8, codes):
-        k = h * 8 + k8
-        code = near[k, subs:subs + 1, :]
-        fits = (code.astype(jnp.int32) // 256 == slots).astype(F32).astype(BF16)
-        hi, lo = split(near[k, :subs, :])
-        o = dot(jnp.concatenate([fits, fits], axis=1), jnp.concatenate([hi, lo], axis=0))
-        rows = pl.ds(pl.multiple_of(k8 * 32, 32), 32)
-        for p in range(PAIRS):
-            box[h, p, rows, :] = o[p * 32:(p + 1) * 32]
-        return jnp.where(line == k8, code, codes)
-
+    codes = jnp.zeros((8, subs), F32)
     for g in range(4):
         h = g // 2
-        if g % 2 == 0:
-            codes = jnp.zeros((8, subs), F32)
-
-        def one(i, codes):
+        for i in range(4):
             k8 = (g % 2) * 4 + i
-            near_copy(h * 8 + k8).wait_recv()
-            return unfold(h, k8, codes)
-
-        if g == 0:
-            codes = unfold(0, 0, codes)
-        codes = lax.fori_loop(1 if g == 0 else 0, 4, one, codes)
+            k = h * 8 + k8
+            if k:
+                near_copy(k).wait_recv()
+            code = near[k, subs:subs + 1, :]
+            fits = (code.astype(jnp.int32) // 256 == slots).astype(F32).astype(BF16)
+            hi, lo = split(near[k, :subs, :])
+            o = dot(jnp.concatenate([fits, fits], axis=1), jnp.concatenate([hi, lo], axis=0))
+            for p in range(PAIRS):
+                box[h, p, k8 * 32:k8 * 32 + 32, :] = o[p * 32:(p + 1) * 32]
+            codes = jnp.where(line == k8, code, codes)
         if g % 2 == 1:
             for p in range(PAIRS):
                 box[h, p, 256:264, :] = codes
-        loop(1, 16, lambda k: far_copy(g, k).start())
+        for k in range(15):
+            far_copy(g, k).start()
         if g % 2 == 1:
-            held[h, 0] = box[h, group]
+            held[h, 15] = box[h, group]
 
     pos = lax.broadcasted_iota(jnp.int32, (256, 256), 0).astype(F32)
     for h in range(2):
         for g in (2 * h, 2 * h + 1):
-            loop(1, 16, lambda k: far_copy(g, k).wait_recv())
+            for k in range(15):
+                far_copy(g, k).wait_recv()
         code = jnp.concatenate([held[h, k, 256:264, :] for k in range(16)], axis=0).T.astype(jnp.int32)
         at = code // 256 - group * 32
         value = (code % 256 + 1).astype(F32)
 
-        def put(i, _):
+        def put(i):
             hot, data = [], []
             for rank in range(2):
                 slot = i * 2 + rank
@@ -419,91 +428,74 @@
                 where = i // 8 * 8 + bc
                 add = v[bc * 32:(bc + 1) * 32]
                 grid_ref[where, rows, :] = add if h == 0 else grid_ref[where, rows, :] + add
-            return 0
+
+        def flip(i):
+            x_ref[pl.ds(pl.multiple_of(i * 128, 128), 128), :] = grid_ref[i].T
 
         if h == 0:
-            lax.fori_loop(0, 16, put, 0)
+            loop(0, 16, put)
         else:
-            lax.fori_loop(8, 16, put, 0)
+            loop(8, 16, put)
             edge_src[...] = grid_ref[8].T[:64]
+            tx, ty = (x + 1) % 4, (y + (x + 1) // 4) % 4
             edge = pltpu.make_async_remote_copy(
                 src_ref=edge_src, dst_ref=edge_in, send_sem=edge_send, recv_sem=edge_recv,
-                device_id=device((group + 1) % 16, kind), device_id_type=MESH,
+                device_id=(ty, core, z, tx), device_id_type=MESH,
             )
             edge.start()
-            lax.fori_loop(0, 8, put, 0)
-
-    def flip(i):
-        out_ref[i] = grid_ref[i].T
-
-    loop(0, 16, flip)
-    edge.wait()
-    extra_ref[...] = edge_in[...]
-    loop(1, 16, lambda k: near_copy(k).wait_send())
-    for g in range(4):
-        loop(1, 16, lambda k: far_copy(g, k).wait_send())
-
-
-def exchange(payload):
-    tall = payload.shape[0] // CLASSES
-    vmem = pl.BlockSpec(memory_space=pltpu.VMEM)
-    dma = pltpu.SemaphoreType.DMA
-    return pl.pallas_call(
-        exchange_kernel,
-        in_specs=[vmem],
-        out_specs=[vmem, vmem],
-        out_shape=[jax.ShapeDtypeStruct((16, 128, 256), F32), jax.ShapeDtypeStruct((64, 256), F32)],
-        scratch_shapes=[
-            pltpu.VMEM((16, tall, 128), F32),
-            pltpu.VMEM((2, 16, 264, 128), F32),
-            pltpu.VMEM((2, 16, 264, 128), F32),
-            pltpu.VMEM((16, 256, 128), F32),
-            pltpu.VMEM((64, 256), F32),
-            pltpu.VMEM((64, 256), F32),
-            dma((16,)), dma((16,)), dma((4, 16)), dma((4, 16)), dma(()), dma(()),
-        ],
-        compiler_params=pltpu.CompilerParams(
-            collective_id=0, has_side_effects=True, vmem_limit_bytes=40 * MB
-        ),
-        name="exchange",
-    )(payload)
-
-
-def down_kernel(flag_ref, x_ref, extra_ref, wh, wl, t_ref, eh, el, out_ref, lh, ll):
-    zero_class = flag_ref[0] == 1
-    special = flag_ref[1]
-    x0_ref, x1_ref = x_ref.at[0:1024, :], x_ref.at[1024:2048, :]
-    near = lambda ref, bc: ref[bc * 128:bc * 128 + 64, :]
-    far = lambda ref, bc: ref[bc * 128 + 64:bc * 128 + 128, :]
+            loop(8, 16, flip)
+            loop(0, 8, put)
+            loop(0, 8, flip)
+
+    edge.wait_recv()
+    zero_class = kind == 0
+    special = jnp.where((kind == 0) & (group == 0), 1, 0)
+    near_x = lambda s, bc: x_ref[s * 1024 + bc * 128:s * 1024 + bc * 128 + 64, :]
+    far_x = lambda s, bc: x_ref[s * 1024 + bc * 128 + 64:s * 1024 + bc * 128 + 128, :]
     for bc in range(8):
         for s in range(2):
             if s == 0:
-                own = near(x0_ref, bc)
-                edge = extra_ref[...] if bc == 0 else near(x1_ref, 8 - bc)
-                mirror = jnp.where(zero_class, edge, far(x1_ref, 7 - bc))
+                own = near_x(0, bc)
+                first = edge_in[...] if bc == 0 else near_x(1, 8 - bc)
+                mirror = jnp.where(zero_class, first, far_x(1, 7 - bc))
             else:
-                own = jnp.where(zero_class, far(x0_ref, bc), near(x1_ref, bc))
-                mirror = jnp.where(zero_class, far(x1_ref, 7 - bc), far(x0_ref, 7 - bc))
+                own = jnp.where(zero_class, far_x(0, bc), near_x(1, bc))
+                mirror = jnp.where(zero_class, far_x(1, 7 - bc), far_x(0, 7 - bc))
             for c2, v in enumerate((own, mirror)):
-                h, l = split(v)
+                hi, lo = split(v)
                 row = (bc * 2 + s) * 64 + c2 * 32
                 for ri in range(2):
-                    lh[row:row + 32, ri * 256:(ri + 1) * 256] = h[ri * 32:(ri + 1) * 32]
-                    ll[row:row + 32, ri * 256:(ri + 1) * 256] = l[ri * 32:(ri + 1) * 32]
+                    lh[row:row + 32, ri * 256:(ri + 1) * 256] = hi[ri * 32:(ri + 1) * 32]
+                    ll[row:row + 32, ri * 256:(ri + 1) * 256] = lo[ri * 32:(ri + 1) * 32]
+    for c in tables:
+        c.wait()
     e2 = jnp.concatenate([eh[...], eh[...]], axis=1)
     low = lax.broadcasted_iota(jnp.int32, (32, 128), 1) < 64
 
-    def one(i, _):
-        rows = pl.ds(pl.multiple_of(i * 256, 256), 256)
-        for nt in range(2):
-            cols = slice(nt * 512, (nt + 1) * 512)
-            y = dot3(lh[rows, :], ll[rows, :], wh[:, cols], wl[:, cols])
+    def near2_copy(nt, t, dc):
+        zh, tc = (z // 2 + t) % 4, (core + dc) % 2
+        tz = zh * 2 + nt
+        return (tz * 2 + tc) != kind, pltpu.make_async_remote_copy(
+            src_ref=kbuf.at[pl.ds(pl.multiple_of((nt * 8 + tc * 4 + zh) * 128, 128), 128), :],
+            dst_ref=near2.at[kind],
+            send_sem=near2_send.at[nt, t, dc],
+            recv_sem=near2_recv.at[kind],
+            device_id=(y, tc, tz, x),
+            device_id_type=MESH,
+        )
+
+    for nt in range(2):
+        cols = slice(nt * 512, (nt + 1) * 512)
+
+        def one(i):
+            rows = pl.ds(pl.multiple_of(i * 256, 256), 256)
+            v = dot3(lh[rows, :], ll[rows, :], wh[:, cols], wl[:, cols])
             for k in range(2):
                 bc = i * 2 + k
                 parts = []
                 for s in range(2):
                     r = (k * 2 + s) * 64
-                    ya, yb = y[r:r + 64, :256], y[r:r + 64, 256:]
+                    ya, yb = v[r:r + 64, :256], v[r:r + 64, 256:]
                     which = 0
                     if s == 0 and k == 0:
                         which = jnp.where(i == 0, special, 0)
@@ -515,34 +507,117 @@
                 for g in range(2):
                     o0 = o[:, g * 128:(g + 1) * 128]
                     o1 = o[:, 256 + g * 128:256 + (g + 1) * 128]
-                    q = nt * 4 + g * 2
-                    out_ref[pl.ds(q * 8 + bc, 32, stride=64), :] = jnp.where(low, o0, pltpu.roll(o1, 64, 1))
-                    out_ref[pl.ds((q + 1) * 8 + bc, 32, stride=64), :] = jnp.where(low, pltpu.roll(o0, 64, 1), o1)
-        return 0
-
-    lax.fori_loop(0, 4, one, 0)
-
-
-def down(flags, x, extra):
+                    pair = (jnp.where(low, o0, pltpu.roll(o1, 64, 1)), jnp.where(low, pltpu.roll(o0, 64, 1), o1))
+                    for e in range(2):
+                        for ty in range(4):
+                            first = nt * 1024 + ty * 32 + (g * 2 + e) * 8 + bc
+                            kbuf[pl.ds(first, 8, stride=128), :] = pair[e][ty * 8:(ty + 1) * 8]
+
+        loop(0, 4, one)
+        for t in (0, 1, 3, 2):
+            for dc in range(2):
+                other, copy = near2_copy(nt, t, dc)
+
+                @pl.when(other)
+                def _():
+                    copy.start()
+
+    mine = (z % 2) * 8 + core * 4 + z // 2
+    near2[kind] = kbuf[pl.ds(pl.multiple_of(mine * 128, 128), 128), :]
+
+    def far2_copy(t, k):
+        ty, tx = to_far(k)
+        kinds = pl.ds(((z // 2 - t + 4) % 4) * 4, 4)
+        return pltpu.make_async_remote_copy(
+            src_ref=near2.at[kinds, pl.ds(pl.multiple_of((ty * 4 + tx) * 8, 8), 8), :],
+            dst_ref=out_ref.at[kinds, pl.ds(pl.multiple_of(group * 8, 8), 8), :],
+            send_sem=far2_send.at[t, k],
+            recv_sem=far2_recv.at[t, k],
+            device_id=(ty, core, z, tx),
+            device_id_type=MESH,
+        )
+
+    for t in (0, 1, 3, 2):
+        base = ((z // 2 - t + 4) % 4) * 4
+        for i in range(4):
+            sender = base + i
+
+            @pl.when(sender != kind)
+            def _():
+                pltpu.make_async_remote_copy(
+                    src_ref=kbuf.at[pl.ds(0, 128), :], dst_ref=near2.at[sender],
+                    send_sem=near2_send.at[0, 0, 0], recv_sem=near2_recv.at[sender],
+                    device_id=(y, 1 - core, z, x), device_id_type=MESH,
+                ).wait_recv()
+
+        for k in range(15):
+            far2_copy(t, k).start()
+        own = pl.ds(pl.multiple_of(group * 8, 8), 8)
+        out_ref[pl.ds(base, 4), own, :] = near2[pl.ds(base, 4), own, :]
+
+    for t in range(4):
+        for k in range(15):
+            far2_copy(t, k).wait_recv()
+    edge.wait_send()
+    for k in range(1, 16):
+        near_copy(k).wait_send()
+    for g in range(4):
+        for k in range(15):
+            far_copy(g, k).wait_send()
+    for nt in range(2):
+        for t in range(4):
+            for dc in range(2):
+                other, copy = near2_copy(nt, t, dc)
+
+                @pl.when(other)
+                def _():
+                    copy.wait_send()
+    for t in range(4):
+        for k in range(15):
+            far2_copy(t, k).wait_send()
+
+
+def exchange(payload):
+    tall = payload.shape[0] // CLASSES
     w, t, e = down_tables()
     wh, wl = halves(w)
     eh, el = halves(e)
     vmem = pl.BlockSpec(memory_space=pltpu.VMEM)
+    hbm = pl.BlockSpec(memory_space=pl.ANY)
+    dma = pltpu.SemaphoreType.DMA
     return pl.pallas_call(
-        down_kernel,
-        in_specs=[pl.BlockSpec(memory_space=pltpu.SMEM)] + [vmem] * 7,
-        out_shape=jax.ShapeDtypeStruct((2048, 128), F32),
-        scratch_shapes=[pltpu.VMEM((1024, 512), BF16), pltpu.VMEM((1024, 512), BF16)],
-        compiler_params=pltpu.CompilerParams(vmem_limit_bytes=40 * MB),
-        name="down",
-    )(flags, x, extra, wh, wl, t, eh, el)
+        exchange_kernel,
+        in_specs=[vmem, hbm, hbm, hbm, vmem, vmem],
+        out_specs=vmem,
+        out_shape=jax.ShapeDtypeStruct((16, 128, 128), F32),
+        scratch_shapes=[
+            pltpu.VMEM((16, tall, 128), F32),
+            pltpu.VMEM((2, 16, 264, 128), F32),
+            pltpu.VMEM((2, 16, 264, 128), F32),
+            pltpu.VMEM((16, 256, 128), F32),
+            pltpu.VMEM((2048, 256), F32),
+            pltpu.VMEM((64, 256), F32),
+            pltpu.VMEM((64, 256), F32),
+            pltpu.VMEM((512, 1024), BF16),
+            pltpu.VMEM((512, 1024), BF16),
+            pltpu.VMEM((16, 64, 256), F32),
+            pltpu.VMEM((1024, 512), BF16),
+            pltpu.VMEM((1024, 512), BF16),
+            pltpu.VMEM((2048, 128), F32),
+            pltpu.VMEM((16, 128, 128), F32),
+            dma((16,)), dma((16,)), dma((4, 16)), dma((4, 16)), dma(()), dma(()), dma((3,)),
+            dma((2, 4, 2)), dma((16,)), dma((4, 16)), dma((4, 16)),
+        ],
+        compiler_params=pltpu.CompilerParams(
+            collective_id=0, has_side_effects=True, vmem_limit_bytes=48 * MB
+        ),
+        name="exchange",
+    )(payload, wh, wl, t, eh, el)
 
 
 def across_kernel(k_ref, wh, wl, zh, zl, twist, out_ref, lh, ll, y_ref):
     for j in range(16):
-        z, core = j // 2, j % 2
-        at = [((y * 2 + core) * 32 + z * 4) * 8 for y in range(4)]
-        a = jnp.concatenate([k_ref[i:i + 32, :] for i in at], axis=0).T
+        a = k_ref[j * 128:(j + 1) * 128, :].T
         h, l = split(a)
         for i in range(4):
             lh[j * 32:(j + 1) * 32, i * 128:(i + 1) * 128] = h[i * 32:(i + 1) * 32]
@@ -608,10 +683,6 @@
 
 
 def body(uv, vis, left, right, block_subgrid, subgrid_tile, block_row, block_col):
-    every = ("y", "core", "z", "x")
-    devices = math.prod(lax.axis_size(a) for a in every)
-    group = lax.axis_index("y") * lax.axis_size("x") + lax.axis_index("x")
-    kind = lax.axis_index("z") * lax.axis_size("core") + lax.axis_index("core")
     visible = uv.shape[2]
 
     l, r = left.astype(F32), right.astype(F32)
@@ -622,11 +693,7 @@
     payload = make_payload(
         uv, vis, beam, block_subgrid, subgrid_tile, block_row[None], block_col[None], subgrid_tables(visible)
     )
-    x, extra = exchange(payload)
-    flags = jnp.stack([kind == 0, (kind == 0) & (group == 0)]).astype(jnp.int32)
-    k = down(flags, x.reshape(2048, 256), extra)
-    k = lax.all_to_all(k.reshape(devices, 8, 128), every, split_axis=0, concat_axis=0, tiled=True)
-    return across(k.reshape(2048, 128))
+    return across(exchange(payload).reshape(2048, 128))
 
 
 def solution(mesh):

time: 178 us -> 157 us (0.88)
  blocking collectives: 45.1 us -> 0 us
  Pallas kernels: 123 us -> 150 us
  local copies, waits for them, and re-layouts: 4.79 us -> 2.56 us
    all_to_all x1 -> x0, blocking collectives: 45.1 us -> none  [body(): lax.all_to_all(k.reshape(devices, 8, 128), every, split_axis=0, concat_ax...]
    pallas_call x2 -> x1, Pallas kernels: 82.7 us -> 110 us  [exchange(): pl.pallas_call(exchange_kernel, in_specs=[vmem, hbm, hbm, hbm, vmem, vmem...]
    unnamed x37 -> x39, local copies, waits for them, and re-layouts: 4.79 us -> 2.56 us
where the time goes in v3:
time: 157 us; the launch traced here: 156 us
  Pallas kernels  150 us (96%)
  other arithmetic  3.04 us (2%)
  local copies, waits for them, and re-layouts  2.56 us (2%)
    pallas_call x1, Pallas kernels, exchange(): pl.pallas_call(exchange_kernel, in_specs=[vmem, hbm, hbm, hbm, vmem, vmem...  110 us
    pallas_call x1, Pallas kernels, make_payload(): pl.pallas_call(grid_kernel, grid=(blocks // STEP,), in_specs=[pl.BlockSpe...  37.1 us

profile of v3, /device:TPU:32, one launch (start us, length us, event | category | flops | bytes accessed | tf_op | source)
XLA Modules:
  0.0 156.1 jit_solution(9895241111366478349)
XLA Ops:
  0.0 2.3 %copy_convert_fusion = (f32[256,2,1024]{2,0,1:T(8,128)S(1)}, f32[256,2,1024]{2,0,1:T(8,128)S(1)}) fusion(bf16[256,2,1024]{2,1,0:T(2,128)(2,1)} %param.25, bf16[256,2,1024]{2,1,0:T(2,128)(2,1)} %param.24), kind=kLoop, calls=%fused_computation.1 | loop fusion | flops 1048576 | bytes 6291456 | tf_op jit(solution)/shard_map/convert_element_type | solution.py:688
  2.3 0.6 add_bitcast_fusion
  2.9 0.0 copy-start.18
  2.9 0.0 copy-start.8
  2.9 0.0 copy-start.9
  3.0 0.0 copy-start.10
  3.0 0.0 copy-start.11
  3.0 0.0 copy-start.15
  3.0 0.0 copy-start.16
  3.0 0.0 copy-start.17
  3.0 0.1 pad_maximum_fusion.beam_ref
  3.2 0.4 copy-done.18
  3.6 0.1 copy.25.tile_ref
  3.7 0.2 copy-done.8
  3.9 0.1 copy-done.9
  4.0 0.0 copy-done.10
  4.0 0.0 copy-done.11
  4.0 0.0 copy-done.15
  4.0 0.0 copy-done.16
  4.0 0.0 copy-done.17
  4.1 0.0 copy-start
  4.1 1.6 %copy-done = bf16[1024,1024]{1,0:T(8,128)(2,1)S(1)} copy-done((bf16[1024,1024]{1,0:T(8,128)(2,1)S(1)}, bf16[1024,1024]{1,0:T(8,128)(2,1)}, u32[]{:S(2)}) %copy-start) | copy-done | bytes 2097176
  5.6 0.0 copy-start.1
  5.6 0.0 copy-start.2
  5.6 0.0 copy-start.3
  5.7 0.0 copy-start.13
  5.7 0.0 copy-start.14
  5.7 37.1 %gridding.1.src_ref = f32[2176,128]{1,0:T(8,128)S(1)} custom-call(f32[256,2,128]{2,1,0:T(2,128)S(1)} %copy-done.8, f32[256,2,128]{2,1,0:T(2,128)S(1)} %copy-done.9, f32[2,256,1024]{2,1,0:T(8,128)S(1)} %pad_maximum_fusion.beam_ref, s32[1,256]{1,0:T(1,128)S(1)} %copy-done.15, s32[128,1]{1,0:T(8,128)S(1)} %copy.25.tile_ref, s32[1,128]{1,0:T(1,128)S(1)} %bitcast.8, ...), custom_call_target="tpu_custom_call" | custom-call | tf_op jit(solution)/shard_map/gridding/pallas_call | solution.py:275
  42.8 0.0 copy-done.1
  42.8 0.0 copy-done.2
  42.8 0.0 copy-done.3
  42.9 0.0 copy-done.13
  42.9 0.0 copy-done.14
  42.9 0.0 copy-start.4
  42.9 0.0 copy-start.5
  42.9 0.0 copy-start.6
  42.9 0.0 copy-start.7
  42.9 0.0 copy-start.12
  42.9 110.3 %exchange.1 = f32[16,128,128]{2,1,0:T(8,128)S(1)} custom-call(f32[2176,128]{1,0:T(8,128)S(1)} %gridding.1.src_ref, bf16[512,1024]{1,0:T(8,128)(2,1)S(1)} %copy-done.1, bf16[512,1024]{1,0:T(8,128)(2,1)S(1)} %copy-done.2, f32[16,64,256]{2,1,0:T(8,128)S(1)} %copy-done.3, bf16[32,128]{1,0:T(8,128)(2,1)S(1)} %copy-done.13, bf16[32,128]{1,0:T(8,128)(2,1)S(1)} %copy-done.14), custom_call_target="tpu_custom_call" | custom-call | tf_op jit(solution)/shard_map/exchange/pallas_call | solution.py:588
  153.2 0.0 copy-done.4
  153.2 0.0 copy-done.5
  153.2 0.0 copy-done.6
  153.3 0.0 copy-done.7
  153.3 0.0 copy-done.12
  153.3 2.9 %across.1 = f32[32,8192]{1,0:T(8,128)} custom-call(f32[2048,128]{1,0:T(8,128)S(1)} %bitcast.7, bf16[512,512]{1,0:T(8,128)(2,1)S(1)} %copy-done.4, bf16[512,512]{1,0:T(8,128)(2,1)S(1)} %copy-done.5, bf16[256,512]{1,0:T(8,128)(2,1)S(1)} %copy-done.6, bf16[256,512]{1,0:T(8,128)(2,1)S(1)} %copy-done.7, f32[17,512]{1,0:T(8,128)S(1)} %copy-done.12), custom_call_target="tpu_custom_call" | custom-call | tf_op jit(solution)/shard_map/across/pallas_call | solution.py:674
Async XLA Ops:
  2.9 0.7 copy-start.18
  2.9 1.0 copy-start.8
  2.9 1.0 copy-start.9
  3.0 1.0 copy-start.10
  3.0 1.1 copy-start.11
  3.0 1.1 copy-start.15
  3.0 1.1 copy-start.16
  3.0 1.0 copy-start.17
  4.1 1.6 %copy-start = (bf16[1024,1024]{1,0:T(8,128)(2,1)S(1)}, bf16[1024,1024]{1,0:T(8,128)(2,1)}, u32[]{:S(2)}) copy-start(bf16[1024,1024]{1,0:T(8,128)(2,1)} %constant.30.clone.d2h) | copy-start | bytes 6291460
  5.6 37.2 %copy-start.1 = (bf16[512,1024]{1,0:T(8,128)(2,1)S(1)}, bf16[512,1024]{1,0:T(8,128)(2,1)}, u32[]{:S(2)}) copy-start(bf16[512,1024]{1,0:T(8,128)(2,1)} %constant.32.clone.wh_hbm) | copy-start | bytes 3145732
  5.6 37.2 %copy-start.2 = (bf16[512,1024]{1,0:T(8,128)(2,1)S(1)}, bf16[512,1024]{1,0:T(8,128)(2,1)}, u32[]{:S(2)}) copy-start(bf16[512,1024]{1,0:T(8,128)(2,1)} %constant.33.clone.wl_hbm) | copy-start | bytes 3145732
  5.6 37.2 %copy-start.3 = (f32[16,64,256]{2,1,0:T(8,128)S(1)}, f32[16,64,256]{2,1,0:T(8,128)}, u32[]{:S(2)}) copy-start(f32[16,64,256]{2,1,0:T(8,128)} %constant.34.clone.t_hbm) | copy-start | bytes 3145732
  5.7 37.2 %copy-start.13 = (bf16[32,128]{1,0:T(8,128)(2,1)S(1)}, bf16[32,128]{1,0:T(8,128)(2,1)}, u32[]{:S(2)}) copy-start(bf16[32,128]{1,0:T(8,128)(2,1)} %constant.35.clone.eh) | copy-start | bytes 24580
  5.7 37.2 %copy-start.14 = (bf16[32,128]{1,0:T(8,128)(2,1)S(1)}, bf16[32,128]{1,0:T(8,128)(2,1)}, u32[]{:S(2)}) copy-start(bf16[32,128]{1,0:T(8,128)(2,1)} %constant.36.clone.el) | copy-start | bytes 24580
  42.9 110.3 %copy-start.4 = (bf16[512,512]{1,0:T(8,128)(2,1)S(1)}, bf16[512,512]{1,0:T(8,128)(2,1)}, u32[]{:S(2)}) copy-start(bf16[512,512]{1,0:T(8,128)(2,1)} %constant.37.clone.wh) | copy-start | bytes 1572868
  42.9 110.3 %copy-start.5 = (bf16[512,512]{1,0:T(8,128)(2,1)S(1)}, bf16[512,512]{1,0:T(8,128)(2,1)}, u32[]{:S(2)}) copy-start(bf16[512,512]{1,0:T(8,128)(2,1)} %constant.38.clone.wl) | copy-start | bytes 1572868
  42.9 110.3 %copy-start.6 = (bf16[256,512]{1,0:T(8,128)(2,1)S(1)}, bf16[256,512]{1,0:T(8,128)(2,1)}, u32[]{:S(2)}) copy-start(bf16[256,512]{1,0:T(8,128)(2,1)} %constant.39.clone.zh) | copy-start | bytes 786436
  42.9 110.3 %copy-start.7 = (bf16[256,512]{1,0:T(8,128)(2,1)S(1)}, bf16[256,512]{1,0:T(8,128)(2,1)}, u32[]{:S(2)}) copy-start(bf16[256,512]{1,0:T(8,128)(2,1)} %constant.40.clone.zl) | copy-start | bytes 786436
  42.9 110.3 %copy-start.12 = (f32[17,512]{1,0:T(8,128)S(1)}, f32[17,512]{1,0:T(8,128)}, u32[]{:S(2)}) copy-start(f32[17,512]{1,0:T(8,128)} %constant.41.clone.twist) | copy-start | bytes 104452

commit v4 on v3

--- a/solution.py
+++ b/solution.py
@@ -198,27 +198,35 @@
         line = pl.ds(b, 1)
         bl = (base_l[0, rows, :], base_l[1, rows, :])
         bm = (base_m[0, rows, :], base_m[1, rows, :])
-        left, right = [], []
+        real, imag = [], []
         for t in range(4):
             w = bl if t == 0 else times(bl, (fact_l[2 * t - 2, line, :], fact_l[2 * t - 1, line, :]))
-            left += [w[0], w[1]]
-            right += [-w[1], w[0]]
-        lh, ll = split(jnp.concatenate(
-            [jnp.concatenate(left, axis=0), jnp.concatenate(right, axis=0)], axis=1))
+            real.append(w[0])
+            imag.append(w[1])
+        rh, rl = split(jnp.concatenate(real, axis=0))
+        ih, il = split(jnp.concatenate(imag, axis=0))
+        lh = jnp.concatenate([rh, ih], axis=1)
+        ll = jnp.concatenate([rl, il], axis=1)
         cosine, sine = [], []
         for t in range(4):
             i = {0: 0, 1: 1, 3: 2}.get(t)
             w = bm if i is None else times(bm, (fact_m[2 * i, line, :], fact_m[2 * i + 1, line, :]))
             cosine.append(w[0])
             sine.append(w[1])
-        mh, ml = split(jnp.concatenate(
-            [jnp.concatenate(cosine, axis=0), jnp.concatenate(sine, axis=0)], axis=1))
-        o = dot_nt(lh, mh) + (dot_nt(ll, mh) + dot_nt(lh, ml))
-        image[0, rows, :] = jnp.concatenate([o[16 * t:16 * t + 8] for t in range(4)], axis=1)
-        image[1, rows, :] = jnp.concatenate([o[16 * t + 8:16 * t + 16] for t in range(4)], axis=1)
+        cosh, cosl = split(jnp.concatenate(cosine, axis=0))
+        sinh, sinl = split(jnp.concatenate(sine, axis=0))
+        mh = jnp.concatenate(
+            [jnp.concatenate([cosh, sinh], axis=0), jnp.concatenate([-sinh, cosh], axis=0)], axis=1)
+        ml = jnp.concatenate(
+            [jnp.concatenate([cosl, sinl], axis=0), jnp.concatenate([-sinl, cosl], axis=0)], axis=1)
+        o = dot_nt(jnp.concatenate([lh, ll], axis=0), mh)
+        o = o[:32] + (o[32:] + dot_nt(lh, ml))
+        for ri in range(2):
+            lanes = slice(ri * 32, ri * 32 + 32)
+            image[ri, rows, :] = jnp.concatenate([o[8 * t:8 * t + 8, lanes] for t in range(4)], axis=1)
         return 0
 
-    lax.fori_loop(0, n, one_block, 0, unroll=4)
+    lax.fori_loop(0, n, one_block, 0, unroll=n)
 
     here = pl.ds(pl.multiple_of(step * n, n), n)
     for l8 in range(8):

time: 157 us -> 141 us (0.90)
  Pallas kernels: 150 us -> 135 us
    pallas_call x1, Pallas kernels: 37.1 us -> 21.9 us  [make_payload(): pl.pallas_call(grid_kernel, grid=(blocks // STEP,), in_specs=[pl.BlockSpe...]
where the time goes in v4:
time: 141 us
  Pallas kernels  135 us (96%)
  other arithmetic  3.04 us (2%)
  local copies, waits for them, and re-layouts  2.56 us (2%)
    pallas_call x1, Pallas kernels, exchange(): pl.pallas_call(exchange_kernel, in_specs=[vmem, hbm, hbm, hbm, vmem, vmem...  110 us
    pallas_call x1, Pallas kernels, make_payload(): pl.pallas_call(grid_kernel, grid=(blocks // STEP,), in_specs=[pl.BlockSpe...  21.9 us
    pallas_call x1, Pallas kernels, across(): pl.pallas_call(across_kernel, out_shape=jax.ShapeDtypeStruct((32, G), F32...  2.88 us

profile of v4, /device:TPU:32, one launch (start us, length us, event | category | flops | bytes accessed | tf_op | source)
XLA Modules:
  0.0 140.6 jit_solution(10296342557539689889)
XLA Ops:
  0.0 2.3 %copy_convert_fusion = (f32[256,2,1024]{2,0,1:T(8,128)S(1)}, f32[256,2,1024]{2,0,1:T(8,128)S(1)}) fusion(bf16[256,2,1024]{2,1,0:T(2,128)(2,1)} %param.25, bf16[256,2,1024]{2,1,0:T(2,128)(2,1)} %param.24), kind=kLoop, calls=%fused_computation.1 | loop fusion | flops 1048576 | bytes 6291456 | tf_op jit(solution)/shard_map/convert_element_type | solution.py:696
  2.3 0.6 add_bitcast_fusion
  2.9 0.0 copy-start.18
  2.9 0.0 copy-start.8
  2.9 0.0 copy-start.9
  3.0 0.0 copy-start.10
  3.0 0.0 copy-start.11
  3.0 0.0 copy-start.15
  3.0 0.0 copy-start.16
  3.0 0.0 copy-start.17
  3.0 0.1 pad_maximum_fusion.beam_ref
  3.2 0.4 copy-done.18
  3.6 0.1 copy.25.tile_ref
  3.7 0.2 copy-done.8
  3.9 0.1 copy-done.9
  4.0 0.0 copy-done.10
  4.0 0.0 copy-done.11
  4.0 0.0 copy-done.15
  4.0 0.0 copy-done.16
  4.0 0.0 copy-done.17
  4.1 0.0 copy-start
  4.1 1.6 %copy-done = bf16[1024,1024]{1,0:T(8,128)(2,1)S(1)} copy-done((bf16[1024,1024]{1,0:T(8,128)(2,1)S(1)}, bf16[1024,1024]{1,0:T(8,128)(2,1)}, u32[]{:S(2)}) %copy-start) | copy-done | bytes 2097176
  5.6 0.0 copy-start.1
  5.6 0.0 copy-start.2
  5.6 0.0 copy-start.3
  5.7 0.0 copy-start.13
  5.7 0.0 copy-start.14
  5.7 21.9 %gridding.1.src_ref = f32[2176,128]{1,0:T(8,128)S(1)} custom-call(f32[256,2,128]{2,1,0:T(2,128)S(1)} %copy-done.8, f32[256,2,128]{2,1,0:T(2,128)S(1)} %copy-done.9, f32[2,256,1024]{2,1,0:T(8,128)S(1)} %pad_maximum_fusion.beam_ref, s32[1,256]{1,0:T(1,128)S(1)} %copy-done.15, s32[128,1]{1,0:T(8,128)S(1)} %copy.25.tile_ref, s32[1,128]{1,0:T(1,128)S(1)} %bitcast.8, ...), custom_call_target="tpu_custom_call" | custom-call | tf_op jit(solution)/shard_map/gridding/pallas_call | solution.py:283
  27.6 0.0 copy-done.1
  27.6 0.0 copy-done.2
  27.6 0.0 copy-done.3
  27.6 0.0 copy-done.13
  27.7 0.0 copy-done.14
  27.7 0.0 copy-start.4
  27.7 0.0 copy-start.5
  27.7 0.0 copy-start.6
  27.7 0.0 copy-start.7
  27.7 0.0 copy-start.12
  27.7 110.0 %exchange.1 = f32[16,128,128]{2,1,0:T(8,128)S(1)} custom-call(f32[2176,128]{1,0:T(8,128)S(1)} %gridding.1.src_ref, bf16[512,1024]{1,0:T(8,128)(2,1)S(1)} %copy-done.1, bf16[512,1024]{1,0:T(8,128)(2,1)S(1)} %copy-done.2, f32[16,64,256]{2,1,0:T(8,128)S(1)} %copy-done.3, bf16[32,128]{1,0:T(8,128)(2,1)S(1)} %copy-done.13, bf16[32,128]{1,0:T(8,128)(2,1)S(1)} %copy-done.14), custom_call_target="tpu_custom_call" | custom-call | tf_op jit(solution)/shard_map/exchange/pallas_call | solution.py:596
  137.7 0.0 copy-done.4
  137.7 0.0 copy-done.5
  137.7 0.0 copy-done.6
  137.7 0.0 copy-done.7
  137.7 0.0 copy-done.12
  137.8 2.9 %across.1 = f32[32,8192]{1,0:T(8,128)} custom-call(f32[2048,128]{1,0:T(8,128)S(1)} %bitcast.7, bf16[512,512]{1,0:T(8,128)(2,1)S(1)} %copy-done.4, bf16[512,512]{1,0:T(8,128)(2,1)S(1)} %copy-done.5, bf16[256,512]{1,0:T(8,128)(2,1)S(1)} %copy-done.6, bf16[256,512]{1,0:T(8,128)(2,1)S(1)} %copy-done.7, f32[17,512]{1,0:T(8,128)S(1)} %copy-done.12), custom_call_target="tpu_custom_call" | custom-call | tf_op jit(solution)/shard_map/across/pallas_call | solution.py:682
Async XLA Ops:
  2.9 0.7 copy-start.18
  2.9 1.0 copy-start.8
  2.9 1.0 copy-start.9
  3.0 1.0 copy-start.10
  3.0 1.1 copy-start.11
  3.0 1.1 copy-start.15
  3.0 1.1 copy-start.16
  3.0 1.0 copy-start.17
  4.1 1.6 %copy-start = (bf16[1024,1024]{1,0:T(8,128)(2,1)S(1)}, bf16[1024,1024]{1,0:T(8,128)(2,1)}, u32[]{:S(2)}) copy-start(bf16[1024,1024]{1,0:T(8,128)(2,1)} %constant.30.clone.d2h) | copy-start | bytes 6291460
  5.6 22.0 %copy-start.1 = (bf16[512,1024]{1,0:T(8,128)(2,1)S(1)}, bf16[512,1024]{1,0:T(8,128)(2,1)}, u32[]{:S(2)}) copy-start(bf16[512,1024]{1,0:T(8,128)(2,1)} %constant.32.clone.wh_hbm) | copy-start | bytes 3145732
  5.6 22.0 %copy-start.2 = (bf16[512,1024]{1,0:T(8,128)(2,1)S(1)}, bf16[512,1024]{1,0:T(8,128)(2,1)}, u32[]{:S(2)}) copy-start(bf16[512,1024]{1,0:T(8,128)(2,1)} %constant.33.clone.wl_hbm) | copy-start | bytes 3145732
  5.6 22.0 %copy-start.3 = (f32[16,64,256]{2,1,0:T(8,128)S(1)}, f32[16,64,256]{2,1,0:T(8,128)}, u32[]{:S(2)}) copy-start(f32[16,64,256]{2,1,0:T(8,128)} %constant.34.clone.t_hbm) | copy-start | bytes 3145732
  5.7 22.0 %copy-start.13 = (bf16[32,128]{1,0:T(8,128)(2,1)S(1)}, bf16[32,128]{1,0:T(8,128)(2,1)}, u32[]{:S(2)}) copy-start(bf16[32,128]{1,0:T(8,128)(2,1)} %constant.35.clone.eh) | copy-start | bytes 24580
  5.7 22.0 %copy-start.14 = (bf16[32,128]{1,0:T(8,128)(2,1)S(1)}, bf16[32,128]{1,0:T(8,128)(2,1)}, u32[]{:S(2)}) copy-start(bf16[32,128]{1,0:T(8,128)(2,1)} %constant.36.clone.el) | copy-start | bytes 24580
  27.7 110.0 %copy-start.4 = (bf16[512,512]{1,0:T(8,128)(2,1)S(1)}, bf16[512,512]{1,0:T(8,128)(2,1)}, u32[]{:S(2)}) copy-start(bf16[512,512]{1,0:T(8,128)(2,1)} %constant.37.clone.wh) | copy-start | bytes 1572868
  27.7 110.0 %copy-start.5 = (bf16[512,512]{1,0:T(8,128)(2,1)S(1)}, bf16[512,512]{1,0:T(8,128)(2,1)}, u32[]{:S(2)}) copy-start(bf16[512,512]{1,0:T(8,128)(2,1)} %constant.38.clone.wl) | copy-start | bytes 1572868
  27.7 110.0 %copy-start.6 = (bf16[256,512]{1,0:T(8,128)(2,1)S(1)}, bf16[256,512]{1,0:T(8,128)(2,1)}, u32[]{:S(2)}) copy-start(bf16[256,512]{1,0:T(8,128)(2,1)} %constant.39.clone.zh) | copy-start | bytes 786436
  27.7 110.0 %copy-start.7 = (bf16[256,512]{1,0:T(8,128)(2,1)S(1)}, bf16[256,512]{1,0:T(8,128)(2,1)}, u32[]{:S(2)}) copy-start(bf16[256,512]{1,0:T(8,128)(2,1)} %constant.40.clone.zl) | copy-start | bytes 786436
  27.7 110.0 %copy-start.12 = (f32[17,512]{1,0:T(8,128)S(1)}, f32[17,512]{1,0:T(8,128)}, u32[]{:S(2)}) copy-start(f32[17,512]{1,0:T(8,128)} %constant.41.clone.twist) | copy-start | bytes 104452

commit v5 on v4

--- a/solution.py
+++ b/solution.py
@@ -115,20 +115,21 @@
 
 
 def across_tables():
-    p, bc = np.meshgrid(np.arange(16), np.arange(8), indexing="ij")
-    m1 = np.arange(256)[None, None, :]
-    w = np.zeros((2, 2, 128, 2, 256))
-    for s in range(2):
-        v1 = (8 * p + bc if s == 0 else 8 * (31 - p) + bc).reshape(128, 1)
-        phi = 2 * math.pi * ((v1 * np.arange(256)[None, :]) % 256) / 256
-        w[s, 0, :, 0], w[s, 1, :, 0] = np.cos(phi), -np.sin(phi)
-        w[s, 0, :, 1], w[s, 1, :, 1] = np.sin(phi), np.cos(phi)
-    zero = w[0].copy()
-    zero[1, 0, 0] = 1 - 2 * (np.arange(256) % 2)
-    zero[1, 0, 1] = 0
+    w = np.zeros((3, 2, 2, 2, 4, 16, 2, 256))
+    m1 = np.arange(256)
+    bc2, p = np.meshgrid(np.arange(4), np.arange(16), indexing="ij")
+    for bcl in range(2):
+        bc = bc2 * 2 + bcl
+        for kind, s, v1 in ((0, 0, 8 * p + bc), (0, 1, 8 * (31 - p) + bc), (1, 0, 8 * p + bc), (2, 1, 8 * p + bc)):
+            phi = 2 * math.pi * ((v1[:, :, None] * m1) % 256) / 256
+            w[kind, bcl, 0, s, :, :, 0], w[kind, bcl, 1, s, :, :, 0] = np.cos(phi), -np.sin(phi)
+            w[kind, bcl, 0, s, :, :, 1], w[kind, bcl, 1, s, :, :, 1] = np.sin(phi), np.cos(phi)
+    w[1, 0, 1, 0, 0, 0, 0] = 1 - 2 * (m1 % 2)
+    w[1, 0, 1, 0, 0, 0, 1] = 0
+    w = w.reshape(3, 512, 512)
     psi = 2 * math.pi * np.arange(17)[:, None] * np.arange(256)[None, :] / G
     twist = np.concatenate([np.cos(psi), np.sin(psi)], axis=1).astype(np.float32)
-    return w.reshape(512, 512), zero.reshape(256, 512), twist
+    return w[0], np.concatenate([w[1], w[2]], axis=1), twist
 
 
 def turn(t):
@@ -155,12 +156,21 @@
 
 
 def grid_kernel(
-    uv_ref, vis_ref, beam_ref, seg_ref, tile_ref, row_ref, col_ref, d1h, d1l, d2h, d2l,
+    uv_ref, vis_ref, beam_ref, seg_ref, tile_ref, row_ref, col_ref, d1h, d1l, d2h_hbm, d2l_hbm,
     out_ref,
-    base_l, base_m, fact_l, fact_m, image, ch, cl, ah, al,
+    base_l, base_m, fact_l, fact_m, image, ch, cl, ah, al, d2h, d2l, table_sem,
 ):
     step = pl.program_id(0)
     n = STEP
+    tables = [
+        pltpu.make_async_copy(a, b, table_sem.at[i]) for i, (a, b) in enumerate(((d2h_hbm, d2h), (d2l_hbm, d2l)))
+    ]
+
+    @pl.when(step == 0)
+    def _():
+        for c in tables:
+            c.start()
+
     zu = turn(uv_ref[:, 0, :] * (1 / 32))
     zv = turn(uv_ref[:, 1, :] * (1 / 32))
     vis = (vis_ref[:, 0, :], vis_ref[:, 1, :])
@@ -254,7 +264,9 @@
         slot = pair * 32 + side * 16 + (tile // 32) * 2 + rank
         code = (slot * 256 + col_ref[...] * 32 + row_ref[...]).astype(F32)
         for j in range(CLASSES):
-            out_ref[j * tall + subs:(j + 1) * tall, :] = jnp.broadcast_to(code, (8, subs))
+            out_ref[j * tall + 64:j * tall + 72, :] = jnp.broadcast_to(code, (8, subs))
+        swap = down_it.astype(jnp.int32) % 32 >= 16
+        half = lax.broadcasted_iota(jnp.int32, (64, 128), 1) < 64
         blocks = seg_ref.shape[1]
         pick = (seg_ref[...] == lax.broadcasted_iota(jnp.int32, (subs, blocks), 0)).astype(F32).astype(BF16)
         for l8 in range(8):
@@ -265,13 +277,20 @@
                 h, l = split(a[:, cg * 128:(cg + 1) * 128])
                 ah[cg * subs:(cg + 1) * subs, l8 * 128:(l8 + 1) * 128] = h
                 al[cg * subs:(cg + 1) * subs, l8 * 128:(l8 + 1) * 128] = l
+        for c in tables:
+            c.wait()
         for tile in range(4):
             lanes = slice(tile * 256, (tile + 1) * 256)
             spec = dot3(ah[...], al[...], d2h[:, lanes], d2l[:, lanes])
             for cg in range(2):
                 for k in range(2):
                     j = cg * 8 + tile * 2 + k
-                    out_ref[j * tall:j * tall + subs, :] = spec[cg * subs:(cg + 1) * subs, k * 128:(k + 1) * 128]
+                    f = spec[cg * subs:(cg + 1) * subs, k * 128:(k + 1) * 128]
+                    r = pltpu.roll(f, 64, 1)
+                    if j:
+                        f, r = jnp.where(swap, r, f), jnp.where(swap, f, r)
+                    out_ref[j * tall:j * tall + 64, :] = jnp.where(half, f[:64], r[64:])
+                    out_ref[j * tall + 72:j * tall + 136, :] = jnp.where(half, r[:64], f[64:])
 
 
 def make_payload(uv, vis, beam, seg, tile, row, col, tables):
@@ -288,7 +307,8 @@
             pl.BlockSpec((STEP, 2, visible), lambda i: (i, 0, 0)),
             pl.BlockSpec((2, STEP, SUB * SUB), lambda i: (0, i, 0)),
             whole((1, blocks)), whole((subs, 1)), whole((1, subs)), whole((1, subs)),
-            whole((256, 256)), whole((256, 256)), whole((1024, 1024)), whole((1024, 1024)),
+            whole((256, 256)), whole((256, 256)),
+            pl.BlockSpec(memory_space=pl.ANY), pl.BlockSpec(memory_space=pl.ANY),
         ],
         out_specs=whole((CLASSES * tall, 128)),
         out_shape=jax.ShapeDtypeStruct((CLASSES * tall, 128), F32),
@@ -302,6 +322,9 @@
             pltpu.VMEM((blocks, 2048), BF16),
             pltpu.VMEM((2 * subs, 1024), BF16),
             pltpu.VMEM((2 * subs, 1024), BF16),
+            pltpu.VMEM((1024, 1024), BF16),
+            pltpu.VMEM((1024, 1024), BF16),
+            pltpu.SemaphoreType.DMA((2,)),
         ],
         compiler_params=pltpu.CompilerParams(vmem_limit_bytes=48 * MB),
         name="gridding",
@@ -319,7 +342,7 @@
 
 def exchange_kernel(
     src_ref, wh_hbm, wl_hbm, t_hbm, eh, el, out_ref,
-    near, box, held, grid_ref, x_ref, edge_src, edge_in, wh, wl, t_ref, lh, ll, kbuf, near2,
+    near, box, held, grid_ref, x_ref, edge_src, edge_in, wh, wl, t_ref, lh, ll, kbuf, near2, fwd,
     near_send, near_recv, far_send, far_recv, edge_send, edge_recv, table_sem,
     near2_send, near2_recv, far2_send, far2_recv,
 ):
@@ -359,230 +382,264 @@
         pl.semaphore_signal(barrier, inc=1, device_id=(ty, core, z, tx), device_id_type=MESH)
     pl.semaphore_wait(barrier, 30)
 
-    def near_copy(k):
+    def near_copy(ab, k):
         tz, tc = to_near(k)
+        first, rows = (72, 64) if ab else (0, 72)
         return pltpu.make_async_remote_copy(
-            src_ref=src_ref.at[pl.ds(pl.multiple_of((tz * 2 + tc) * tall, 8), tall), :],
-            dst_ref=near.at[k],
-            send_sem=near_send.at[k],
-            recv_sem=near_recv.at[k],
+            src_ref=src_ref.at[pl.ds(pl.multiple_of((tz * 2 + tc) * tall + first, 8), rows), :],
+            dst_ref=near.at[k, pl.ds(first, rows), :],
+            send_sem=near_send.at[ab, k],
+            recv_sem=near_recv.at[ab, k],
             device_id=(y, tc, tz, x),
             device_id_type=MESH,
         )
 
-    def far_copy(g, k):
+    def far_copy(ab, g, k):
         ty, tx = to_far(k)
-        h, rows = g // 2, pl.ds((g % 2) * 128, 128 + 8 * (g % 2))
+        h, rows = g // 2, pl.ds((g % 2) * 64, 64 + (8 if g % 2 and ab == 0 else 0))
         return pltpu.make_async_remote_copy(
-            src_ref=box.at[h, ty * 4 + tx, rows, :],
-            dst_ref=held.at[h, k, rows, :],
-            send_sem=far_send.at[g, k],
-            recv_sem=far_recv.at[g, k],
+            src_ref=box.at[ab, h, ty * 4 + tx, rows, :],
+            dst_ref=held.at[ab, h, k, rows, :],
+            send_sem=far_send.at[ab, g, k],
+            recv_sem=far_recv.at[ab, g, k],
             device_id=(ty, core, z, tx),
             device_id_type=MESH,
         )
 
-    for k in range(1, 16):
-        near_copy(k).start()
+    window = 8
+    queue = [(ab, k) for ab in range(2) for k in range(1, 16)]
+    for item in queue[:window]:
+        near_copy(*item).start()
     near[0] = src_ref[pl.ds(pl.multiple_of(kind * tall, 8), tall), :]
 
-    slots = lax.broadcasted_iota(jnp.int32, (512, subs), 0)
+    zero_class = kind == 0
+    special = jnp.where((kind == 0) & (group == 0), 1, 0)
+    row = lax.broadcasted_iota(jnp.int32, (512, subs), 0)
     line = lax.broadcasted_iota(jnp.int32, (8, subs), 0)
-    codes = jnp.zeros((8, subs), F32)
-    for g in range(4):
-        h = g // 2
-        for i in range(4):
-            k8 = (g % 2) * 4 + i
-            k = h * 8 + k8
-            if k:
-                near_copy(k).wait_recv()
-            code = near[k, subs:subs + 1, :]
-            fits = (code.astype(jnp.int32) // 256 == slots).astype(F32).astype(BF16)
-            hi, lo = split(near[k, :subs, :])
-            o = dot(jnp.concatenate([fits, fits], axis=1), jnp.concatenate([hi, lo], axis=0))
-            for p in range(PAIRS):
-                box[h, p, k8 * 32:k8 * 32 + 32, :] = o[p * 32:(p + 1) * 32]
-            codes = jnp.where(line == k8, code, codes)
-        if g % 2 == 1:
-            for p in range(PAIRS):
-                box[h, p, 256:264, :] = codes
-        for k in range(15):
-            far_copy(g, k).start()
-        if g % 2 == 1:
-            held[h, 15] = box[h, group]
+    left = lax.broadcasted_iota(jnp.int32, (256, 128), 1) < 64
+    for ab in range(2):
+        side = jnp.where(zero_class, 0, ab)
+        slots = row % 256 // 16 * 32 + (row // 256 + side) % 2 * 16 + row % 16
+        first = 72 if ab else 0
+        codes = jnp.zeros((8, subs), F32)
+        for g in range(4):
+            h = g // 2
+            for i in range(4):
+                k8 = (g % 2) * 4 + i
+                k = h * 8 + k8
+                if k:
+                    near_copy(ab, k).wait()
+                    after = queue.index((ab, k)) + window
+                    if after < len(queue):
+                        near_copy(*queue[after]).start()
+                code = near[k, 64:65, :]
+                fits = (code.astype(jnp.int32) // 256 == slots).astype(F32).astype(BF16)
+                data = near[k, first:first + 64, :]
+                turned = pltpu.roll(data, 64, 1)
+                hi, lo = split(jnp.concatenate(
+                    [jnp.where(left[:64], data, turned), jnp.where(left[:64], turned, data)], axis=0))
+                o = dot(jnp.concatenate([fits, fits], axis=1), jnp.concatenate([hi, lo], axis=0))
+                o = jnp.where(left, o[:256], o[256:])
+                for p in range(PAIRS):
+                    box[ab, h, p, k8 * 16:k8 * 16 + 16, :] = o[p * 16:(p + 1) * 16]
+                codes = jnp.where(line == k8, code, codes)
+            if g % 2 == 1 and ab == 0:
+                for p in range(PAIRS):
+                    box[0, h, p, 128:136, :] = codes
+            for k in range(15):
+                if ab:
+                    far_copy(0, g, k).wait_send()
+                far_copy(ab, g, k).start()
+            if g % 2 == 1:
+                rows = slice(0, 136 if ab == 0 else 128)
+                held[ab, h, 15, rows, :] = box[ab, h, group, rows, :]
 
     pos = lax.broadcasted_iota(jnp.int32, (256, 256), 0).astype(F32)
-    for h in range(2):
-        for g in (2 * h, 2 * h + 1):
-            for k in range(15):
-                far_copy(g, k).wait_recv()
-        code = jnp.concatenate([held[h, k, 256:264, :] for k in range(16)], axis=0).T.astype(jnp.int32)
-        at = code // 256 - group * 32
-        value = (code % 256 + 1).astype(F32)
-
-        def put(i):
-            hot, data = [], []
-            for rank in range(2):
-                slot = i * 2 + rank
-                label = jnp.sum(jnp.where(at == slot, value, 0.0), axis=0, keepdims=True) - 1.0
-                hot.append(label)
-                data += [held[h, k, pl.ds(slot, 8, stride=32), :] for k in range(16)]
-            fits = (jnp.concatenate(hot, axis=1) == pos).astype(F32).astype(BF16)
-            hi, lo = split(jnp.concatenate(data, axis=0))
-            v = dot(fits, jnp.concatenate([hi, lo], axis=1))
-            v = v[:, :128] + v[:, 128:]
-            rows = pl.ds(pl.multiple_of(i % 8 * 32, 32), 32)
-            for bc in range(8):
-                where = i // 8 * 8 + bc
-                add = v[bc * 32:(bc + 1) * 32]
-                grid_ref[where, rows, :] = add if h == 0 else grid_ref[where, rows, :] + add
+
+    def place(ab):
+        side = jnp.where(zero_class, 0, ab)
+        if ab == 0:
+            grid_ref[0, :, 64:128] = jnp.zeros((256, 64), F32)
+            grid_ref[8] = jnp.zeros((256, 128), F32)
+            last = jnp.where(zero_class, 8, 7)
+        else:
+            last = 7
+        for h in range(2):
+            for g in (2 * h, 2 * h + 1):
+                for k in range(15):
+                    far_copy(ab, g, k).wait_recv()
+            code = jnp.concatenate([held[0, h, k, 128:136, :] for k in range(16)], axis=0).T.astype(jnp.int32)
+            at = code // 256 - group * 32
+            value = (code % 256 + 1).astype(F32)
+
+            def put(r):
+                hot = [[], []]
+                data = []
+                for rank in range(2):
+                    slot = r * 2 + rank
+                    for n, which in enumerate((side, 1 - side)):
+                        hot[n].append(jnp.sum(
+                            jnp.where(at == slot + which * 16, value, 0.0), axis=0, keepdims=True) - 1.0)
+                    data += [held[ab, h, k, pl.ds(slot, 8, stride=16), :] for k in range(16)]
+                fits = jnp.concatenate(
+                    [(jnp.concatenate(x, axis=1) == pos).astype(F32).astype(BF16) for x in hot], axis=0)
+                hi, lo = split(jnp.concatenate(data, axis=0))
+                v = dot(fits, jnp.concatenate([hi, lo], axis=1))
+                v = v[:, :128] + v[:, 128:]
+                rows = pl.ds(pl.multiple_of(r * 32, 32), 32)
+                for bc in range(8):
+                    own = v[bc * 32:(bc + 1) * 32, 0:64]
+                    mirror = v[256 + bc * 32:256 + (bc + 1) * 32, 64:128]
+                    if h == 1:
+                        own = grid_ref[bc, rows, 0:64] + own
+                        mirror = grid_ref[last - bc, rows, 64:128] + mirror
+                    grid_ref[bc, rows, 0:64] = own
+                    grid_ref[last - bc, rows, 64:128] = mirror
+
+            loop(0, 8, put)
 
         def flip(i):
             x_ref[pl.ds(pl.multiple_of(i * 128, 128), 128), :] = grid_ref[i].T
 
-        if h == 0:
-            loop(0, 16, put)
-        else:
-            loop(8, 16, put)
-            edge_src[...] = grid_ref[8].T[:64]
-            tx, ty = (x + 1) % 4, (y + (x + 1) // 4) % 4
-            edge = pltpu.make_async_remote_copy(
-                src_ref=edge_src, dst_ref=edge_in, send_sem=edge_send, recv_sem=edge_recv,
-                device_id=(ty, core, z, tx), device_id_type=MESH,
-            )
-            edge.start()
-            loop(8, 16, flip)
-            loop(0, 8, put)
-            loop(0, 8, flip)
-
-    edge.wait_recv()
-    zero_class = kind == 0
-    special = jnp.where((kind == 0) & (group == 0), 1, 0)
-    near_x = lambda s, bc: x_ref[s * 1024 + bc * 128:s * 1024 + bc * 128 + 64, :]
-    far_x = lambda s, bc: x_ref[s * 1024 + bc * 128 + 64:s * 1024 + bc * 128 + 128, :]
-    for bc in range(8):
-        for s in range(2):
-            if s == 0:
-                own = near_x(0, bc)
-                first = edge_in[...] if bc == 0 else near_x(1, 8 - bc)
-                mirror = jnp.where(zero_class, first, far_x(1, 7 - bc))
-            else:
-                own = jnp.where(zero_class, far_x(0, bc), near_x(1, bc))
-                mirror = jnp.where(zero_class, far_x(1, 7 - bc), far_x(0, 7 - bc))
+        loop(0, 8, flip)
+
+    tx, ty = (x + 1) % 4, (y + (x + 1) // 4) % 4
+    edge = pltpu.make_async_remote_copy(
+        src_ref=edge_src, dst_ref=edge_in, send_sem=edge_send, recv_sem=edge_recv,
+        device_id=(ty, core, z, tx), device_id_type=MESH,
+    )
+
+    e2 = jnp.concatenate([eh[...], eh[...]], axis=1)
+    low = lax.broadcasted_iota(jnp.int32, (32, 128), 1) < 64
+
+    def near2_copy(ab, nt, t, dc):
+        zh, tc = (z // 2 + t) % 4, (core + dc) % 2
+        tz = zh * 2 + nt
+        return (tz * 2 + tc) != kind, pltpu.make_async_remote_copy(
+            src_ref=kbuf.at[pl.ds(pl.multiple_of(((ab * 2 + nt) * 8 + tc * 4 + zh) * 64, 64), 64), :],
+            dst_ref=near2.at[ab, kind],
+            send_sem=near2_send.at[ab, nt, t, dc],
+            recv_sem=near2_recv.at[ab, kind],
+            device_id=(y, tc, tz, x),
+            device_id_type=MESH,
+        )
+
+    def transform(ab):
+        for bc in range(8):
+            own = x_ref[bc * 128:bc * 128 + 64, :]
+            mirror = x_ref[bc * 128 + 64:bc * 128 + 128, :]
+            if ab == 0 and bc == 0:
+                mirror = jnp.where(zero_class, edge_in[...], mirror)
             for c2, v in enumerate((own, mirror)):
                 hi, lo = split(v)
-                row = (bc * 2 + s) * 64 + c2 * 32
+                row = bc * 64 + c2 * 32
                 for ri in range(2):
                     lh[row:row + 32, ri * 256:(ri + 1) * 256] = hi[ri * 32:(ri + 1) * 32]
                     ll[row:row + 32, ri * 256:(ri + 1) * 256] = lo[ri * 32:(ri + 1) * 32]
+        for nt in range(2):
+            cols = slice(nt * 512, (nt + 1) * 512)
+
+            def one(i):
+                rows = pl.ds(pl.multiple_of(i * 256, 256), 256)
+                v = dot3(lh[rows, :], ll[rows, :], wh[:, cols], wl[:, cols])
+                for k in range(2):
+                    parts = []
+                    for b in range(2):
+                        r = (k * 2 + b) * 64
+                        ya, yb = v[r:r + 64, :256], v[r:r + 64, 256:]
+                        which = 0
+                        if ab == 0 and k == 0 and b == 0:
+                            which = jnp.where(i == 0, special, 0)
+                        tab = lambda n: t_ref[which * 8 + n * 2 + nt]
+                        parts.append(jnp.concatenate(
+                            [ya * tab(0) + yb * tab(1), ya * tab(2) + yb * tab(3)], axis=0))
+                    th, tl = split(jnp.concatenate(parts, axis=1))
+                    o = dot(e2, jnp.concatenate([th, tl], axis=0)) + dot(el[...], th)
+                    for g in range(2):
+                        o0 = o[:, g * 128:(g + 1) * 128]
+                        o1 = o[:, 256 + g * 128:256 + (g + 1) * 128]
+                        pair = (jnp.where(low, o0, pltpu.roll(o1, 64, 1)), jnp.where(low, pltpu.roll(o0, 64, 1), o1))
+                        for e in range(2):
+                            for ty in range(4):
+                                first = (ab * 2 + nt) * 512 + ty * 16 + (g * 2 + e) * 4 + i * 2 + k
+                                kbuf[pl.ds(first, 8, stride=64), :] = pair[e][ty * 8:(ty + 1) * 8]
+
+            loop(0, 2, one)
+            for t in (0, 1, 3, 2):
+                for dc in range(2):
+                    other, copy = near2_copy(ab, nt, t, dc)
+
+                    @pl.when(other)
+                    def _():
+                        copy.start()
+
+        mine = ab * 1024 + ((z % 2) * 8 + core * 4 + z // 2) * 64
+        near2[ab, kind] = kbuf[pl.ds(pl.multiple_of(mine, 64), 64), :]
+
+    place(0)
+    edge_src[...] = grid_ref[8].T[64:]
+    edge.start()
     for c in tables:
         c.wait()
-    e2 = jnp.concatenate([eh[...], eh[...]], axis=1)
-    low = lax.broadcasted_iota(jnp.int32, (32, 128), 1) < 64
-
-    def near2_copy(nt, t, dc):
-        zh, tc = (z // 2 + t) % 4, (core + dc) % 2
-        tz = zh * 2 + nt
-        return (tz * 2 + tc) != kind, pltpu.make_async_remote_copy(
-            src_ref=kbuf.at[pl.ds(pl.multiple_of((nt * 8 + tc * 4 + zh) * 128, 128), 128), :],
-            dst_ref=near2.at[kind],
-            send_sem=near2_send.at[nt, t, dc],
-            recv_sem=near2_recv.at[kind],
-            device_id=(y, tc, tz, x),
-            device_id_type=MESH,
-        )
-
-    for nt in range(2):
-        cols = slice(nt * 512, (nt + 1) * 512)
-
-        def one(i):
-            rows = pl.ds(pl.multiple_of(i * 256, 256), 256)
-            v = dot3(lh[rows, :], ll[rows, :], wh[:, cols], wl[:, cols])
-            for k in range(2):
-                bc = i * 2 + k
-                parts = []
-                for s in range(2):
-                    r = (k * 2 + s) * 64
-                    ya, yb = v[r:r + 64, :256], v[r:r + 64, 256:]
-                    which = 0
-                    if s == 0 and k == 0:
-                        which = jnp.where(i == 0, special, 0)
-                    tab = lambda n: t_ref[which * 8 + n * 2 + nt]
-                    parts.append(jnp.concatenate(
-                        [ya * tab(0) + yb * tab(1), ya * tab(2) + yb * tab(3)], axis=0))
-                th, tl = split(jnp.concatenate(parts, axis=1))
-                o = dot(e2, jnp.concatenate([th, tl], axis=0)) + dot(el[...], th)
-                for g in range(2):
-                    o0 = o[:, g * 128:(g + 1) * 128]
-                    o1 = o[:, 256 + g * 128:256 + (g + 1) * 128]
-                    pair = (jnp.where(low, o0, pltpu.roll(o1, 64, 1)), jnp.where(low, pltpu.roll(o0, 64, 1), o1))
-                    for e in range(2):
-                        for ty in range(4):
-                            first = nt * 1024 + ty * 32 + (g * 2 + e) * 8 + bc
-                            kbuf[pl.ds(first, 8, stride=128), :] = pair[e][ty * 8:(ty + 1) * 8]
-
-        loop(0, 4, one)
-        for t in (0, 1, 3, 2):
-            for dc in range(2):
-                other, copy = near2_copy(nt, t, dc)
-
-                @pl.when(other)
-                def _():
-                    copy.start()
-
-    mine = (z % 2) * 8 + core * 4 + z // 2
-    near2[kind] = kbuf[pl.ds(pl.multiple_of(mine * 128, 128), 128), :]
-
-    def far2_copy(t, k):
+    edge.wait_recv()
+    transform(0)
+    place(1)
+    transform(1)
+
+    def far2_copy(ab, t, k):
         ty, tx = to_far(k)
-        kinds = pl.ds(((z // 2 - t + 4) % 4) * 4, 4)
         return pltpu.make_async_remote_copy(
-            src_ref=near2.at[kinds, pl.ds(pl.multiple_of((ty * 4 + tx) * 8, 8), 8), :],
-            dst_ref=out_ref.at[kinds, pl.ds(pl.multiple_of(group * 8, 8), 8), :],
-            send_sem=far2_send.at[t, k],
-            recv_sem=far2_recv.at[t, k],
+            src_ref=fwd.at[ab, t, ty * 4 + tx],
+            dst_ref=out_ref.at[ab, (z // 2 - t + 4) % 4, group],
+            send_sem=far2_send.at[ab, t, k],
+            recv_sem=far2_recv.at[ab, t, k],
             device_id=(ty, core, z, tx),
             device_id_type=MESH,
         )
 
-    for t in (0, 1, 3, 2):
-        base = ((z // 2 - t + 4) % 4) * 4
-        for i in range(4):
-            sender = base + i
-
-            @pl.when(sender != kind)
-            def _():
-                pltpu.make_async_remote_copy(
-                    src_ref=kbuf.at[pl.ds(0, 128), :], dst_ref=near2.at[sender],
-                    send_sem=near2_send.at[0, 0, 0], recv_sem=near2_recv.at[sender],
-                    device_id=(y, 1 - core, z, x), device_id_type=MESH,
-                ).wait_recv()
-
-        for k in range(15):
-            far2_copy(t, k).start()
-        own = pl.ds(pl.multiple_of(group * 8, 8), 8)
-        out_ref[pl.ds(base, 4), own, :] = near2[pl.ds(base, 4), own, :]
-
-    for t in range(4):
-        for k in range(15):
-            far2_copy(t, k).wait_recv()
+    for ab in range(2):
+        for t in (0, 1, 3, 2):
+            zh = (z // 2 - t + 4) % 4
+            for i in range(4):
+                sender = zh * 4 + i
+
+                @pl.when(sender != kind)
+                def _():
+                    pltpu.make_async_remote_copy(
+                        src_ref=kbuf.at[pl.ds(0, 64), :], dst_ref=near2.at[ab, sender],
+                        send_sem=near2_send.at[0, 0, 0, 0], recv_sem=near2_recv.at[ab, sender],
+                        device_id=(y, 1 - core, z, x), device_id_type=MESH,
+                    ).wait_recv()
+
+                for m in range(8):
+                    v = near2[ab, sender, m * 8:(m + 1) * 8, :]
+                    for e in range(2):
+                        fwd[ab, t, m * 2 + e, i * 4:i * 4 + 4, :] = v[e * 4:(e + 1) * 4]
+            for k in range(15):
+                far2_copy(ab, t, k).start()
+            out_ref[ab, zh, group] = fwd[ab, t, group]
+
+    for ab in range(2):
+        for t in range(4):
+            for k in range(15):
+                far2_copy(ab, t, k).wait_recv()
     edge.wait_send()
-    for k in range(1, 16):
-        near_copy(k).wait_send()
     for g in range(4):
         for k in range(15):
-            far_copy(g, k).wait_send()
-    for nt in range(2):
+            far_copy(1, g, k).wait_send()
+    for ab in range(2):
+        for nt in range(2):
+            for t in range(4):
+                for dc in range(2):
+                    other, copy = near2_copy(ab, nt, t, dc)
+
+                    @pl.when(other)
+                    def _():
+                        copy.wait_send()
+    for ab in range(2):
         for t in range(4):
-            for dc in range(2):
-                other, copy = near2_copy(nt, t, dc)
-
-                @pl.when(other)
-                def _():
-                    copy.wait_send()
-    for t in range(4):
-        for k in range(15):
-            far2_copy(t, k).wait_send()
+            for k in range(15):
+                far2_copy(ab, t, k).wait_send()
 
 
 def exchange(payload):
@@ -597,24 +654,25 @@
         exchange_kernel,
         in_specs=[vmem, hbm, hbm, hbm, vmem, vmem],
         out_specs=vmem,
-        out_shape=jax.ShapeDtypeStruct((16, 128, 128), F32),
+        out_shape=jax.ShapeDtypeStruct((2, 4, 16, 16, 128), F32),
         scratch_shapes=[
             pltpu.VMEM((16, tall, 128), F32),
-            pltpu.VMEM((2, 16, 264, 128), F32),
-            pltpu.VMEM((2, 16, 264, 128), F32),
-            pltpu.VMEM((16, 256, 128), F32),
-            pltpu.VMEM((2048, 256), F32),
+            pltpu.VMEM((2, 2, 16, 136, 128), F32),
+            pltpu.VMEM((2, 2, 16, 136, 128), F32),
+            pltpu.VMEM((9, 256, 128), F32),
+            pltpu.VMEM((1024, 256), F32),
             pltpu.VMEM((64, 256), F32),
             pltpu.VMEM((64, 256), F32),
             pltpu.VMEM((512, 1024), BF16),
             pltpu.VMEM((512, 1024), BF16),
             pltpu.VMEM((16, 64, 256), F32),
-            pltpu.VMEM((1024, 512), BF16),
-            pltpu.VMEM((1024, 512), BF16),
+            pltpu.VMEM((512, 512), BF16),
+            pltpu.VMEM((512, 512), BF16),
             pltpu.VMEM((2048, 128), F32),
-            pltpu.VMEM((16, 128, 128), F32),
-            dma((16,)), dma((16,)), dma((4, 16)), dma((4, 16)), dma(()), dma(()), dma((3,)),
-            dma((2, 4, 2)), dma((16,)), dma((4, 16)), dma((4, 16)),
+            pltpu.VMEM((2, 16, 64, 128), F32),
+            pltpu.VMEM((2, 4, 16, 16, 128), F32),
+            dma((2, 16)), dma((2, 16)), dma((2, 4, 16)), dma((2, 4, 16)), dma(()), dma(()), dma((3,)),
+            dma((2, 2, 4, 2)), dma((2, 16)), dma((2, 4, 16)), dma((2, 4, 16)),
         ],
         compiler_params=pltpu.CompilerParams(
             collective_id=0, has_side_effects=True, vmem_limit_bytes=48 * MB
@@ -625,13 +683,15 @@
 
 def across_kernel(k_ref, wh, wl, zh, zl, twist, out_ref, lh, ll, y_ref):
     for j in range(16):
-        a = k_ref[j * 128:(j + 1) * 128, :].T
+        first = [(ab * 4 + j // 4) * 256 + j % 4 * 4 + bc2 for ab in range(2) for bc2 in range(4)]
+        a = jnp.concatenate([k_ref[pl.ds(i, PAIRS, stride=16), :] for i in first], axis=0).T
         h, l = split(a)
         for i in range(4):
             lh[j * 32:(j + 1) * 32, i * 128:(i + 1) * 128] = h[i * 32:(i + 1) * 32]
             ll[j * 32:(j + 1) * 32, i * 128:(i + 1) * 128] = l[i * 32:(i + 1) * 32]
-    y_ref[0:32] = dot3(lh[0:32, :256], ll[0:32, :256], zh[...], zl[...])
-    y_ref[512:544] = dot3(lh[0:32, 256:], ll[0:32, 256:], wh[:256, :], wl[:256, :])
+    edge = dot3(lh[0:32, :], ll[0:32, :], zh[...], zl[...])
+    y_ref[0:32] = edge[:, :512]
+    y_ref[512:544] = edge[:, 512:]
     y_ref[32:512] = dot3(lh[32:512, :], ll[32:512, :], wh[...], wl[...])
 
     cos = [math.cos(2 * math.pi * i / 32) for i in range(32)]

time: 141 us -> 133 us (0.943)
  Pallas kernels: 135 us -> 127 us
    pallas_call x1, Pallas kernels: 110 us -> 104 us  [exchange(): pl.pallas_call(exchange_kernel, in_specs=[vmem, hbm, hbm, hbm, vmem, vmem...]
where the time goes in v5:
time: 133 us
  Pallas kernels  127 us (95%)
  other arithmetic  3.04 us (2%)
  local copies, waits for them, and re-layouts  2.56 us (2%)
    pallas_call x1, Pallas kernels, exchange(): pl.pallas_call(exchange_kernel, in_specs=[vmem, hbm, hbm, hbm, vmem, vmem...  104 us
    pallas_call x1, Pallas kernels, make_payload(): pl.pallas_call(grid_kernel, grid=(blocks // STEP,), in_specs=[pl.BlockSpe...  20.6 us
    pallas_call x1, Pallas kernels, across(): pl.pallas_call(across_kernel, out_shape=jax.ShapeDtypeStruct((32, G), F32...  3.27 us

profile of v5, /device:TPU:32, one launch (start us, length us, event | category | flops | bytes accessed | tf_op | source)
XLA Modules:
  0.0 133.3 jit_solution(14440001199739990106)
XLA Ops:
  0.0 2.3 %copy_convert_fusion = (f32[256,2,1024]{2,0,1:T(8,128)S(1)}, f32[256,2,1024]{2,0,1:T(8,128)S(1)}) fusion(bf16[256,2,1024]{2,1,0:T(2,128)(2,1)} %param.25, bf16[256,2,1024]{2,1,0:T(2,128)(2,1)} %param.24), kind=kLoop, calls=%fused_computation.1 | loop fusion | flops 1048576 | bytes 6291456 | tf_op jit(solution)/shard_map/convert_element_type | solution.py:756
  2.3 0.6 add_bitcast_fusion
  2.9 0.0 copy-start.18
  2.9 0.0 copy-start.8
  2.9 0.0 copy-start.9
  3.0 0.0 copy-start.10
  3.0 0.0 copy-start.11
  3.0 0.0 copy-start.15
  3.0 0.0 copy-start.16
  3.0 0.0 copy-start.17
  3.0 0.1 pad_maximum_fusion.beam_ref
  3.2 0.4 copy-done.18
  3.6 0.1 copy.25.tile_ref
  3.7 0.2 copy-done.8
  3.9 0.1 copy-done.9
  4.0 0.0 copy-done.10
  4.0 0.0 copy-done.11
  4.0 0.0 copy-done.15
  4.0 0.0 copy-done.16
  4.0 0.0 copy-done.17
  4.1 0.0 copy-start
  4.1 1.6 %copy-done = bf16[1024,1024]{1,0:T(8,128)(2,1)S(1)} copy-done((bf16[1024,1024]{1,0:T(8,128)(2,1)S(1)}, bf16[1024,1024]{1,0:T(8,128)(2,1)}, u32[]{:S(2)}) %copy-start) | copy-done | bytes 2097176
  5.6 0.0 copy-start.3
  5.6 0.0 copy-start.4
  5.6 0.0 copy-start.5
  5.7 0.0 copy-start.13
  5.7 0.0 copy-start.14
  5.7 20.6 %gridding.1.src_ref = f32[2176,128]{1,0:T(8,128)S(1)} custom-call(f32[256,2,128]{2,1,0:T(2,128)S(1)} %copy-done.8, f32[256,2,128]{2,1,0:T(2,128)S(1)} %copy-done.9, f32[2,256,1024]{2,1,0:T(8,128)S(1)} %pad_maximum_fusion.beam_ref, s32[1,256]{1,0:T(1,128)S(1)} %copy-done.15, s32[128,1]{1,0:T(8,128)S(1)} %copy.25.tile_ref, s32[1,128]{1,0:T(1,128)S(1)} %bitcast.8, ...), custom_call_target="tpu_custom_call" | custom-call | tf_op jit(solution)/shard_map/gridding/pallas_call | solution.py:302
  26.3 0.0 copy-done.3
  26.3 0.0 copy-done.4
  26.3 0.0 copy-done.5
  26.4 0.0 copy-done.13
  26.4 0.0 copy-done.14
  26.4 0.0 copy-start.1
  26.4 0.0 copy-start.2
  26.4 0.0 copy-start.6
  26.4 0.0 copy-start.7
  26.4 0.0 copy-start.12
  26.4 103.5 %exchange.1 = f32[2,4,16,16,128]{4,3,2,1,0:T(8,128)S(1)} custom-call(f32[2176,128]{1,0:T(8,128)S(1)} %gridding.1.src_ref, bf16[512,1024]{1,0:T(8,128)(2,1)S(1)} %copy-done.3, bf16[512,1024]{1,0:T(8,128)(2,1)S(1)} %copy-done.4, f32[16,64,256]{2,1,0:T(8,128)S(1)} %copy-done.5, bf16[32,128]{1,0:T(8,128)(2,1)S(1)} %copy-done.13, bf16[32,128]{1,0:T(8,128)(2,1)S(1)} %copy-done.14), custom_call_target="tpu_custom_call" | custom-call | tf_op jit(solution)/shard_map/exchange/pallas_call | solution.py:653
  130.0 0.0 copy-done.1
  130.0 0.0 copy-done.2
  130.0 0.0 copy-done.6
  130.0 0.0 copy-done.7
  130.0 0.0 copy-done.12
  130.0 3.3 %across.1 = f32[32,8192]{1,0:T(8,128)} custom-call(f32[2048,128]{1,0:T(8,128)S(1)} %bitcast.7, bf16[512,512]{1,0:T(8,128)(2,1)S(1)} %copy-done.6, bf16[512,512]{1,0:T(8,128)(2,1)S(1)} %copy-done.7, bf16[512,1024]{1,0:T(8,128)(2,1)S(1)} %copy-done.1, bf16[512,1024]{1,0:T(8,128)(2,1)S(1)} %copy-done.2, f32[17,512]{1,0:T(8,128)S(1)} %copy-done.12), custom_call_target="tpu_custom_call" | custom-call | tf_op jit(solution)/shard_map/across/pallas_call | solution.py:742
Async XLA Ops:
  2.9 0.7 copy-start.18
  2.9 1.0 copy-start.8
  2.9 1.0 copy-start.9
  3.0 1.0 copy-start.10
  3.0 1.1 copy-start.11
  3.0 1.1 copy-start.15
  3.0 1.1 copy-start.16
  3.0 1.0 copy-start.17
  4.1 1.6 %copy-start = (bf16[1024,1024]{1,0:T(8,128)(2,1)S(1)}, bf16[1024,1024]{1,0:T(8,128)(2,1)}, u32[]{:S(2)}) copy-start(bf16[1024,1024]{1,0:T(8,128)(2,1)} %constant.30.clone.d2h_hbm) | copy-start | bytes 6291460
  5.6 20.7 %copy-start.3 = (bf16[512,1024]{1,0:T(8,128)(2,1)S(1)}, bf16[512,1024]{1,0:T(8,128)(2,1)}, u32[]{:S(2)}) copy-start(bf16[512,1024]{1,0:T(8,128)(2,1)} %constant.32.clone.wh_hbm) | copy-start | bytes 3145732
  5.6 20.7 %copy-start.4 = (bf16[512,1024]{1,0:T(8,128)(2,1)S(1)}, bf16[512,1024]{1,0:T(8,128)(2,1)}, u32[]{:S(2)}) copy-start(bf16[512,1024]{1,0:T(8,128)(2,1)} %constant.33.clone.wl_hbm) | copy-start | bytes 3145732
  5.6 20.7 %copy-start.5 = (f32[16,64,256]{2,1,0:T(8,128)S(1)}, f32[16,64,256]{2,1,0:T(8,128)}, u32[]{:S(2)}) copy-start(f32[16,64,256]{2,1,0:T(8,128)} %constant.34.clone.t_hbm) | copy-start | bytes 3145732
  5.7 20.7 %copy-start.13 = (bf16[32,128]{1,0:T(8,128)(2,1)S(1)}, bf16[32,128]{1,0:T(8,128)(2,1)}, u32[]{:S(2)}) copy-start(bf16[32,128]{1,0:T(8,128)(2,1)} %constant.35.clone.eh) | copy-start | bytes 24580
  5.7 20.7 %copy-start.14 = (bf16[32,128]{1,0:T(8,128)(2,1)S(1)}, bf16[32,128]{1,0:T(8,128)(2,1)}, u32[]{:S(2)}) copy-start(bf16[32,128]{1,0:T(8,128)(2,1)} %constant.36.clone.el) | copy-start | bytes 24580
  26.4 103.6 %copy-start.1 = (bf16[512,1024]{1,0:T(8,128)(2,1)S(1)}, bf16[512,1024]{1,0:T(8,128)(2,1)}, u32[]{:S(2)}) copy-start(bf16[512,1024]{1,0:T(8,128)(2,1)} %constant.39.clone.zh) | copy-start | bytes 3145732
  26.4 103.6 %copy-start.2 = (bf16[512,1024]{1,0:T(8,128)(2,1)S(1)}, bf16[512,1024]{1,0:T(8,128)(2,1)}, u32[]{:S(2)}) copy-start(bf16[512,1024]{1,0:T(8,128)(2,1)} %constant.40.clone.zl) | copy-start | bytes 3145732
  26.4 103.6 %copy-start.6 = (bf16[512,512]{1,0:T(8,128)(2,1)S(1)}, bf16[512,512]{1,0:T(8,128)(2,1)}, u32[]{:S(2)}) copy-start(bf16[512,512]{1,0:T(8,128)(2,1)} %constant.37.clone.wh) | copy-start | bytes 1572868
  26.4 103.6 %copy-start.7 = (bf16[512,512]{1,0:T(8,128)(2,1)S(1)}, bf16[512,512]{1,0:T(8,128)(2,1)}, u32[]{:S(2)}) copy-start(bf16[512,512]{1,0:T(8,128)(2,1)} %constant.38.clone.wl) | copy-start | bytes 1572868
  26.4 103.6 %copy-start.12 = (f32[17,512]{1,0:T(8,128)S(1)}, f32[17,512]{1,0:T(8,128)}, u32[]{:S(2)}) copy-start(f32[17,512]{1,0:T(8,128)} %constant.41.clone.twist) | copy-start | bytes 104452

commit v6 on v5

--- a/solution.py
+++ b/solution.py
@@ -14,7 +14,7 @@
 SUB = 32
 PAIRS = 16
 CLASSES = 16
-STEP = 32
+STEP = 64
 F32 = jnp.float32
 BF16 = jnp.bfloat16
 MB = 1 << 20
@@ -308,7 +308,7 @@
             pl.BlockSpec((2, STEP, SUB * SUB), lambda i: (0, i, 0)),
             whole((1, blocks)), whole((subs, 1)), whole((1, subs)), whole((1, subs)),
             whole((256, 256)), whole((256, 256)),
-            pl.BlockSpec(memory_space=pl.ANY), pl.BlockSpec(memory_space=pl.ANY),
+            pl.BlockSpec(memory_space=pltpu.HBM), pl.BlockSpec(memory_space=pltpu.HBM),
         ],
         out_specs=whole((CLASSES * tall, 128)),
         out_shape=jax.ShapeDtypeStruct((CLASSES * tall, 128), F32),
@@ -449,7 +449,7 @@
             for k in range(15):
                 if ab:
                     far_copy(0, g, k).wait_send()
-                far_copy(ab, g, k).start()
+                far_copy(ab, g, (k + 4 * g) % 15).start()
             if g % 2 == 1:
                 rows = slice(0, 136 if ab == 0 else 128)
                 held[ab, h, 15, rows, :] = box[ab, h, group, rows, :]
@@ -648,7 +648,7 @@
     wh, wl = halves(w)
     eh, el = halves(e)
     vmem = pl.BlockSpec(memory_space=pltpu.VMEM)
-    hbm = pl.BlockSpec(memory_space=pl.ANY)
+    hbm = pl.BlockSpec(memory_space=pltpu.HBM)
     dma = pltpu.SemaphoreType.DMA
     return pl.pallas_call(
         exchange_kernel,

time: 133 us -> 132 us (level)
  Pallas kernels: 127 us -> 125 us
    pallas_call x1, Pallas kernels: 104 us -> 102 us  [exchange(): pl.pallas_call(exchange_kernel, in_specs=[vmem, hbm, hbm, hbm, vmem, vmem...]
where the time goes in v6:
time: 132 us; the launch traced here: 131 us
  Pallas kernels  125 us (95%)
  other arithmetic  3.04 us (2%)
  local copies, waits for them, and re-layouts  2.56 us (2%)
    pallas_call x1, Pallas kernels, exchange(): pl.pallas_call(exchange_kernel, in_specs=[vmem, hbm, hbm, hbm, vmem, vmem...  102 us
    pallas_call x1, Pallas kernels, make_payload(): pl.pallas_call(grid_kernel, grid=(blocks // STEP,), in_specs=[pl.BlockSpe...  19.9 us
    pallas_call x1, Pallas kernels, across(): pl.pallas_call(across_kernel, out_shape=jax.ShapeDtypeStruct((32, G), F32...  3.27 us

profile of v6, /device:TPU:32, one launch (start us, length us, event | category | flops | bytes accessed | tf_op | source)
XLA Modules:
  0.0 131.2 jit_solution(13539254021635446480)
XLA Ops:
  0.0 2.3 %copy_convert_fusion = (f32[256,2,1024]{2,0,1:T(8,128)S(1)}, f32[256,2,1024]{2,0,1:T(8,128)S(1)}) fusion(bf16[256,2,1024]{2,1,0:T(2,128)(2,1)} %param.25, bf16[256,2,1024]{2,1,0:T(2,128)(2,1)} %param.24), kind=kLoop, calls=%fused_computation.1 | loop fusion | flops 1048576 | bytes 6291456 | tf_op jit(solution)/shard_map/convert_element_type | solution.py:756
  2.3 0.6 add_bitcast_fusion
  2.9 0.0 copy-start.18
  2.9 0.0 copy-start.8
  2.9 0.0 copy-start.9
  3.0 0.0 copy-start.10
  3.0 0.0 copy-start.11
  3.0 0.0 copy-start.15
  3.0 0.0 copy-start.16
  3.0 0.0 copy-start.17
  3.0 0.1 pad_maximum_fusion.beam_ref
  3.2 0.4 copy-done.18
  3.6 0.1 copy.25.tile_ref
  3.7 0.2 copy-done.8
  3.9 0.1 copy-done.9
  4.0 0.0 copy-done.10
  4.0 0.0 copy-done.11
  4.0 0.0 copy-done.15
  4.0 0.0 copy-done.16
  4.0 0.0 copy-done.17
  4.1 0.0 copy-start
  4.1 1.6 %copy-done = bf16[1024,1024]{1,0:T(8,128)(2,1)S(1)} copy-done((bf16[1024,1024]{1,0:T(8,128)(2,1)S(1)}, bf16[1024,1024]{1,0:T(8,128)(2,1)}, u32[]{:S(2)}) %copy-start) | copy-done | bytes 2097176
  5.6 0.0 copy-start.3
  5.6 0.0 copy-start.4
  5.6 0.0 copy-start.5
  5.7 0.0 copy-start.13
  5.7 0.0 copy-start.14
  5.7 19.9 %gridding.1.src_ref = f32[2176,128]{1,0:T(8,128)S(1)} custom-call(f32[256,2,128]{2,1,0:T(2,128)S(1)} %copy-done.8, f32[256,2,128]{2,1,0:T(2,128)S(1)} %copy-done.9, f32[2,256,1024]{2,1,0:T(8,128)S(1)} %pad_maximum_fusion.beam_ref, s32[1,256]{1,0:T(1,128)S(1)} %copy-done.15, s32[128,1]{1,0:T(8,128)S(1)} %copy.25.tile_ref, s32[1,128]{1,0:T(1,128)S(1)} %bitcast.8, ...), custom_call_target="tpu_custom_call" | custom-call | tf_op jit(solution)/shard_map/gridding/pallas_call | solution.py:302
  25.6 0.0 copy-done.3
  25.6 0.0 copy-done.4
  25.6 0.0 copy-done.5
  25.6 0.0 copy-done.13
  25.6 0.0 copy-done.14
  25.6 0.0 copy-start.1
  25.7 0.0 copy-start.2
  25.7 0.0 copy-start.6
  25.7 0.0 copy-start.7
  25.7 0.0 copy-start.12
  25.7 102.1 %exchange.1 = f32[2,4,16,16,128]{4,3,2,1,0:T(8,128)S(1)} custom-call(f32[2176,128]{1,0:T(8,128)S(1)} %gridding.1.src_ref, bf16[512,1024]{1,0:T(8,128)(2,1)S(1)} %copy-done.3, bf16[512,1024]{1,0:T(8,128)(2,1)S(1)} %copy-done.4, f32[16,64,256]{2,1,0:T(8,128)S(1)} %copy-done.5, bf16[32,128]{1,0:T(8,128)(2,1)S(1)} %copy-done.13, bf16[32,128]{1,0:T(8,128)(2,1)S(1)} %copy-done.14), custom_call_target="tpu_custom_call" | custom-call | tf_op jit(solution)/shard_map/exchange/pallas_call | solution.py:653
  127.8 0.0 copy-done.1
  127.8 0.0 copy-done.2
  127.9 0.0 copy-done.6
  127.9 0.0 copy-done.7
  127.9 0.0 copy-done.12
  127.9 3.3 %across.1 = f32[32,8192]{1,0:T(8,128)} custom-call(f32[2048,128]{1,0:T(8,128)S(1)} %bitcast.7, bf16[512,512]{1,0:T(8,128)(2,1)S(1)} %copy-done.6, bf16[512,512]{1,0:T(8,128)(2,1)S(1)} %copy-done.7, bf16[512,1024]{1,0:T(8,128)(2,1)S(1)} %copy-done.1, bf16[512,1024]{1,0:T(8,128)(2,1)S(1)} %copy-done.2, f32[17,512]{1,0:T(8,128)S(1)} %copy-done.12), custom_call_target="tpu_custom_call" | custom-call | tf_op jit(solution)/shard_map/across/pallas_call | solution.py:742
Async XLA Ops:
  2.9 0.7 copy-start.18
  2.9 1.0 copy-start.8
  2.9 1.0 copy-start.9
  3.0 1.0 copy-start.10
  3.0 1.1 copy-start.11
  3.0 1.1 copy-start.15
  3.0 1.1 copy-start.16
  3.0 1.0 copy-start.17
  4.1 1.6 %copy-start = (bf16[1024,1024]{1,0:T(8,128)(2,1)S(1)}, bf16[1024,1024]{1,0:T(8,128)(2,1)}, u32[]{:S(2)}) copy-start(bf16[1024,1024]{1,0:T(8,128)(2,1)} %constant.30.clone.d2h_hbm) | copy-start | bytes 6291460
  5.6 20.0 %copy-start.3 = (bf16[512,1024]{1,0:T(8,128)(2,1)S(1)}, bf16[512,1024]{1,0:T(8,128)(2,1)}, u32[]{:S(2)}) copy-start(bf16[512,1024]{1,0:T(8,128)(2,1)} %constant.32.clone.wh_hbm) | copy-start | bytes 3145732
  5.6 20.0 %copy-start.4 = (bf16[512,1024]{1,0:T(8,128)(2,1)S(1)}, bf16[512,1024]{1,0:T(8,128)(2,1)}, u32[]{:S(2)}) copy-start(bf16[512,1024]{1,0:T(8,128)(2,1)} %constant.33.clone.wl_hbm) | copy-start | bytes 3145732
  5.6 20.0 %copy-start.5 = (f32[16,64,256]{2,1,0:T(8,128)S(1)}, f32[16,64,256]{2,1,0:T(8,128)}, u32[]{:S(2)}) copy-start(f32[16,64,256]{2,1,0:T(8,128)} %constant.34.clone.t_hbm) | copy-start | bytes 3145732
  5.7 20.0 %copy-start.13 = (bf16[32,128]{1,0:T(8,128)(2,1)S(1)}, bf16[32,128]{1,0:T(8,128)(2,1)}, u32[]{:S(2)}) copy-start(bf16[32,128]{1,0:T(8,128)(2,1)} %constant.35.clone.eh) | copy-start | bytes 24580
  5.7 20.0 %copy-start.14 = (bf16[32,128]{1,0:T(8,128)(2,1)S(1)}, bf16[32,128]{1,0:T(8,128)(2,1)}, u32[]{:S(2)}) copy-start(bf16[32,128]{1,0:T(8,128)(2,1)} %constant.36.clone.el) | copy-start | bytes 24580
  25.6 102.2 %copy-start.1 = (bf16[512,1024]{1,0:T(8,128)(2,1)S(1)}, bf16[512,1024]{1,0:T(8,128)(2,1)}, u32[]{:S(2)}) copy-start(bf16[512,1024]{1,0:T(8,128)(2,1)} %constant.39.clone.zh) | copy-start | bytes 3145732
  25.7 102.2 %copy-start.2 = (bf16[512,1024]{1,0:T(8,128)(2,1)S(1)}, bf16[512,1024]{1,0:T(8,128)(2,1)}, u32[]{:S(2)}) copy-start(bf16[512,1024]{1,0:T(8,128)(2,1)} %constant.40.clone.zl) | copy-start | bytes 3145732
  25.7 102.2 %copy-start.6 = (bf16[512,512]{1,0:T(8,128)(2,1)S(1)}, bf16[512,512]{1,0:T(8,128)(2,1)}, u32[]{:S(2)}) copy-start(bf16[512,512]{1,0:T(8,128)(2,1)} %constant.37.clone.wh) | copy-start | bytes 1572868
  25.7 102.2 %copy-start.7 = (bf16[512,512]{1,0:T(8,128)(2,1)S(1)}, bf16[512,512]{1,0:T(8,128)(2,1)}, u32[]{:S(2)}) copy-start(bf16[512,512]{1,0:T(8,128)(2,1)} %constant.38.clone.wl) | copy-start | bytes 1572868
  25.7 102.2 %copy-start.12 = (f32[17,512]{1,0:T(8,128)S(1)}, f32[17,512]{1,0:T(8,128)}, u32[]{:S(2)}) copy-start(f32[17,512]{1,0:T(8,128)} %constant.41.clone.twist) | copy-start | bytes 104452
